TPU v7x, 128 devices: a whole 4x4x4 slice. The times are simulated.
128 devices in a mesh: dp: 8 (over x, z_hi), gallery: 16 (over z_lo, y, core).
Axes of the slice: x: 4, y: 4, z: 4 (z_hi: 2, z_lo: 2; z = z_hi * 2 + z_lo), core: 2. Of those that a mesh axis runs over, the one named last changes fastest.
Arguments:
- query_hidden: bfloat16 [1024, 32, 1536], P(('dp', 'gallery')), may hold values from -6 to 6
- document_states: bfloat16 [512, 768, 1536], P(('dp', 'gallery')), may hold values from -6 to 6
- projection: bfloat16 [1536, 128], replicated, may hold values from -0.15625 to 0.15625
- lengths: int32 [512], P(('dp', 'gallery')), may hold values from 192 to 768
- best_token: int32 [1024, 32, 64], P('dp', None, 'gallery'), may hold values from 0 to 767, as said below
Outputs:
- weight_grad: float32 [1536, 128], replicated
- query_grad: float32 [1024, 32, 128], P(('dp', 'gallery'))
Inputs may be any that keep to these rules, and one draw needn't show every extreme that they name: best_token[b, i, p] is below the length of page p of query b's data group, that is below lengths[(b // 128) * 64 + p].
All inputs are finite; a program needn't handle non-finite values.
Results may differ from a plain program's by a relative error of at most 0.0041.
Values may be sent and summed in bfloat16 or wider, within the bound.
No kernel may reach another device: no remote copies, remote signals or barrier semaphores. Data moves between devices by JAX's collectives and lax.ppermute only.
A program may use at most 64 MiB of HBM per device.

v0:
```python
import math

import jax
import jax.numpy as jnp
from jax import lax
from jax.sharding import PartitionSpec as P

TILE = 256


epsilon = 1e-06
sharpness_divisor = 0.02


def unit_parts(hidden_rows, projection):
    raw = jnp.dot(hidden_rows, projection, preferred_element_type=jnp.float32)
    inverse = lax.rsqrt(jnp.sum(raw * raw, axis=1, keepdims=True) + epsilon)
    return (raw, inverse)


def unit_backward(grad_unit, raw, inverse):
    unit = raw * inverse
    return (grad_unit - unit * jnp.sum(unit * grad_unit, axis=1, keepdims=True)) * inverse


def page_maxima(query_tokens, page_units, page_lengths):
    token_total = query_tokens.shape[0]
    tile_count = page_units.shape[1] // TILE

    def one_page(carry, inputs):
        page_unit, length = inputs

        def one_tile(best, tile_index):
            start = tile_index * TILE
            block = lax.dynamic_slice_in_dim(page_unit, start, TILE, 0)
            scores = lax.dot_general(
                query_tokens, block, (((1,), (1,)), ((), ())), preferred_element_type=jnp.float32
            )
            positions = start + jnp.arange(TILE)
            scores = jnp.where(positions[None, :] < length, scores, -jnp.inf)
            best = jnp.maximum(best, jnp.max(scores, axis=1))
            return (best, None)

        start_best = jnp.full((token_total,), -jnp.inf, jnp.float32)
        best, unused = lax.scan(one_tile, start_best, jnp.arange(tile_count))
        return (carry, best)

    unused, maxima = lax.scan(one_page, 0, (page_units, page_lengths))
    return maxima


def page_derivative(index_rows, weight_rows, query_flat, page_length):
    row_total = index_rows.shape[0]
    block_rows = math.gcd(row_total, 2048)
    block_count = row_total // block_rows
    positions = jnp.arange(page_length, dtype=jnp.int32)
    emb_size = query_flat.shape[1]
    query_blocks = query_flat.reshape(block_count, block_rows, emb_size)

    def one_page(carry, inputs):
        index_col, weight_col = inputs
        index_blocks = index_col.reshape(block_count, block_rows)
        weight_blocks = weight_col.reshape(block_count, block_rows)

        def one_block(total, block_inputs):
            index_block, weight_block, query_block = block_inputs
            table = jnp.where(
                index_block[:, None] == positions[None, :], weight_block[:, None], 0.0
            )
            part = lax.dot_general(
                table,
                query_block,
                (((0,), (0,)), ((), ())),
                precision=lax.Precision.HIGHEST,
                preferred_element_type=jnp.float32,
            )
            return (total + part, None)

        start_total = jnp.zeros((page_length, emb_size), jnp.float32)
        total, unused = lax.scan(
            one_block, start_total, (index_blocks, weight_blocks, query_blocks)
        )
        return (carry, total)

    unused, result = lax.scan(one_page, 0, (index_rows.T, weight_rows.T))
    return result


def per_device(query_hidden, document_states, projection, lengths, best_token):
    query_count, number_items, hidden_size = query_hidden.shape
    page_count, page_length, unused_size = document_states.shape
    emb_size = projection.shape[1]
    gallery_size = lax.axis_size("gallery")
    gallery_rank = lax.axis_index("gallery")
    group_queries = query_count * gallery_size
    group_pages = page_count * gallery_size
    similarity_multiplier = 1.0 / (number_items * sharpness_divisor)
    query_rows = query_hidden.reshape(-1, hidden_size)
    query_raw, query_inverse = unit_parts(query_rows, projection)
    query_unit = (
        (query_raw * query_inverse)
        .astype(jnp.bfloat16)
        .reshape(query_count, number_items, emb_size)
    )
    every_query = lax.all_gather(query_unit, "gallery", axis=0, tiled=True)
    page_rows = document_states.reshape(-1, hidden_size)
    page_raw, page_inverse = unit_parts(page_rows, projection)
    page_flat = (page_raw * page_inverse).astype(jnp.bfloat16)
    page_unit = page_flat.reshape(page_count, page_length, emb_size)
    maxima = page_maxima(every_query.reshape(-1, emb_size), page_unit, lengths)
    score = jnp.sum(maxima.T.reshape(group_queries, number_items, page_count), axis=1)
    expo = jnp.exp(score * similarity_multiplier)
    total = lax.psum(jnp.sum(expo, axis=1), "gallery")
    target = jnp.arange(group_queries) * group_pages // group_queries
    page_ids = gallery_rank * page_count + jnp.arange(page_count)
    onehot = (target[:, None] == page_ids[None, :]).astype(jnp.float32)
    score_grad = (expo / total[:, None] - onehot) * similarity_multiplier
    positions = jnp.arange(page_length, dtype=jnp.int32)
    summed_term = jnp.zeros((group_queries, number_items, emb_size), jnp.float32)
    for page in range(page_count):
        index_col = best_token[:, :, page].reshape(-1)
        table = (index_col[:, None] == positions[None, :]).astype(jnp.bfloat16)
        chosen = jnp.dot(table, page_unit[page], preferred_element_type=jnp.float32)
        chosen = chosen.reshape(group_queries, number_items, emb_size)
        summed_term = summed_term + chosen * score_grad[:, page][:, None, None]
    summed = lax.psum(summed_term, "gallery")
    query_grad = lax.dynamic_slice_in_dim(summed, gallery_rank * query_count, query_count, 0)
    query_dir = unit_backward(query_grad.reshape(-1, emb_size), query_raw, query_inverse).astype(
        jnp.bfloat16
    )
    local_grad = lax.dot_general(
        query_rows, query_dir, (((0,), (0,)), ((), ())), preferred_element_type=jnp.float32
    )
    index_rows = best_token.reshape(-1, page_count)
    weight_rows = jnp.broadcast_to(
        score_grad[:, None, :], (group_queries, number_items, page_count)
    ).reshape(-1, page_count)
    query_flat = every_query.reshape(-1, emb_size).astype(jnp.float32)
    normalized_derivative = page_derivative(
        index_rows, weight_rows, query_flat, page_length
    ).reshape(-1, emb_size)
    page_direction = unit_backward(normalized_derivative, page_raw, page_inverse).astype(
        jnp.bfloat16
    )
    local_grad = local_grad + lax.dot_general(
        page_rows, page_direction, (((0,), (0,)), ((), ())), preferred_element_type=jnp.float32
    )
    weight_grad = lax.psum(local_grad, ("dp", "gallery"))
    return (weight_grad, query_grad)


def solution(mesh):
    return jax.shard_map(
        per_device,
        mesh=mesh,
        in_specs=(
            P(("dp", "gallery"), None, None),
            P(("dp", "gallery"), None, None),
            P(),
            P(("dp", "gallery")),
            P("dp", None, "gallery"),
        ),
        out_specs=(P(), P(("dp", "gallery"), None, None)),
        check_vma=False,
    )
```

profile of v0, /device:TPU:1, one launch (start us, length us, event | category | flops | bytes accessed | tf_op | source)
XLA Modules:
  0.0 425.3 jit_solution(2869538407203894984)
XLA Ops:
  7.2 1.1 copy-done
  8.3 1.4 multiply_reduce_fusion.1
  10.6 5.4 %multiply_reduce_fusion = (f32[3072]{0:T(1024)S(1)}, f32[3072,128]{1,0:T(8,128)S(1)}) fusion(bf16[3072,1536]{1,0:T(8,128)(2,1)} %bitcast.103, bf16[1536,128]{1,0:T(8,128)(2,1)} %param.15), kind=kOutput, calls=%fused_computation.45 | convolution fusion | flops 1208742912 | bytes 11415552 | tf_op jit(solution)/shard_map/dot_general | solution.py:16
  19.2 3.5 fusion.21
  22.6 3.4 fusion.20
  26.1 3.4 fusion.19
  29.5 17.3 %all-gather.2.cloned.1.call-done = bf16[128,32,128]{2,1,0:T(8,128)(2,1)} async-done(((bf16[8,32,128]{2,1,0:T(8,128)(2,1)}), bf16[128,32,128]{2,1,0:T(8,128)(2,1)}) %all-gather.2.cloned.1.call-update) | async-done | bytes 1048592 | tf_op jit(solution)/shard_map/all_gather | solution.py:105
  46.8 54.6 %while.45 = (s32[]{:T(128)}, f32[4,4096]{1,0:T(4,128)}, bf16[4,768,128]{2,1,0:T(8,128)(2,1)S(1)}, s32[4]{0:T(128)S(1)}, bf16[4096,128]{1,0:T(8,128)(2,1)}, /*ind...) while((s32[]{:T(128)}, f32[4,4096]{1,0:T(4,128)}, ...), condition=%wide.region_6.7_spmd, body=%wide.region_2.6_spmd.sunk | while | flops 270537216 | bytes 1606826 | solution.py:48
  47.4 11.5 %while.48 = (s32[]{:T(128)}, f32[4096]{0:T(1024)S(1)}, s32[3]{0:T(128)S(1)}, s32[]{:T(128)}, bf16[768,128]{1,0:T(8,128)(2,1)S(1)}, /*index=5*/bf16[4096,128]{1,0...) while((s32[]{:T(128)}, f32[4096]{0:T(1024)S(1)}, s32[3]{0:T(128)S(1)}, s32[]{:T(128)}, ...), condition=%wide.region_5.5_spmd.clone, body=%wide.region_3.4_spmd.clone.sunk | while | flops 270537216 | bytes 1180605 | solution.py:45
  49.2 1.9 fusion.58
  53.1 1.9 fusion.58
  56.9 1.9 fusion.58
  58.9 1.5 dynamic_update_slice.12
  61.0 11.5 %while.48 = (s32[]{:T(128)}, f32[4096]{0:T(1024)S(1)}, s32[3]{0:T(128)S(1)}, s32[]{:T(128)}, bf16[768,128]{1,0:T(8,128)(2,1)S(1)}, /*index=5*/bf16[4096,128]{1,0...) while((s32[]{:T(128)}, f32[4096]{0:T(1024)S(1)}, s32[3]{0:T(128)S(1)}, s32[]{:T(128)}, ...), condition=%wide.region_5.5_spmd.clone, body=%wide.region_3.4_spmd.clone.sunk | while | flops 270537216 | bytes 1180605 | solution.py:45
  62.9 1.9 fusion.58
  66.7 1.9 fusion.58
  70.6 1.9 fusion.58
  72.6 1.5 dynamic_update_slice.12
  74.7 11.5 %while.48 = (s32[]{:T(128)}, f32[4096]{0:T(1024)S(1)}, s32[3]{0:T(128)S(1)}, s32[]{:T(128)}, bf16[768,128]{1,0:T(8,128)(2,1)S(1)}, /*index=5*/bf16[4096,128]{1,0...) while((s32[]{:T(128)}, f32[4096]{0:T(1024)S(1)}, s32[3]{0:T(128)S(1)}, s32[]{:T(128)}, ...), condition=%wide.region_5.5_spmd.clone, body=%wide.region_3.4_spmd.clone.sunk | while | flops 270537216 | bytes 1180605 | solution.py:45
  76.6 1.9 fusion.58
  80.4 1.9 fusion.58
  84.2 1.9 fusion.58
  86.2 1.5 dynamic_update_slice.12
  88.4 11.5 %while.48 = (s32[]{:T(128)}, f32[4096]{0:T(1024)S(1)}, s32[3]{0:T(128)S(1)}, s32[]{:T(128)}, bf16[768,128]{1,0:T(8,128)(2,1)S(1)}, /*index=5*/bf16[4096,128]{1,0...) while((s32[]{:T(128)}, f32[4096]{0:T(1024)S(1)}, s32[3]{0:T(128)S(1)}, s32[]{:T(128)}, ...), condition=%wide.region_5.5_spmd.clone, body=%wide.region_3.4_spmd.clone.sunk | while | flops 270537216 | bytes 1180605 | solution.py:45
  90.2 1.9 fusion.58
  94.1 1.9 fusion.58
  97.9 1.9 fusion.58
  99.9 1.5 dynamic_update_slice.12
  101.4 1.0 reshape.215
  102.6 26.8 %psum.21 = f32[128]{0:T(128)S(1)} all-reduce(f32[128]{0:T(128)S(1)} %fusion.35), channel_id=1, replica_groups=mesh['dp'=8,'gallery'=16] {'gallery'}, use_global_device_ids=true, to_apply=%region_9.10 | all-reduce | flops 128 | bytes 1024 | tf_op jit(solution)/shard_map/psum | solution.py:113
  131.6 2.9 bitcast_convert_fusion
  134.4 5.9 %multiply_add_fusion = f32[128,32,128]{2,0,1:T(8,128)} fusion(f32[128,32,128]{2,0,1:T(8,128)S(1)} %copy-done.11, f32[128,32,128]{2,0,1:T(8,128)} %fusion.20, f32[128,32,128]{2,0,1:T(8,128)} %fusion.19, s32[128,32]{0,1:T(8,128)S(1)} %bitcast.116, f32[128]{0:T(128)S(1)} %copy-done.7, f32[128]{0:T(128)S(1)} %copy-done.8, f32[128]{0:T(128)S(1)} %copy-done.9, ...), kind=kOutput, calls=%fused_computation.39 | convolution fusion | flops 812122112 | bytes 8603648 | tf_op jit(solution)/shard_map/dot_general | solution.py:123
  140.6 105.3 %while.47 = (s32[]{:T(128)}, f32[4,768,128]{2,1,0:T(8,128)}, s32[4,4096]{1,0:T(4,128)}, f32[4,4096]{1,0:T(4,128)}, f32[2,2048,128]{2,1,0:T(8,128)}, /*index=5*/s32[]{:T(128)}, s32[]{:T(128)}, s32[]{:T(128)}, s32[]{:T(128)}) while((s32[]{:T(128)}, f32[4,768,128]{2,1,0:T(8,128)}, s32[4,4096]{1,0:T(4,128)}, f32[4,4096]{1,0:T(4,128)}, ...), condition=%wide.region_15.16_spmd.clone, body=%wide.region_12.15_spmd.clone.sunk | while | flops 2419261440 | bytes 2808108 | solution.py:85
  140.6 0.9 dynamic-slice_reduce_fusion.4
  141.5 0.9 dynamic-slice_reduce_fusion.5
  142.4 23.7 %while.49 = (s32[]{:T(128)}, f32[768,128]{1,0:T(8,128)S(1)}, s32[2,2048]{1,0:T(2,128)S(1)}, s32[768]{0:T(1024)S(1)}, f32[2,2048]{1,0:T(2,128)S(1)}, /*index=5*/f32[2,2048,128]{2,1,0:T(8,128)}, s32[]{:T(128)}, s32[]{:T(128)}) while((s32[]{:T(128)}, f32[768,128]{1,0:T(8,128)S(1)}, s32[2,2048]{1,0:T(2,128)S(1)}, ...), condition=%wide.region_14.14_spmd.clone, body=%wide.region_13.13_spmd.clone.sunk | while | flops 2419261440 | bytes 1887347 | solution.py:80
  142.5 11.8 %fusion.55 = f32[768,128]{1,0:T(8,128)S(1)} fusion(f32[2048]{0:T(1024)S(1)} %bitcast.106, s32[768]{0:T(1024)S(1)} %get-tuple-element.435, s32[2048]{0:T(1024)S(1)} %bitcast.107, f32[2,2048,128]{2,1,0:T(8,128)} %get-tuple-element.437, s32[]{:T(128)S(6)} %copy.20, f32[768,128]{1,0:T(8,128)S(1)} %get-tuple-element.425, pred[]{:T(512)S(6)} %compare.13), kind=kOutput, calls=%fused_computation.15.clone.1 | convolution fusion | flops 2419261440 | bytes 1854469 | tf_op jit(solution)/shard_map/while/body/eval_jaxpr/while/body/eval_jaxpr/dot_general | solution.py:70
  154.3 11.8 %fusion.55 = f32[768,128]{1,0:T(8,128)S(1)} fusion(f32[2048]{0:T(1024)S(1)} %bitcast.106, s32[768]{0:T(1024)S(1)} %get-tuple-element.435, s32[2048]{0:T(1024)S(1)} %bitcast.107, f32[2,2048,128]{2,1,0:T(8,128)} %get-tuple-element.437, s32[]{:T(128)S(6)} %copy.20, f32[768,128]{1,0:T(8,128)S(1)} %get-tuple-element.425, pred[]{:T(512)S(6)} %compare.13), kind=kOutput, calls=%fused_computation.15.clone.1 | convolution fusion | flops 2419261440 | bytes 1854469 | tf_op jit(solution)/shard_map/while/body/eval_jaxpr/while/body/eval_jaxpr/dot_general | solution.py:70
  166.1 0.8 bitcast_dynamic-update-slice_fusion.2
  166.9 0.9 dynamic-slice_reduce_fusion.4
  167.9 0.9 dynamic-slice_reduce_fusion.5
  168.8 23.7 %while.49 = (s32[]{:T(128)}, f32[768,128]{1,0:T(8,128)S(1)}, s32[2,2048]{1,0:T(2,128)S(1)}, s32[768]{0:T(1024)S(1)}, f32[2,2048]{1,0:T(2,128)S(1)}, /*index=5*/f32[2,2048,128]{2,1,0:T(8,128)}, s32[]{:T(128)}, s32[]{:T(128)}) while((s32[]{:T(128)}, f32[768,128]{1,0:T(8,128)S(1)}, s32[2,2048]{1,0:T(2,128)S(1)}, ...), condition=%wide.region_14.14_spmd.clone, body=%wide.region_13.13_spmd.clone.sunk | while | flops 2419261440 | bytes 1887347 | solution.py:80
  168.8 11.8 %fusion.55 = f32[768,128]{1,0:T(8,128)S(1)} fusion(f32[2048]{0:T(1024)S(1)} %bitcast.106, s32[768]{0:T(1024)S(1)} %get-tuple-element.435, s32[2048]{0:T(1024)S(1)} %bitcast.107, f32[2,2048,128]{2,1,0:T(8,128)} %get-tuple-element.437, s32[]{:T(128)S(6)} %copy.20, f32[768,128]{1,0:T(8,128)S(1)} %get-tuple-element.425, pred[]{:T(512)S(6)} %compare.13), kind=kOutput, calls=%fused_computation.15.clone.1 | convolution fusion | flops 2419261440 | bytes 1854469 | tf_op jit(solution)/shard_map/while/body/eval_jaxpr/while/body/eval_jaxpr/dot_general | solution.py:70
  180.7 11.8 %fusion.55 = f32[768,128]{1,0:T(8,128)S(1)} fusion(f32[2048]{0:T(1024)S(1)} %bitcast.106, s32[768]{0:T(1024)S(1)} %get-tuple-element.435, s32[2048]{0:T(1024)S(1)} %bitcast.107, f32[2,2048,128]{2,1,0:T(8,128)} %get-tuple-element.437, s32[]{:T(128)S(6)} %copy.20, f32[768,128]{1,0:T(8,128)S(1)} %get-tuple-element.425, pred[]{:T(512)S(6)} %compare.13), kind=kOutput, calls=%fused_computation.15.clone.1 | convolution fusion | flops 2419261440 | bytes 1854469 | tf_op jit(solution)/shard_map/while/body/eval_jaxpr/while/body/eval_jaxpr/dot_general | solution.py:70
  192.5 0.8 bitcast_dynamic-update-slice_fusion.2
  193.3 0.9 dynamic-slice_reduce_fusion.4
  194.2 0.9 dynamic-slice_reduce_fusion.5
  195.1 23.7 %while.49 = (s32[]{:T(128)}, f32[768,128]{1,0:T(8,128)S(1)}, s32[2,2048]{1,0:T(2,128)S(1)}, s32[768]{0:T(1024)S(1)}, f32[2,2048]{1,0:T(2,128)S(1)}, /*index=5*/f32[2,2048,128]{2,1,0:T(8,128)}, s32[]{:T(128)}, s32[]{:T(128)}) while((s32[]{:T(128)}, f32[768,128]{1,0:T(8,128)S(1)}, s32[2,2048]{1,0:T(2,128)S(1)}, ...), condition=%wide.region_14.14_spmd.clone, body=%wide.region_13.13_spmd.clone.sunk | while | flops 2419261440 | bytes 1887347 | solution.py:80
  195.2 11.8 %fusion.55 = f32[768,128]{1,0:T(8,128)S(1)} fusion(f32[2048]{0:T(1024)S(1)} %bitcast.106, s32[768]{0:T(1024)S(1)} %get-tuple-element.435, s32[2048]{0:T(1024)S(1)} %bitcast.107, f32[2,2048,128]{2,1,0:T(8,128)} %get-tuple-element.437, s32[]{:T(128)S(6)} %copy.20, f32[768,128]{1,0:T(8,128)S(1)} %get-tuple-element.425, pred[]{:T(512)S(6)} %compare.13), kind=kOutput, calls=%fused_computation.15.clone.1 | convolution fusion | flops 2419261440 | bytes 1854469 | tf_op jit(solution)/shard_map/while/body/eval_jaxpr/while/body/eval_jaxpr/dot_general | solution.py:70
  207.0 11.8 %fusion.55 = f32[768,128]{1,0:T(8,128)S(1)} fusion(f32[2048]{0:T(1024)S(1)} %bitcast.106, s32[768]{0:T(1024)S(1)} %get-tuple-element.435, s32[2048]{0:T(1024)S(1)} %bitcast.107, f32[2,2048,128]{2,1,0:T(8,128)} %get-tuple-element.437, s32[]{:T(128)S(6)} %copy.20, f32[768,128]{1,0:T(8,128)S(1)} %get-tuple-element.425, pred[]{:T(512)S(6)} %compare.13), kind=kOutput, calls=%fused_computation.15.clone.1 | convolution fusion | flops 2419261440 | bytes 1854469 | tf_op jit(solution)/shard_map/while/body/eval_jaxpr/while/body/eval_jaxpr/dot_general | solution.py:70
  218.8 0.8 bitcast_dynamic-update-slice_fusion.2
  219.6 0.9 dynamic-slice_reduce_fusion.4
  220.5 0.9 dynamic-slice_reduce_fusion.5
  221.4 23.7 %while.49 = (s32[]{:T(128)}, f32[768,128]{1,0:T(8,128)S(1)}, s32[2,2048]{1,0:T(2,128)S(1)}, s32[768]{0:T(1024)S(1)}, f32[2,2048]{1,0:T(2,128)S(1)}, /*index=5*/f32[2,2048,128]{2,1,0:T(8,128)}, s32[]{:T(128)}, s32[]{:T(128)}) while((s32[]{:T(128)}, f32[768,128]{1,0:T(8,128)S(1)}, s32[2,2048]{1,0:T(2,128)S(1)}, ...), condition=%wide.region_14.14_spmd.clone, body=%wide.region_13.13_spmd.clone.sunk | while | flops 2419261440 | bytes 1887347 | solution.py:80
  221.5 11.8 %fusion.55 = f32[768,128]{1,0:T(8,128)S(1)} fusion(f32[2048]{0:T(1024)S(1)} %bitcast.106, s32[768]{0:T(1024)S(1)} %get-tuple-element.435, s32[2048]{0:T(1024)S(1)} %bitcast.107, f32[2,2048,128]{2,1,0:T(8,128)} %get-tuple-element.437, s32[]{:T(128)S(6)} %copy.20, f32[768,128]{1,0:T(8,128)S(1)} %get-tuple-element.425, pred[]{:T(512)S(6)} %compare.13), kind=kOutput, calls=%fused_computation.15.clone.1 | convolution fusion | flops 2419261440 | bytes 1854469 | tf_op jit(solution)/shard_map/while/body/eval_jaxpr/while/body/eval_jaxpr/dot_general | solution.py:70
  233.3 11.8 %fusion.55 = f32[768,128]{1,0:T(8,128)S(1)} fusion(f32[2048]{0:T(1024)S(1)} %bitcast.106, s32[768]{0:T(1024)S(1)} %get-tuple-element.435, s32[2048]{0:T(1024)S(1)} %bitcast.107, f32[2,2048,128]{2,1,0:T(8,128)} %get-tuple-element.437, s32[]{:T(128)S(6)} %copy.20, f32[768,128]{1,0:T(8,128)S(1)} %get-tuple-element.425, pred[]{:T(512)S(6)} %compare.13), kind=kOutput, calls=%fused_computation.15.clone.1 | convolution fusion | flops 2419261440 | bytes 1854469 | tf_op jit(solution)/shard_map/while/body/eval_jaxpr/while/body/eval_jaxpr/dot_general | solution.py:70
  245.9 2.4 fusion.28
  248.4 1.7 fusion.30
  250.1 5.2 %fusion.37 = f32[128,1536]{1,0:T(8,128)S(1)} fusion(bf16[3072,128]{1,0:T(8,128)(2,1)S(1)} %fusion.30, bf16[3072,1536]{1,0:T(8,128)(2,1)} %bitcast.104), kind=kOutput, calls=%fused_computation.76 | convolution fusion | flops 1207959552 | bytes 11010048 | tf_op jit(solution)/shard_map/dot_general | solution.py:145
  255.3 8.3 %all-reduce.3.cloned.1.call-done = f32[128,32,128]{2,0,1:T(8,128)} async-done(((f32[128,32,128]{2,0,1:T(8,128)}), f32[128,32,128]{2,0,1:T(8,128)}) %all-reduce.3.cloned.1.call-update) | async-done | bytes 2097168 | tf_op jit(solution)/shard_map/psum | solution.py:126
  263.6 0.9 constant_dynamic-slice_fusion.2
  264.9 1.2 fusion.27
  266.1 150.3 %all-reduce.5.cloned.1.call-done = f32[1536,128]{0,1:T(8,128)} async-done(((f32[1536,128]{0,1:T(8,128)}), f32[1536,128]{0,1:T(8,128)}) %all-reduce.5.cloned.1.call-update) | async-done | bytes 786448 | tf_op jit(solution)/shard_map/psum | solution.py:148
  416.4 2.3 copy.16
  (134 shorter events, 24.9 us)
Async XLA Ops:
  7.2 1.1 copy-start
  7.2 39.6 %all-gather.2.cloned.1.call-start = ((), (), s32[]{:S(2)}) async-start(), calls=%async_computation | async-start | bytes 1114112 | tf_op jit(solution)/shard_map/all_gather | solution.py:105
  9.7 0.8 copy-start.4
  10.5 253.1 %all-reduce.3.cloned.1.call-start = ((), (), s32[]{:S(2)}) async-start(), calls=%async_computation.1 | async-start | bytes 4194304 | tf_op jit(solution)/shard_map/psum | solution.py:126
  10.6 6.0 %copy-start.3 = (s32[128,32,4]{0,2,1:T(4,128)S(1)}, s32[128,32,4]{0,2,1:T(4,128)}, u32[]{:S(2)}) copy-start(s32[128,32,4]{0,2,1:T(4,128)} %param.17) | copy-start | bytes 196612
  26.0 20.7 %copy-start.10 = (s32[4]{0:T(128)S(1)}, s32[4]{0:T(128)}, u32[]{:S(2)}) copy-start(s32[4]{0:T(128)} %param.16) | copy-start | bytes 52
  131.5 2.9 copy-start.6
  131.5 2.9 copy-start.7
  131.5 2.9 copy-start.8
  131.5 2.9 copy-start.9
  131.6 2.9 copy-start.11
  140.3 276.1 %all-reduce.5.cloned.1.call-start = ((), (), s32[]{:S(2)}) async-start(), calls=%async_computation.2 | async-start | bytes 1572864 | tf_op jit(solution)/shard_map/psum | solution.py:148
  245.9 2.4 copy-start.1
  250.1 14.5 %copy-start.5 = (f32[256]{0:T(256)S(1)}, f32[256]{0:T(256)}, u32[]{:S(2)}) copy-start(f32[256]{0:T(256)} %copy-done.4) | copy-start | bytes 3076
  264.6 154.1 %copy-start.2 = (f32[8,32,128]{2,1,0:T(8,128)}, f32[8,32,128]{2,1,0:T(8,128)S(1)}, u32[]{:S(2)}) copy-start(f32[8,32,128]{2,1,0:T(8,128)S(1)} %copy.14) | copy-start | bytes 393220
Sparse Core Ops, SparseCore 0:
  10.6 36.1 all-gather.1
  140.5 123.1 all-reduce.2
  268.9 147.5 all-reduce.4
where the time goes:
time: 427 us; the launch traced here: 425 us
  waiting for transfers between devices  176 us (41%)
  matrix products  147 us (34%)
  local copies, waits for them, and re-layouts  35 us (8%)
  blocking collectives  26.8 us (6%)
  other arithmetic  17.6 us (4%)
  between operations  13.9 us (3%)
  loops' own time  8.81 us (2%)
    psum x1, waiting for transfers between devices, per_device(): weight_grad = lax.psum(local_grad, ('dp', 'gallery'))  150 us
    dot_general x8, matrix products, one_block(): lax.dot_general(table, query_block, (((0,), (0,)), ((), ())), precision=l...  94.2 us
    psum x1, blocking collectives, per_device(): total = lax.psum(jnp.sum(expo, axis=1), 'gallery')  26.8 us
    dot_general x12, matrix products, one_tile(): lax.dot_general(query_tokens, block, (((1,), (1,)), ((), ())), preferred_...  23.3 us
    all_gather x1, waiting for transfers between devices, per_device(): every_query = lax.all_gather(query_unit, 'gallery', axis=0, tiled=True)  17.3 us
    dot_general x4, matrix products, per_device(): chosen = jnp.dot(table, page_unit[page], preferred_element_type=jnp.float32)  16.2 us
  transfers between devices with their start and end apart: 3, of which 3 were waited for; matrix products, arithmetic and copies ran while one was open for 31% of the time, Pallas kernels for 0%

commit v1 on v0

v1 whole, which is shorter than its diff:
```python
import jax
import jax.numpy as jnp
from jax import lax
from jax.experimental import pallas as pl
from jax.experimental.pallas import tpu as pltpu
from jax.sharding import PartitionSpec as P

F32 = jnp.float32
BF16 = jnp.bfloat16
EPSILON = 1e-06
TEMPERATURE = 0.02
VMEM_LIMIT = 48 * 1024 * 1024

NT = (((1,), (1,)), ((), ()))
TN = (((0,), (0,)), ((), ()))


def inverse_norm(raw):
    return lax.rsqrt(jnp.sum(raw * raw, axis=1, keepdims=True) + EPSILON)


def unit_backward(grad_unit, raw, inverse):
    unit = raw * inverse
    return (grad_unit - unit * jnp.sum(unit * grad_unit, axis=1, keepdims=True)) * inverse


def lane_iota(shape):
    return lax.broadcasted_iota(jnp.int32, shape, len(shape) - 1)


def query_kernel(hidden_ref, weight_ref, raw_ref, unit_ref):
    raw = jnp.dot(hidden_ref[...], weight_ref[...], preferred_element_type=F32)
    raw_ref[...] = raw
    unit_ref[...] = (raw * inverse_norm(raw)).astype(BF16)


def page_kernel(length_ref, hidden_ref, weight_ref, index_ref, raw_ref, unit_ref, chosen_ref):
    page = pl.program_id(0)
    raw = jnp.dot(hidden_ref[0], weight_ref[...], preferred_element_type=F32)
    raw_ref[0] = raw
    unit = raw * inverse_norm(raw)
    slots = raw.shape[0]
    rows = lax.broadcasted_iota(jnp.int32, raw.shape, 0)
    unit_ref[0] = jnp.where(rows < length_ref[page], unit, unit[0:1]).astype(BF16)
    unit_t = unit.T.astype(BF16)
    positions = lax.broadcasted_iota(jnp.int32, (slots, 256), 0)

    def one_tile(tile, carry):
        at = pl.ds(pl.multiple_of(tile * 256, 256), 256)
        table = jnp.where(index_ref[0, :, at] == positions, 1.0, 0.0).astype(BF16)
        chosen_ref[0, :, at] = jnp.dot(unit_t, table, preferred_element_type=F32).astype(BF16)
        return carry

    lax.fori_loop(0, index_ref.shape[2] // 256, one_tile, 0)


def score_kernel(multiplier, rank_ref, query_ref, unit_ref, chosen_ref, expo_ref, send_ref, own_ref, target_ref, best, total):
    tile = pl.program_id(0)
    pages, slots, dim = unit_ref.shape
    queries = query_ref[0]
    for page in range(pages):
        top = None
        for start in range(0, slots, 256):
            scores = lax.dot_general(unit_ref[page, start:start + 256], queries, NT, preferred_element_type=F32)
            part = jnp.max(scores.reshape(32, 8, 256), axis=0)
            top = part if top is None else jnp.maximum(top, part)
        best[page:page + 1, :] = jnp.max(top, axis=0, keepdims=True)
    segment = jnp.where(
        lax.broadcasted_iota(jnp.int32, (256, 256), 0) // 32 == lane_iota((256, 256)) // 32, 1.0, 0.0
    ).astype(BF16)
    value = best[...]
    score = jnp.zeros_like(value)
    for _ in range(3):
        part = value.astype(BF16)
        score = score + jnp.dot(part, segment, preferred_element_type=F32)
        value = value - part.astype(F32)
    expo = jnp.exp(score * multiplier)
    mixed = jnp.zeros((dim, 256), F32)
    for page in range(pages):
        expo_ref[page, pl.ds(tile, 1), :] = expo[page:page + 1]
        mixed = mixed + expo[page:page + 1] * chosen_ref[page].astype(F32)
    mixed = mixed.T
    send_ref[tile, 0:256, :] = mixed.astype(BF16)
    row = jnp.sum(expo[0:pages], axis=0, keepdims=True)
    total[pl.ds(tile, 1), :] = jnp.where(lane_iota((1, 128)) % 32 < 16, row[:, :128], row[:, 128:])

    @pl.when(tile == rank_ref[0])
    def _():
        own_ref[...] = mixed
        picked = jnp.zeros((dim, 256), F32)
        for page in range(pages):
            picked = jnp.where(lane_iota((dim, 256)) // 64 == page, chosen_ref[page].astype(F32), picked)
        target_ref[...] = picked.T

    @pl.when(tile == pl.num_programs(0) - 1)
    def _():
        high = total[...].astype(BF16)
        low = (total[...] - high.astype(F32)).astype(BF16)
        for block in range(send_ref.shape[0]):
            send_ref[block, 256:272, :] = high
            send_ref[block, 272:288, :] = low


def gradient_kernel(multiplier, rank_ref, index_ref, expo_ref, received_ref, own_ref, target_ref, query_ref, page_raw_ref,
                    hidden_ref, query_raw_ref, query_hidden_ref, weight_ref, query_grad_ref, inverse_total, score_grad, accumulated):
    page = pl.program_id(0)
    rank = rank_ref[0]
    tiles = query_ref.shape[0]
    slots = hidden_ref.shape[1]

    @pl.when(page == 0)
    def _():
        total = jnp.zeros((tiles, 128), F32)
        for source in range(tiles):
            total = total + received_ref[source, 256:272, :].astype(F32) + received_ref[source, 272:288, :].astype(F32)
        inverse = 1.0 / total
        low_half = lane_iota((tiles, 128)) % 32 < 16
        inverse_total[:, 0:128] = jnp.where(low_half, inverse, pltpu.roll(inverse, 16, 1))
        inverse_total[:, 128:256] = jnp.where(low_half, pltpu.roll(inverse, 112, 1), inverse)
        summed = own_ref[...]
        for source in range(tiles):
            summed = summed + jnp.where(rank == source, 0.0, received_ref[source, 0:256, :].astype(F32))
        scale = jnp.broadcast_to(inverse_total[pl.ds(rank, 1), :], (128, 256)).T
        query_grad = (summed * scale - target_ref[...]) * multiplier
        query_grad_ref[...] = query_grad
        raw = query_raw_ref[...]
        direction = unit_backward(query_grad, raw, inverse_norm(raw)).astype(BF16)
        accumulated[...] = lax.dot_general(direction, query_hidden_ref[...], TN, preferred_element_type=F32)

    is_target = (lax.broadcasted_iota(jnp.int32, (tiles, 256), 0) == rank) & (lane_iota((tiles, 256)) // 64 == page)
    score_grad[...] = (expo_ref[0] * inverse_total[...] - jnp.where(is_target, 1.0, 0.0)) * multiplier
    positions = lax.broadcasted_iota(jnp.int32, (slots, 256), 0)

    def one_group(group, grad):
        for inner in range(4):
            tile = group * 4 + inner
            at = pl.ds(pl.multiple_of(tile * 256, 256), 256)
            table = jnp.where(index_ref[0, :, at] == positions, score_grad[pl.ds(tile, 1), :], 0.0).astype(BF16)
            grad = grad + jnp.dot(table, query_ref[tile], preferred_element_type=F32)
        return grad

    grad = lax.fori_loop(0, tiles // 4, one_group, jnp.zeros((slots, 128), F32))
    raw = page_raw_ref[0]
    direction = unit_backward(grad, raw, inverse_norm(raw)).astype(BF16)
    accumulated[...] += lax.dot_general(direction, hidden_ref[0], TN, preferred_element_type=F32)

    @pl.when(page == pl.num_programs(0) - 1)
    def _():
        weight_ref[...] = accumulated[...].T.astype(BF16)


def whole(shape):
    return pl.BlockSpec(shape, lambda i: (0,) * len(shape))


def per_device(query_hidden, document_states, projection, lengths, best_token):
    query_count, tokens, hidden_size = query_hidden.shape
    pages, slots, _ = document_states.shape
    dim = projection.shape[1]
    ranks = lax.axis_size("gallery")
    rank = lax.axis_index("gallery").astype(jnp.int32).reshape(1)
    rows = query_count * tokens
    all_rows = rows * ranks
    multiplier = 1.0 / (tokens * TEMPERATURE)
    smem = pl.BlockSpec(memory_space=pltpu.SMEM)
    params = pltpu.CompilerParams(vmem_limit_bytes=VMEM_LIMIT)
    query_rows = query_hidden.reshape(rows, hidden_size)

    query_raw, query_unit = pl.pallas_call(
        query_kernel,
        out_shape=(jax.ShapeDtypeStruct((rows, dim), F32), jax.ShapeDtypeStruct((rows, dim), BF16)),
        compiler_params=params,
        name="query_project",
    )(query_rows, projection)
    every_query = lax.all_to_all(jnp.broadcast_to(query_unit[None], (ranks, rows, dim)), "gallery", 0, 0, tiled=True)

    index = jnp.transpose(best_token, (2, 0, 1)).reshape(pages, 1, all_rows)
    page_raw, page_unit, chosen = pl.pallas_call(
        page_kernel,
        grid=(pages,),
        in_specs=[
            smem,
            pl.BlockSpec((1, slots, hidden_size), lambda i: (i, 0, 0)),
            whole((hidden_size, dim)),
            pl.BlockSpec((1, 1, all_rows), lambda i: (i, 0, 0)),
        ],
        out_specs=[
            pl.BlockSpec((1, slots, dim), lambda i: (i, 0, 0)),
            pl.BlockSpec((1, slots, dim), lambda i: (i, 0, 0)),
            pl.BlockSpec((1, dim, all_rows), lambda i: (i, 0, 0)),
        ],
        out_shape=(
            jax.ShapeDtypeStruct((pages, slots, dim), F32),
            jax.ShapeDtypeStruct((pages, slots, dim), BF16),
            jax.ShapeDtypeStruct((pages, dim, all_rows), BF16),
        ),
        compiler_params=params,
        cost_estimate=pl.CostEstimate(flops=2 * pages * slots * dim * (hidden_size + all_rows), bytes_accessed=16 << 20, transcendentals=0),
        name="page_project",
    )(lengths, document_states, projection, index)

    expo, send, own, target = pl.pallas_call(
        lambda *refs: score_kernel(multiplier, *refs),
        grid=(ranks,),
        in_specs=[
            smem,
            pl.BlockSpec((1, rows, dim), lambda i: (i, 0, 0)),
            whole((pages, slots, dim)),
            pl.BlockSpec((pages, dim, rows), lambda i: (0, 0, i)),
        ],
        out_specs=[whole((pages, ranks, rows)), whole((ranks, rows + 32, dim)), whole((rows, dim)), whole((rows, dim))],
        out_shape=(
            jax.ShapeDtypeStruct((pages, ranks, rows), F32),
            jax.ShapeDtypeStruct((ranks, rows + 32, dim), BF16),
            jax.ShapeDtypeStruct((rows, dim), F32),
            jax.ShapeDtypeStruct((rows, dim), F32),
        ),
        scratch_shapes=[pltpu.VMEM((8, rows), F32), pltpu.VMEM((ranks, 128), F32)],
        compiler_params=params,
        cost_estimate=pl.CostEstimate(flops=2 * pages * slots * dim * all_rows, bytes_accessed=8 << 20, transcendentals=0),
        name="scores",
    )(rank, every_query, page_unit, chosen)
    received = lax.all_to_all(send, "gallery", 0, 0, tiled=True)

    weight_part, query_grad = pl.pallas_call(
        lambda *refs: gradient_kernel(multiplier, *refs),
        grid=(pages,),
        in_specs=[
            smem,
            pl.BlockSpec((1, 1, all_rows), lambda i: (i, 0, 0)),
            pl.BlockSpec((1, ranks, rows), lambda i: (i, 0, 0)),
            whole((ranks, rows + 32, dim)),
            whole((rows, dim)),
            whole((rows, dim)),
            whole((ranks, rows, dim)),
            pl.BlockSpec((1, slots, dim), lambda i: (i, 0, 0)),
            pl.BlockSpec((1, slots, hidden_size), lambda i: (i, 0, 0)),
            whole((rows, dim)),
            whole((rows, hidden_size)),
        ],
        out_specs=[whole((hidden_size, dim)), whole((rows, dim))],
        out_shape=(jax.ShapeDtypeStruct((hidden_size, dim), BF16), jax.ShapeDtypeStruct((rows, dim), F32)),
        scratch_shapes=[pltpu.VMEM((ranks, rows), F32), pltpu.VMEM((ranks, rows), F32), pltpu.VMEM((dim, hidden_size), F32)],
        compiler_params=params,
        cost_estimate=pl.CostEstimate(flops=2 * pages * slots * dim * (hidden_size + all_rows), bytes_accessed=16 << 20, transcendentals=0),
        name="gradients",
    )(rank, index, expo, received, own, target, every_query, page_raw, document_states, query_raw, query_rows)

    devices = ranks * lax.axis_size("dp")
    chunk = hidden_size // devices
    parts = lax.all_to_all(weight_part.reshape(devices, chunk, dim), ("dp", "gallery"), 0, 0, tiled=True)
    mine = jnp.sum(parts.astype(F32), axis=0).astype(BF16)
    shared = lax.all_to_all(jnp.broadcast_to(mine[None], (devices, chunk, dim)), ("dp", "gallery"), 0, 0, tiled=True)
    weight_grad = shared.reshape(hidden_size, dim).astype(F32)
    return (weight_grad, query_grad.reshape(query_count, tokens, dim))


def solution(mesh):
    return jax.shard_map(
        per_device,
        mesh=mesh,
        in_specs=(
            P(("dp", "gallery"), None, None),
            P(("dp", "gallery"), None, None),
            P(),
            P(("dp", "gallery")),
            P("dp", None, "gallery"),
        ),
        out_specs=(P(), P(("dp", "gallery"), None, None)),
        check_vma=False,
    )
```

time: 427 us -> 132 us (0.31)
  waiting for transfers between devices: 176 us -> 0.01 us
  matrix products: 147 us -> 0 us
  Pallas kernels: 0 us -> 53.7 us
  blocking collectives: 26.8 us -> 62.4 us
  local copies, waits for them, and re-layouts: 35 us -> 6.74 us
  other arithmetic: 17.6 us -> 0.14 us
  between operations: 13.9 us -> 0.72 us
  loops' own time: 8.81 us -> 0 us
  starting transfers between devices: 0.3 us -> 7.47 us
    psum x2 -> x0, waiting for transfers between devices: 159 us -> none  [the longest x1 150 us: per_device(): weight_grad = lax.psum(local_grad, ('dp', 'gallery'))]
    dot_general x28 -> x0, matrix products: 147 us -> none  [the longest x8 94.2 us: one_block(): lax.dot_general(table, query_block, (((0,), (0,)), ((), ())), precision=l...]
    all_to_all x0 -> x3, blocking collectives: none -> 62.4 us  [the longest x1 23 us: per_device(): received = lax.all_to_all(send, 'gallery', 0, 0, tiled=True)]
    pallas_call x0 -> x4, Pallas kernels: none -> 53.7 us  [the longest x1 20.9 us: per_device(): pl.pallas_call(page_kernel, grid=(pages,), in_specs=[smem, pl.BlockSpec((...]
    psum x1 -> x0, blocking collectives: 26.8 us -> none  [per_device(): total = lax.psum(jnp.sum(expo, axis=1), 'gallery')]
    dynamic_slice x42 -> x0, local copies, waits for them, and re-layouts: 18 us -> none  [the longest x12 7.36 us: one_page(): best, unused = lax.scan(one_tile, start_best, jnp.arange(tile_count))]
    all_gather x1 -> x0, waiting for transfers between devices: 17.3 us -> none  [per_device(): every_query = lax.all_gather(query_unit, 'gallery', axis=0, tiled=True)]
    dynamic_update_slice x8 -> x0, local copies, waits for them, and re-layouts: 9.42 us -> none  [the longest x4 6.2 us: page_maxima(): unused, maxima = lax.scan(one_page, 0, (page_units, page_lengths))]
  transfers between devices with their start and end apart: 3 -> 1, of which waited for: 3 -> 0; matrix products, arithmetic and copies ran while one was open for 31% -> 0% of each run, Pallas kernels for 0% -> 16%
where the time goes in v1:
time: 132 us; the launch traced here: 131 us
  blocking collectives  62.4 us (47%)
  Pallas kernels  53.7 us (41%)
  starting transfers between devices  7.47 us (6%)
  local copies, waits for them, and re-layouts  6.74 us (5%)
    all_to_all x1, blocking collectives, per_device(): received = lax.all_to_all(send, 'gallery', 0, 0, tiled=True)  23 us
    all_to_all x1, blocking collectives, per_device(): lax.all_to_all(weight_part.reshape(devices, chunk, dim), ('dp', 'gallery'...  21.4 us
    pallas_call x1, Pallas kernels, per_device(): pl.pallas_call(page_kernel, grid=(pages,), in_specs=[smem, pl.BlockSpec((...  20.9 us
    all_to_all x1, blocking collectives, per_device(): lax.all_to_all(jnp.broadcast_to(mine[None], (devices, chunk, dim)), ('dp'...  18.1 us
    pallas_call x1, Pallas kernels, per_device(): pl.pallas_call(lambda *refs: score_kernel(multiplier, *refs), grid=(ranks...  16.4 us
    pallas_call x1, Pallas kernels, per_device(): pl.pallas_call(lambda *refs: gradient_kernel(multiplier, *refs), grid=(pa...  15.9 us
    all_to_all x1, starting transfers between devices, per_device(): lax.all_to_all(jnp.broadcast_to(query_unit[None], (ranks, rows, dim)), 'g...  7.47 us
    unnamed x16, local copies, waits for them, and re-layouts  4.16 us
  transfers between devices with their start and end apart: 1, of which 0 were waited for; matrix products, arithmetic and copies ran while one was open for 0% of the time, Pallas kernels for 16%

profile of v1, /device:TPU:1, one launch (start us, length us, event | category | flops | bytes accessed | tf_op | source)
XLA Modules:
  0.0 131.1 jit_solution(13589294327776883071)
XLA Ops:
  0.6 0.0 copy-start
  0.6 1.1 copy-done
  1.8 0.0 copy-start.2
  1.8 1.0 copy-done.2
  2.8 0.4 query_project.1
  3.2 0.0 copy-start.7
  3.2 1.2 broadcast_in_dim.4
  4.4 0.0 copy-start.3
  4.4 0.0 copy-start.4
  4.4 7.5 %all-to-all-start = ((bf16[16,256,128]{2,1,0:T(8,128)(2,1)}), bf16[16,256,128]{2,1,0:T(8,128)(2,1)S(1)}, u32[]{:S(2)}, u32[]{:S(2)}) async-start(bf16[16,256,128]{2,1,0:T(8,128)(2,1)} %broadcast_in_dim.4), calls=%async_computation | async-start | bytes 2097152 | tf_op jit(solution)/shard_map/all_to_all | solution.py:175
  11.9 0.0 copy-done.7
  11.9 0.1 copy.8
  12.0 0.2 reshape.30.index_ref.refs_1_
  12.2 0.0 copy-done.3
  12.2 0.0 copy-done.4
  12.2 20.9 %page_project.1 = (f32[4,768,128]{2,1,0:T(8,128)S(1)}, bf16[4,768,128]{2,1,0:T(8,128)(2,1)S(1)}, bf16[4,128,4096]{2,1,0:T(8,128)(2,1)}) custom-call(s32[4]{0:T(128)S(1)} %copy-done.4, bf16[4,768,1536]{2,1,0:T(8,128)(2,1)} %refs_8_.1, bf16[1536,128]{1,0:T(8,128)(2,1)S(1)} %copy-done.3, s32[4,1,4096]{2,1,0:T(1,128)S(1)} %reshape.30.index_ref.refs_1_), custom_call_target="tpu_custom_call" | custom-call | flops 4429185024 | bytes 16777216 | tf_op jit(solution)/shard_map/page_project/pallas_call | solution.py:178
  33.1 0.0 copy-start.5
  33.1 0.9 copy-done.5
  34.0 0.0 all-to-all-done.refs_1_.refs_6_
  34.0 0.0 copy-start.6
  34.0 1.1 copy-done.6
  35.1 16.4 %scores.1 = (f32[4,16,256]{2,1,0:T(8,128)S(1)}, bf16[16,288,128]{2,1,0:T(8,128)(2,1)S(1)}, f32[256,128]{1,0:T(8,128)S(1)}, f32[256,128]{1,0:T(8,128)S(1)}) custom-call(s32[1]{0:T(128)} %bitcast.refs_0_, bf16[16,256,128]{2,1,0:T(8,128)(2,1)S(1)} %all-to-all-done.refs_1_.refs_6_, bf16[4,768,128]{2,1,0:T(8,128)(2,1)S(1)} %copy-done.6, ...), custom_call_target="tpu_custom_call" | custom-call | flops 3221225472 | bytes 8388608 | tf_op jit(solution)/shard_map/scores/pallas_call | solution.py:202
  51.5 0.0 copy-start.1
  51.5 23.0 %all_to_all.20.refs_3_ = bf16[16,288,128]{2,1,0:T(8,128)(2,1)S(1)} all-to-all(bf16[16,288,128]{2,1,0:T(8,128)(2,1)S(1)} %get-tuple-element.17), channel_id=1, replica_groups=mesh['dp'=8,'gallery'=16] {'gallery'}, dimensions={0} | all-to-all | bytes 2359296 | tf_op jit(solution)/shard_map/all_to_all | solution.py:223
  74.5 0.0 copy-done.1
  74.5 15.9 %gradients.1 = (bf16[1536,128]{1,0:T(8,128)(2,1)S(1)}, f32[256,128]{1,0:T(8,128)}) custom-call(s32[1]{0:T(128)} %bitcast.refs_0_, s32[4,1,4096]{2,1,0:T(1,128)S(1)} %reshape.30.index_ref.refs_1_, f32[4,16,256]{2,1,0:T(8,128)S(1)} %get-tuple-element.16.refs_2_, bf16[16,288,128]{2,1,0:T(8,128)(2,1)S(1)} %all_to_all.20.refs_3_, ...), custom_call_target="tpu_custom_call" | custom-call | flops 4429185024 | bytes 16777216 | tf_op jit(solution)/shard_map/gradients/pallas_call | solution.py:225
  90.4 0.1 reshape.27
  90.5 21.4 %all_to_all.21 = bf16[128,12,128]{2,1,0:T(8,128)(2,1)S(1)} all-to-all(bf16[128,12,128]{2,1,0:T(8,128)(2,1)S(1)} %reshape.27), channel_id=1, replica_groups=mesh['dp'=8,'gallery'=16] {'dp','gallery'}, dimensions={0} | all-to-all | bytes 786432 | tf_op jit(solution)/shard_map/all_to_all | solution.py:251
  111.9 0.1 reduce_sum.12
  112.0 0.1 broadcast_in_dim.5
  112.1 18.1 %all_to_all.22 = bf16[128,12,128]{2,1,0:T(8,128)(2,1)S(1)} all-to-all(bf16[128,12,128]{2,1,0:T(8,128)(2,1)S(1)} %broadcast_in_dim.5), channel_id=1, replica_groups=mesh['dp'=8,'gallery'=16] {'dp','gallery'}, dimensions={0} | all-to-all | bytes 786432 | tf_op jit(solution)/shard_map/all_to_all | solution.py:253
  130.2 1.0 reshape.29
Async XLA Ops:
  0.6 1.1 copy-start
  1.8 1.0 copy-start.2
  3.2 8.7 %copy-start.7 = (s32[128,32,4]{0,2,1:T(4,128)S(1)}, s32[128,32,4]{0,2,1:T(4,128)}, u32[]{:S(2)}) copy-start(s32[128,32,4]{0,2,1:T(4,128)} %param.9) | copy-start | bytes 196612
  4.4 7.8 %copy-start.3 = (bf16[1536,128]{1,0:T(8,128)(2,1)S(1)}, bf16[1536,128]{1,0:T(8,128)(2,1)}, u32[]{:S(2)}) copy-start(bf16[1536,128]{1,0:T(8,128)(2,1)} %weight_ref.3) | copy-start | bytes 1179652
  4.4 7.8 %copy-start.4 = (s32[4]{0:T(128)S(1)}, s32[4]{0:T(128)}, u32[]{:S(2)}) copy-start(s32[4]{0:T(128)} %length_ref.1) | copy-start | bytes 52
  4.4 29.6 %all-to-all-start = ((bf16[16,256,128]{2,1,0:T(8,128)(2,1)}), bf16[16,256,128]{2,1,0:T(8,128)(2,1)S(1)}, u32[]{:S(2)}, u32[]{:S(2)}) async-start(bf16[16,256,128]{2,1,0:T(8,128)(2,1)} %broadcast_in_dim.4), calls=%async_computation | async-start | bytes 2097152 | tf_op jit(solution)/shard_map/all_to_all | solution.py:175
  33.1 0.9 copy-start.5
  34.0 1.1 copy-start.6
  51.5 23.0 %copy-start.1 = (bf16[8,32,1536]{2,1,0:T(8,128)(2,1)S(1)}, bf16[8,32,1536]{2,1,0:T(8,128)(2,1)}, u32[]{:S(2)}) copy-start(bf16[8,32,1536]{2,1,0:T(8,128)(2,1)} %param.5) | copy-start | bytes 2359300

commit v2 on v1

v2 whole, which is shorter than its diff:
```python
import jax
import jax.numpy as jnp
from jax import lax
from jax.experimental import pallas as pl
from jax.experimental.pallas import tpu as pltpu
from jax.sharding import Mesh, PartitionSpec as P

F32 = jnp.float32
BF16 = jnp.bfloat16
EPSILON = 1e-06
TEMPERATURE = 0.02
MIB = 1024 * 1024

NT = (((1,), (1,)), ((), ()))
TN = (((0,), (0,)), ((), ()))


def inverse_norm(raw, axis):
    value = jnp.sum(raw * raw, axis=axis, keepdims=True) + EPSILON
    guess = lax.rsqrt(value)
    return guess * (1.5 - 0.5 * value * guess * guess)


def unit_backward(grad_unit, raw):
    inverse = inverse_norm(raw, 0)
    unit = raw * inverse
    return (grad_unit - unit * jnp.sum(unit * grad_unit, axis=0, keepdims=True)) * inverse


def iota(shape, axis):
    return lax.broadcasted_iota(jnp.int32, shape, axis)


def one_hot(index, rows):
    return jnp.where(iota((rows, index.shape[1]), 0) == index, 1.0, 0.0).astype(BF16)


def query_kernel(hidden_ref, weight_ref, raw_ref, send_ref):
    raw = jnp.dot(hidden_ref[...], weight_ref[...], preferred_element_type=F32).T
    raw_ref[...] = raw
    unit = (raw * inverse_norm(raw, 0)).astype(BF16)
    for block in range(send_ref.shape[0]):
        send_ref[block] = unit


def page_kernel(length_ref, hidden_ref, weight_ref, index_ref, raw_ref, unit_ref, chosen_ref):
    page = pl.program_id(0)
    raw = jnp.dot(hidden_ref[0], weight_ref[...], preferred_element_type=F32)
    raw_t = raw.T
    raw_ref[0] = raw_t
    unit = raw_t * inverse_norm(raw_t, 0)
    slots = unit.shape[1]
    unit_ref[0] = jnp.where(iota(unit.shape, 1) < length_ref[page], unit, unit[:, 0:1]).T.astype(BF16)
    unit = unit.astype(BF16)
    parts = slots // 256
    table = jnp.concatenate([unit[:, part * 256:(part + 1) * 256] for part in range(parts)], axis=0)

    def one_tile(tile, carry):
        index = index_ref[0, pl.ds(tile, 1), :]
        found = jnp.dot(table, one_hot(index & 255, 256), preferred_element_type=F32)
        which = index >> 8
        chosen = found[0:128]
        for part in range(1, parts):
            chosen = jnp.where(which == part, found[part * 128:(part + 1) * 128], chosen)
        chosen_ref[0, tile] = chosen.astype(BF16)
        return carry

    lax.fori_loop(0, index_ref.shape[1], one_tile, 0, unroll=4)


def best_scores(queries, unit_ref, out, row):
    for page in range(unit_ref.shape[0]):
        scores = jnp.dot(unit_ref[page], queries, preferred_element_type=F32)
        top = jnp.max(scores.reshape(-1, 8, scores.shape[1]), axis=0)
        out[page, pl.ds(row, 1), :] = jnp.max(top, axis=0, keepdims=True)


def near_kernel(query_ref, unit_ref, best_ref):
    def one_tile(tile, carry):
        best_scores(query_ref[tile], unit_ref, best_ref, tile)
        return carry

    lax.fori_loop(0, query_ref.shape[0], one_tile, 0, unroll=2)


def far_kernel(multiplier, place_ref, query_ref, unit_ref, near_ref, chosen_ref, expo_ref, keep_ref, total_ref, pair_ref, target_ref, best):
    core, chip = place_ref[0], place_ref[1]
    pages, chips = near_ref.shape[:2]
    dim, lanes = query_ref.shape[1:]
    near = pl.multiple_of(core * chips, chips)
    far = pl.multiple_of((1 - core) * chips, chips)
    for page in range(pages):
        best[page, pl.ds(near, chips), :] = near_ref[page]

    def one_tile(tile, carry):
        best_scores(query_ref[tile], unit_ref, best, far + tile)
        return carry

    lax.fori_loop(0, chips, one_tile, 0, unroll=2)

    segment = jnp.where(iota((lanes, lanes), 0) // 32 == iota((lanes, lanes), 1) // 32, 1.0, 0.0).astype(BF16)
    value = best[...].reshape(pages * 2 * chips, lanes)
    score = jnp.zeros_like(value)
    for _ in range(3):
        part = value.astype(BF16)
        score = score + jnp.dot(part, segment, preferred_element_type=F32)
        value = value - part.astype(F32)
    expo = jnp.exp(score * multiplier).reshape(pages, 2 * chips, lanes)
    expo_ref[...] = expo
    total = jnp.sum(expo, axis=0)
    total = jnp.where(iota((2 * chips, 128), 1) % 32 < 16, total[:, :128], total[:, 128:])
    total_ref[...] = total
    high = total.astype(BF16)
    low = (total - high.astype(F32)).astype(BF16)

    def mixed(tile):
        result = jnp.zeros((dim, lanes), F32)
        for page in range(pages):
            result = result + expo_ref[page, pl.ds(tile, 1), :] * chosen_ref[page, tile].astype(F32)
        return result

    def one_mix(tile, carry):
        pair_ref[tile, 0:dim, :] = mixed(far + tile).astype(BF16)
        pair_ref[tile, dim:dim + 16, 0:128] = high
        pair_ref[tile, dim:dim + 16, 128:256] = low
        keep_ref[tile] = mixed(near + tile)
        return carry

    lax.fori_loop(0, chips, one_mix, 0, unroll=2)
    picked = jnp.zeros((dim, lanes), F32)
    for page in range(pages):
        picked = jnp.where(iota((dim, lanes), 1) // 64 == page, chosen_ref[page, near + chip].astype(F32), picked)
    target_ref[...] = picked


def add_kernel(place_ref, keep_ref, total_ref, pair_ref, send_ref, own_ref):
    chips, dim, _ = keep_ref.shape
    total = total_ref[...] + (pair_ref[0, dim:dim + 16, 0:128].astype(F32) + pair_ref[0, dim:dim + 16, 128:256].astype(F32))
    high = total.astype(BF16)
    low = (total - high.astype(F32)).astype(BF16)
    for tile in range(chips):
        send_ref[tile, 0:dim, :] = (keep_ref[tile] + pair_ref[tile, 0:dim, :].astype(F32)).astype(BF16)
        send_ref[tile, dim:dim + 16, 0:128] = high
        send_ref[tile, dim:dim + 16, 128:256] = low
    chip = place_ref[1]
    own_ref[...] = keep_ref[chip] + pair_ref[chip, 0:dim, :].astype(F32)


def gradient_kernel(multiplier, place_ref, index_ref, expo_ref, received_ref, own_ref, target_ref, near_ref, far_ref, page_raw_ref,
                    hidden_ref, query_raw_ref, query_hidden_ref, weight_ref, query_grad_ref, inverse_total, score_grad, query_scratch, accumulated):
    page = pl.program_id(0)
    core, chip = place_ref[0], place_ref[1]
    chips, dim, lanes = near_ref.shape
    tiles = 2 * chips
    mine = core * chips + chip
    slots = hidden_ref.shape[1]
    parts = slots // 256

    @pl.when(page == 0)
    def _():
        total = jnp.zeros((tiles, 128), F32)
        for source in range(chips):
            total = total + received_ref[source, dim:dim + 16, 0:128].astype(F32) + received_ref[source, dim:dim + 16, 128:256].astype(F32)
        inverse = 1.0 / total
        first = iota((tiles, 128), 1) % 32 < 16
        inverse_total[:, 0:128] = jnp.where(first, inverse, pltpu.roll(inverse, 16, 1))
        inverse_total[:, 128:256] = jnp.where(first, pltpu.roll(inverse, 112, 1), inverse)
        summed = own_ref[...]
        for source in range(chips):
            summed = summed + jnp.where(chip == source, 0.0, received_ref[source, 0:dim, :].astype(F32))
        query_grad = (summed * inverse_total[pl.ds(mine, 1), :] - target_ref[...]) * multiplier
        query_grad_ref[...] = query_grad.T
        direction = unit_backward(query_grad, query_raw_ref[...]).astype(BF16)
        accumulated[...] = jnp.dot(direction, query_hidden_ref[...], preferred_element_type=F32)
        query_scratch[pl.ds(core * chips, chips)] = near_ref[...]
        query_scratch[pl.ds((1 - core) * chips, chips)] = far_ref[...]

    is_target = (iota((tiles, lanes), 0) == mine) & (iota((tiles, lanes), 1) // 64 == page)
    score_grad[...] = (expo_ref[0] * inverse_total[...] - jnp.where(is_target, 1.0, 0.0)) * multiplier

    def one_group(group, grad):
        lefts, tables = [], []
        for inner in range(4):
            tile = group * 4 + inner
            index = index_ref[0, pl.ds(tile, 1), :]
            weighted = query_scratch[tile].astype(F32) * score_grad[pl.ds(tile, 1), :]
            which = index >> 8
            lefts.append(jnp.concatenate([jnp.where(which == part, weighted, 0.0).astype(BF16) for part in range(parts)], axis=0))
            tables.append(one_hot(index & 255, 256))
        left = jnp.concatenate(lefts, axis=1)
        table = jnp.concatenate(tables, axis=1)
        return grad + lax.dot_general(left, table, NT, preferred_element_type=F32)

    grad = lax.fori_loop(0, tiles // 4, one_group, jnp.zeros((parts * dim, 256), F32))
    grad = jnp.concatenate([grad[part * dim:(part + 1) * dim] for part in range(parts)], axis=1)
    direction = unit_backward(grad, page_raw_ref[0]).astype(BF16)
    accumulated[...] += jnp.dot(direction, hidden_ref[0], preferred_element_type=F32)

    @pl.when(page == pl.num_programs(0) - 1)
    def _():
        weight_ref[...] = accumulated[...].T.astype(BF16)


def whole(shape):
    return pl.BlockSpec(shape, lambda *i: (0,) * len(shape))


def shape(dims, kind):
    return jax.ShapeDtypeStruct(dims, kind)


def vmem(mib):
    return pltpu.CompilerParams(vmem_limit_bytes=mib * MIB)


def cost(flops, read):
    return pl.CostEstimate(flops=flops, bytes_accessed=read, transcendentals=0)


def swap_cores(value):
    return lax.ppermute(value, "core", [(0, 1), (1, 0)])


def per_device(query_hidden, document_states, projection, lengths, best_token):
    query_count, tokens, hidden_size = query_hidden.shape
    pages, slots, _ = document_states.shape
    dim = projection.shape[1]
    chips, cores = lax.axis_size("chip"), lax.axis_size("core")
    tiles = chips * cores
    rows = query_count * tokens
    multiplier = 1.0 / (tokens * TEMPERATURE)
    smem = pl.BlockSpec(memory_space=pltpu.SMEM)
    place = jnp.stack([lax.axis_index("core"), lax.axis_index("chip")]).astype(jnp.int32)
    query_rows = query_hidden.reshape(rows, hidden_size)

    query_raw, query_send = pl.pallas_call(
        query_kernel,
        out_shape=(shape((dim, rows), F32), shape((chips, dim, rows), BF16)),
        compiler_params=vmem(8),
        name="query_project",
    )(query_rows, projection)
    near = lax.all_to_all(query_send, "chip", 0, 0, tiled=True)

    index = jnp.transpose(best_token.reshape(chips, cores, query_count, tokens, pages), (4, 1, 0, 2, 3)).reshape(pages, tiles, rows)
    page_raw, page_unit, chosen = pl.pallas_call(
        page_kernel,
        grid=(pages,),
        in_specs=[
            smem,
            pl.BlockSpec((1, slots, hidden_size), lambda i: (i, 0, 0)),
            whole((hidden_size, dim)),
            pl.BlockSpec((1, tiles, rows), lambda i: (i, 0, 0)),
        ],
        out_specs=[
            pl.BlockSpec((1, dim, slots), lambda i: (i, 0, 0)),
            pl.BlockSpec((1, slots, dim), lambda i: (i, 0, 0)),
            pl.BlockSpec((1, tiles, dim, rows), lambda i: (i, 0, 0, 0)),
        ],
        out_shape=(shape((pages, dim, slots), F32), shape((pages, slots, dim), BF16), shape((pages, tiles, dim, rows), BF16)),
        compiler_params=vmem(24),
        cost_estimate=cost(2 * pages * slots * dim * (hidden_size + tiles * rows), 16 * MIB),
        name="page_project",
    )(lengths, document_states, projection, index)

    far = swap_cores(near)
    near_best = pl.pallas_call(
        near_kernel,
        out_shape=shape((pages, chips, rows), F32),
        compiler_params=vmem(16),
        cost_estimate=cost(pages * slots * dim * tiles * rows, 2 * MIB),
        name="near_scores",
    )(near, page_unit)
    expo, keep, total, pair, target = pl.pallas_call(
        lambda *refs: far_kernel(multiplier, *refs),
        in_specs=[smem] + [pl.BlockSpec(memory_space=pltpu.VMEM)] * 4,
        out_shape=(
            shape((pages, tiles, rows), F32),
            shape((chips, dim, rows), F32),
            shape((tiles, 128), F32),
            shape((chips, dim + 16, rows), BF16),
            shape((dim, rows), F32),
        ),
        scratch_shapes=[pltpu.VMEM((pages, tiles, rows), F32)],
        compiler_params=vmem(24),
        cost_estimate=cost(pages * slots * dim * tiles * rows, 8 * MIB),
        name="far_scores",
    )(place, far, page_unit, near_best, chosen)
    send, own = pl.pallas_call(
        add_kernel,
        in_specs=[smem] + [pl.BlockSpec(memory_space=pltpu.VMEM)] * 3,
        out_shape=(shape((chips, dim + 16, rows), BF16), shape((dim, rows), F32)),
        compiler_params=vmem(8),
        name="add_pair",
    )(place, keep, total, swap_cores(pair))
    received = lax.all_to_all(send, "chip", 0, 0, tiled=True)

    weight_part, query_grad = pl.pallas_call(
        lambda *refs: gradient_kernel(multiplier, *refs),
        grid=(pages,),
        in_specs=[
            smem,
            pl.BlockSpec((1, tiles, rows), lambda i: (i, 0, 0)),
            pl.BlockSpec((1, tiles, rows), lambda i: (i, 0, 0)),
            whole((chips, dim + 16, rows)),
            whole((dim, rows)),
            whole((dim, rows)),
            whole((chips, dim, rows)),
            whole((chips, dim, rows)),
            pl.BlockSpec((1, dim, slots), lambda i: (i, 0, 0)),
            pl.BlockSpec((1, slots, hidden_size), lambda i: (i, 0, 0)),
            whole((dim, rows)),
            whole((rows, hidden_size)),
        ],
        out_specs=[whole((hidden_size, dim)), whole((rows, dim))],
        out_shape=(shape((hidden_size, dim), BF16), shape((rows, dim), F32)),
        scratch_shapes=[
            pltpu.VMEM((tiles, rows), F32),
            pltpu.VMEM((tiles, rows), F32),
            pltpu.VMEM((tiles, dim, rows), BF16),
            pltpu.VMEM((dim, hidden_size), F32),
        ],
        compiler_params=vmem(32),
        cost_estimate=cost(2 * pages * slots * dim * (hidden_size + tiles * rows), 16 * MIB),
        name="gradients",
    )(place, index, expo, received, own, target, near, far, page_raw, document_states, query_raw, query_rows)

    everyone = ("dp", "chip", "core")
    devices = lax.axis_size(everyone)
    chunk = hidden_size // devices
    terms = lax.all_to_all(weight_part.reshape(devices, chunk, dim), everyone, 0, 0, tiled=True)
    mine = jnp.sum(terms.astype(F32), axis=0).astype(BF16)
    shared = lax.all_to_all(jnp.broadcast_to(mine[None], (devices, chunk, dim)), everyone, 0, 0, tiled=True)
    weight_grad = shared.reshape(hidden_size, dim).astype(F32)
    return (weight_grad, query_grad.reshape(query_count, tokens, dim))


def solution(mesh):
    groups, gallery = mesh.devices.shape
    levels = Mesh(mesh.devices.reshape(groups, gallery // 2, 2), ("dp", "chip", "core"))
    every = ("dp", "chip", "core")
    return jax.shard_map(
        per_device,
        mesh=levels,
        in_specs=(P(every, None, None), P(every, None, None), P(), P(every), P("dp", None, ("chip", "core"))),
        out_specs=(P(), P(every, None, None)),
        check_vma=False,
    )
```

time: 132 us -> 116 us (0.88)
  Pallas kernels: 53.7 us -> 33.5 us
  waiting for transfers between devices: 0.01 us -> 11 us
  blocking collectives: 62.4 us -> 53.2 us
  local copies, waits for them, and re-layouts: 6.74 us -> 9.7 us
    pallas_call x1, Pallas kernels: 20.9 us -> 10.6 us  [per_device(): pl.pallas_call(page_kernel, grid=(pages,), in_specs=[smem, pl.BlockSpec((...]
    all_to_all x3, blocking collectives: 62.4 us -> 53.2 us  [the longest x1 21.9 us: per_device(): lax.all_to_all(weight_part.reshape(devices, chunk, dim), everyone, 0, 0,...]
    all_to_all x1, waiting for transfers between devices: 0.01 us -> 8.99 us  [per_device(): near = lax.all_to_all(query_send, 'chip', 0, 0, tiled=True)]
    pallas_call x2 -> x4, Pallas kernels: 16.9 us -> 11.3 us  [the longest x1 5.48 us: per_device(): pl.pallas_call(lambda *refs: far_kernel(multiplier, *refs), in_specs=[sme...]
    pallas_call x1, Pallas kernels: 15.9 us -> 11.6 us  [per_device(): pl.pallas_call(lambda *refs: gradient_kernel(multiplier, *refs), grid=(pa...]
    unnamed x16 -> x19, local copies, waits for them, and re-layouts: 4.16 us -> 8.43 us
    ppermute x0 -> x2, waiting for transfers between devices: none -> 1.99 us  [swap_cores(): return lax.ppermute(value, 'core', [(0, 1), (1, 0)])]
  transfers between devices with their start and end apart: 1 -> 3, of which waited for: 0 -> 2; matrix products, arithmetic and copies ran while one was open for 0% -> 1% of each run, Pallas kernels for 16% -> 13%
where the time goes in v2:
time: 116 us
  blocking collectives  53.2 us (46%)
  Pallas kernels  33.5 us (29%)
  waiting for transfers between devices  11 us (9%)
  local copies, waits for them, and re-layouts  9.7 us (8%)
  starting transfers between devices  7.3 us (6%)
    all_to_all x1, blocking collectives, per_device(): lax.all_to_all(weight_part.reshape(devices, chunk, dim), everyone, 0, 0,...  21.9 us
    all_to_all x1, blocking collectives, per_device(): lax.all_to_all(jnp.broadcast_to(mine[None], (devices, chunk, dim)), every...  18.1 us
    all_to_all x1, blocking collectives, per_device(): received = lax.all_to_all(send, 'chip', 0, 0, tiled=True)  13.2 us
    pallas_call x1, Pallas kernels, per_device(): pl.pallas_call(lambda *refs: gradient_kernel(multiplier, *refs), grid=(pa...  11.6 us
    pallas_call x1, Pallas kernels, per_device(): pl.pallas_call(page_kernel, grid=(pages,), in_specs=[smem, pl.BlockSpec((...  10.6 us
    all_to_all x1, waiting for transfers between devices, per_device(): near = lax.all_to_all(query_send, 'chip', 0, 0, tiled=True)  8.99 us
    unnamed x19, local copies, waits for them, and re-layouts  8.43 us
    all_to_all x1, starting transfers between devices, per_device(): near = lax.all_to_all(query_send, 'chip', 0, 0, tiled=True)  6.37 us
  transfers between devices with their start and end apart: 3, of which 2 were waited for; matrix products, arithmetic and copies ran while one was open for 1% of the time, Pallas kernels for 13%

profile of v2, /device:TPU:1, one launch (start us, length us, event | category | flops | bytes accessed | tf_op | source)
XLA Modules:
  0.0 115.7 jit_solution(11791628027533626342)
XLA Ops:
  0.6 0.0 copy-start
  0.6 1.1 copy-done
  1.8 0.0 copy-start.2
  1.8 1.0 copy-done.2
  2.8 1.3 %query_project.1 = (f32[128,256]{1,0:T(8,128)S(1)}, bf16[8,128,256]{2,1,0:T(8,128)(2,1)}) custom-call(bf16[256,1536]{1,0:T(8,128)(2,1)S(1)} %bitcast.9, bf16[1536,128]{1,0:T(8,128)(2,1)S(1)} %copy-done.2), custom_call_target="tpu_custom_call" | custom-call | tf_op jit(solution)/shard_map/query_project/pallas_call | solution.py:236
  4.0 6.4 %all-to-all-start = ((bf16[8,128,256]{2,1,0:T(8,128)(2,1)}), bf16[8,128,256]{2,1,0:T(8,128)(2,1)S(1)}, u32[]{:S(2)}, u32[]{:S(2)}) async-start(bf16[8,128,256]{2,1,0:T(8,128)(2,1)} %get-tuple-element.16), calls=%async_computation | async-start | bytes 1048576 | tf_op jit(solution)/shard_map/all_to_all | solution.py:242
  10.4 1.0 copy.8
  11.4 0.1 reshape.24.index_ref.refs_1_
  11.5 0.1 pad_add_fusion.refs_0_.place_ref
  11.6 9.0 %all-to-all-done.query_ref.refs_6_ = bf16[8,128,256]{2,1,0:T(8,128)(2,1)S(1)} async-done(((bf16[8,128,256]{2,1,0:T(8,128)(2,1)}), bf16[8,128,256]{2,1,0:T(8,128)(2,1)S(1)}, u32[]{:S(2)}, u32[]{:S(2)}) %all-to-all-start) | async-done | bytes 524320 | tf_op jit(solution)/shard_map/all_to_all | solution.py:242
  20.6 0.8 collective-permute-start
  21.4 0.0 copy-start.3
  21.4 1.0 copy-done.3
  22.4 0.0 copy-start.4
  22.4 3.7 %copy-done.4 = bf16[4,768,1536]{2,1,0:T(8,128)(2,1)S(1)} copy-done((bf16[4,768,1536]{2,1,0:T(8,128)(2,1)S(1)}, bf16[4,768,1536]{2,1,0:T(8,128)(2,1)}, u32[]{:S(2)}) %copy-start.4) | copy-done | bytes 9437208
  26.1 0.0 copy-start.5
  26.1 0.7 copy-done.5
  26.8 0.0 slice-start
  26.8 0.0 slice-start.1
  26.8 10.6 %page_project.1 = (f32[4,128,768]{2,1,0:T(8,128)S(1)}, bf16[4,768,128]{2,1,0:T(8,128)(2,1)S(1)}, bf16[4,16,128,256]{3,2,1,0:T(8,128)(2,1)S(1)}) custom-call(s32[4]{0:T(128)S(1)} %copy-done.5, bf16[4,768,1536]{2,1,0:T(8,128)(2,1)S(1)} %copy-done.4, bf16[1536,128]{1,0:T(8,128)(2,1)S(1)} %copy-done.3, s32[4,16,256]{2,1,0:T(8,128)S(1)} %reshape.24.index_ref.refs_1_), custom_call_target="tpu_custom_call" | custom-call | flops 4429185024 | bytes 16777216 | tf_op jit(solution)/shard_map/page_project/pallas_call | solution.py:245
  37.4 0.0 slice-start.2
  37.4 3.9 %near_scores.1.refs_3_ = f32[4,8,256]{2,1,0:T(8,128)S(1)} custom-call(bf16[8,128,256]{2,1,0:T(8,128)(2,1)S(1)} %all-to-all-done.query_ref.refs_6_, bf16[4,768,128]{2,1,0:T(8,128)(2,1)S(1)} %get-tuple-element.17.unit_ref.refs_2_), custom_call_target="tpu_custom_call" | custom-call | flops 1610612736 | bytes 2097152 | tf_op jit(solution)/shard_map/near_scores/pallas_call | solution.py:266
  41.4 0.0 collective-permute-done.refs_1_.refs_7_
  41.4 0.0 copy-start.1
  41.4 5.5 %far_scores.1 = (f32[4,16,256]{2,1,0:T(8,128)S(1)}, f32[8,128,256]{2,1,0:T(8,128)S(1)}, f32[16,128]{1,0:T(8,128)S(1)}, bf16[8,144,256]{2,1,0:T(8,128)(2,1)S(1)}, f32[128,256]{1,0:T(8,128)S(1)}) custom-call(s32[2]{0:T(128)S(1)} %pad_add_fusion.refs_0_.place_ref, bf16[8,128,256]{2,1,0:T(8,128)(2,1)S(1)} %collective-permute-done.refs_1_.refs_7_, ...), custom_call_target="tpu_custom_call" | custom-call | flops 1610612736 | bytes 8388608 | tf_op jit(solution)/shard_map/far_scores/pallas_call | solution.py:273
  46.9 0.1 collective-permute-start.1
  47.0 2.0 %collective-permute-done.1.pair_ref = bf16[8,144,256]{2,1,0:T(8,128)(2,1)S(1)} collective-permute-done((bf16[8,144,256]{2,1,0:T(8,128)(2,1)S(1)}, bf16[8,144,256]{2,1,0:T(8,128)(2,1)S(1)}, u32[]{:S(2)}, u32[]{:S(2)}) %collective-permute-start.1) | collective-permute-done | bytes 589856 | tf_op jit(solution)/shard_map/ppermute | solution.py:221
  48.9 0.6 add_pair.1
  49.6 13.2 %all_to_all.20.refs_3_ = bf16[8,144,256]{2,1,0:T(8,128)(2,1)S(1)} all-to-all(bf16[8,144,256]{2,1,0:T(8,128)(2,1)S(1)} %get-tuple-element.23), channel_id=1, replica_groups=mesh['dp'=8,'chip'=8,'core'=2] {'chip'}, dimensions={0} | all-to-all | bytes 1179648 | tf_op jit(solution)/shard_map/all_to_all | solution.py:295
  62.8 0.0 slice-done
  62.8 0.0 slice-done.1
  62.8 0.0 slice-done.2
  62.8 0.0 copy-done.1
  62.8 11.6 %gradients.1 = (bf16[1536,128]{1,0:T(8,128)(2,1)S(1)}, f32[256,128]{1,0:T(8,128)}) custom-call(s32[2]{0:T(128)S(1)} %pad_add_fusion.refs_0_.place_ref, s32[4,16,256]{2,1,0:T(8,128)S(1)} %reshape.24.index_ref.refs_1_, f32[4,16,256]{2,1,0:T(8,128)S(1)} %get-tuple-element.19.refs_2_, bf16[8,144,256]{2,1,0:T(8,128)(2,1)S(1)} %all_to_all.20.refs_3_, ...), custom_call_target="tpu_custom_call" | custom-call | flops 4429185024 | bytes 16777216 | tf_op jit(solution)/shard_map/gradients/pallas_call | solution.py:297
  74.4 0.1 reshape.26
  74.5 21.9 %all_to_all.21 = bf16[128,12,128]{2,1,0:T(8,128)(2,1)S(1)} all-to-all(bf16[128,12,128]{2,1,0:T(8,128)(2,1)S(1)} %reshape.26), channel_id=1, replica_groups=mesh['dp'=8,'chip'=8,'core'=2] {'dp','chip','core'}, dimensions={0} | all-to-all | bytes 786432 | tf_op jit(solution)/shard_map/all_to_all | solution.py:330
  96.5 0.1 reduce_sum.12
  96.6 0.1 broadcast_in_dim.2
  96.7 18.1 %all_to_all.22 = bf16[128,12,128]{2,1,0:T(8,128)(2,1)S(1)} all-to-all(bf16[128,12,128]{2,1,0:T(8,128)(2,1)S(1)} %broadcast_in_dim.2), channel_id=1, replica_groups=mesh['dp'=8,'chip'=8,'core'=2] {'dp','chip','core'}, dimensions={0} | all-to-all | bytes 786432 | tf_op jit(solution)/shard_map/all_to_all | solution.py:332
  114.8 1.0 reshape.28
  (2 shorter events, 0.0 us)
Async XLA Ops:
  0.6 1.1 copy-start
  1.8 1.0 copy-start.2
  4.0 16.6 %all-to-all-start = ((bf16[8,128,256]{2,1,0:T(8,128)(2,1)}), bf16[8,128,256]{2,1,0:T(8,128)(2,1)S(1)}, u32[]{:S(2)}, u32[]{:S(2)}) async-start(bf16[8,128,256]{2,1,0:T(8,128)(2,1)} %get-tuple-element.16), calls=%async_computation | async-start | bytes 1048576 | tf_op jit(solution)/shard_map/all_to_all | solution.py:242
  20.6 20.8 %collective-permute-start = (bf16[8,128,256]{2,1,0:T(8,128)(2,1)S(1)}, bf16[8,128,256]{2,1,0:T(8,128)(2,1)S(1)}, u32[]{:S(2)}, u32[]{:S(2)}) collective-permute-start(bf16[8,128,256]{2,1,0:T(8,128)(2,1)S(1)} %all-to-all-done.query_ref.refs_6_), channel_id=1, source_target_pairs={{0,1},{1,0},{2,3},{3,2},{4,5},{5,4},{6,7},{7,6},{8,9},{9,8},{10,11... | collective-permute-start | bytes 1572872 | tf_op jit(solution)/shard_map/ppermute | solution.py:221
  21.4 1.0 copy-start.3
  22.4 3.7 %copy-start.4 = (bf16[4,768,1536]{2,1,0:T(8,128)(2,1)S(1)}, bf16[4,768,1536]{2,1,0:T(8,128)(2,1)}, u32[]{:S(2)}) copy-start(bf16[4,768,1536]{2,1,0:T(8,128)(2,1)} %refs_9_.1) | copy-start | bytes 28311556
  26.1 0.7 copy-start.5
  26.8 36.0 %slice-start = ((s8[9437184]{0:T(1024)(128)(4,1)}), s8[4194304]{0:T(1024)(128)(4,1)S(1)}, s32[]{:S(2)}) async-start(s8[9437184]{0:T(1024)(128)(4,1)} %bitcast.11), calls=%async_computation.4 | async-start | bytes 8388608
  26.8 36.0 %slice-start.1 = ((s8[9437184]{0:T(1024)(128)(4,1)}), s8[4194304]{0:T(1024)(128)(4,1)S(1)}, s32[]{:S(2)}) async-start(s8[9437184]{0:T(1024)(128)(4,1)} %bitcast.11), calls=%async_computation.5 | async-start | bytes 8388608
  37.4 25.4 %slice-start.2 = ((s8[9437184]{0:T(1024)(128)(4,1)}), s8[1048576]{0:T(1024)(128)(4,1)S(1)}, s32[]{:S(2)}) async-start(s8[9437184]{0:T(1024)(128)(4,1)} %bitcast.11), calls=%async_computation.6 | async-start | bytes 2097152
  41.4 21.4 %copy-start.1 = (bf16[8,32,1536]{2,1,0:T(8,128)(2,1)S(1)}, bf16[8,32,1536]{2,1,0:T(8,128)(2,1)}, u32[]{:S(2)}) copy-start(bf16[8,32,1536]{2,1,0:T(8,128)(2,1)} %param.5) | copy-start | bytes 2359300
  46.9 2.1 %collective-permute-start.1 = (bf16[8,144,256]{2,1,0:T(8,128)(2,1)S(1)}, bf16[8,144,256]{2,1,0:T(8,128)(2,1)S(1)}, u32[]{:S(2)}, u32[]{:S(2)}) collective-permute-start(bf16[8,144,256]{2,1,0:T(8,128)(2,1)S(1)} %get-tuple-element.22), channel_id=1, source_target_pairs={{0,1},{1,0},{2,3},{3,2},{4,5},{5,4},{6,7},{7,6},{8,9},{9,8},{10,11... | collective-permute-start | bytes 1769480 | tf_op jit(solution)/shard_map/ppermute | solution.py:221

commit v3 on v2

--- a/solution.py
+++ b/solution.py
@@ -10,6 +10,7 @@
 EPSILON = 1e-06
 TEMPERATURE = 0.02
 MIB = 1024 * 1024
+QUERY_MIB, PAGE_MIB, GRADIENT_MIB = 60, 50, 50
 
 NT = (((1,), (1,)), ((), ()))
 TN = (((0,), (0,)), ((), ()))
@@ -31,12 +32,22 @@
     return lax.broadcasted_iota(jnp.int32, shape, axis)
 
 
-def one_hot(index, rows):
-    return jnp.where(iota((rows, index.shape[1]), 0) == index, 1.0, 0.0).astype(BF16)
-
-
-def query_kernel(hidden_ref, weight_ref, raw_ref, send_ref):
-    raw = jnp.dot(hidden_ref[...], weight_ref[...], preferred_element_type=F32).T
+def one_hot(low):
+    index = low.astype(F32).astype(BF16)
+    positions = iota((256, low.shape[1]), 0).astype(F32).astype(BF16)
+    return jnp.where(positions == index, jnp.ones((), BF16), jnp.zeros((), BF16))
+
+
+def query_kernel(hidden_any, weight_any, raw_ref, send_ref, hidden, weight, arrived):
+    copies = [
+        pltpu.make_async_copy(weight_any, weight, arrived.at[0]),
+        pltpu.make_async_copy(hidden_any, hidden, arrived.at[1]),
+    ]
+    for copy in copies:
+        copy.start()
+    for copy in copies:
+        copy.wait()
+    raw = jnp.dot(hidden[...], weight[...], preferred_element_type=F32).T
     raw_ref[...] = raw
     unit = (raw * inverse_norm(raw, 0)).astype(BF16)
     for block in range(send_ref.shape[0]):
@@ -57,7 +68,7 @@
 
     def one_tile(tile, carry):
         index = index_ref[0, pl.ds(tile, 1), :]
-        found = jnp.dot(table, one_hot(index & 255, 256), preferred_element_type=F32)
+        found = jnp.dot(table, one_hot(index & 255), preferred_element_type=F32)
         which = index >> 8
         chosen = found[0:128]
         for part in range(1, parts):
@@ -65,7 +76,7 @@
         chosen_ref[0, tile] = chosen.astype(BF16)
         return carry
 
-    lax.fori_loop(0, index_ref.shape[1], one_tile, 0, unroll=4)
+    lax.fori_loop(0, index_ref.shape[1], one_tile, 0, unroll=8)
 
 
 def best_scores(queries, unit_ref, out, row):
@@ -147,17 +158,25 @@
 
 
 def gradient_kernel(multiplier, place_ref, index_ref, expo_ref, received_ref, own_ref, target_ref, near_ref, far_ref, page_raw_ref,
-                    hidden_ref, query_raw_ref, query_hidden_ref, weight_ref, query_grad_ref, inverse_total, score_grad, query_scratch, accumulated):
+                    hidden_any, query_raw_ref, query_hidden_any, weight_ref, query_grad_ref, inverse_total, score_grad, summed_grad,
+                    accumulated, hidden, query_hidden, arrived):
     page = pl.program_id(0)
     core, chip = place_ref[0], place_ref[1]
     chips, dim, lanes = near_ref.shape
     tiles = 2 * chips
     mine = core * chips + chip
-    slots = hidden_ref.shape[1]
+    pages, slots, _ = hidden.shape
     parts = slots // 256
+    query_copy = pltpu.make_async_copy(query_hidden_any, query_hidden, arrived.at[pages])
+
+    def page_copy(which):
+        return pltpu.make_async_copy(hidden_any.at[which], hidden.at[which], arrived.at[which])
 
     @pl.when(page == 0)
     def _():
+        query_copy.start()
+        for which in range(pages):
+            page_copy(which).start()
         total = jnp.zeros((tiles, 128), F32)
         for source in range(chips):
             total = total + received_ref[source, dim:dim + 16, 0:128].astype(F32) + received_ref[source, dim:dim + 16, 128:256].astype(F32)
@@ -171,30 +190,28 @@
         query_grad = (summed * inverse_total[pl.ds(mine, 1), :] - target_ref[...]) * multiplier
         query_grad_ref[...] = query_grad.T
         direction = unit_backward(query_grad, query_raw_ref[...]).astype(BF16)
-        accumulated[...] = jnp.dot(direction, query_hidden_ref[...], preferred_element_type=F32)
-        query_scratch[pl.ds(core * chips, chips)] = near_ref[...]
-        query_scratch[pl.ds((1 - core) * chips, chips)] = far_ref[...]
+        query_copy.wait()
+        accumulated[...] = jnp.dot(direction, query_hidden[...], preferred_element_type=F32)
 
     is_target = (iota((tiles, lanes), 0) == mine) & (iota((tiles, lanes), 1) // 64 == page)
     score_grad[...] = (expo_ref[0] * inverse_total[...] - jnp.where(is_target, 1.0, 0.0)) * multiplier
 
-    def one_group(group, grad):
-        lefts, tables = [], []
-        for inner in range(4):
-            tile = group * 4 + inner
+    for side, queries_ref in ((core, near_ref), (1 - core, far_ref)):
+        for chip_of in range(chips):
+            tile = side * chips + chip_of
             index = index_ref[0, pl.ds(tile, 1), :]
-            weighted = query_scratch[tile].astype(F32) * score_grad[pl.ds(tile, 1), :]
+            weighted = queries_ref[chip_of].astype(F32) * score_grad[pl.ds(tile, 1), :]
             which = index >> 8
-            lefts.append(jnp.concatenate([jnp.where(which == part, weighted, 0.0).astype(BF16) for part in range(parts)], axis=0))
-            tables.append(one_hot(index & 255, 256))
-        left = jnp.concatenate(lefts, axis=1)
-        table = jnp.concatenate(tables, axis=1)
-        return grad + lax.dot_general(left, table, NT, preferred_element_type=F32)
-
-    grad = lax.fori_loop(0, tiles // 4, one_group, jnp.zeros((parts * dim, 256), F32))
-    grad = jnp.concatenate([grad[part * dim:(part + 1) * dim] for part in range(parts)], axis=1)
+            left = jnp.concatenate([jnp.where(which == part, weighted, 0.0).astype(BF16) for part in range(parts)], axis=0)
+            term = lax.dot_general(left, one_hot(index & 255), NT, preferred_element_type=F32)
+            if queries_ref is near_ref and chip_of == 0:
+                summed_grad[...] = term
+            else:
+                summed_grad[...] += term
+    grad = jnp.concatenate([summed_grad[part * dim:(part + 1) * dim] for part in range(parts)], axis=1)
     direction = unit_backward(grad, page_raw_ref[0]).astype(BF16)
-    accumulated[...] += jnp.dot(direction, hidden_ref[0], preferred_element_type=F32)
+    page_copy(page).wait()
+    accumulated[...] += jnp.dot(direction, hidden[page], preferred_element_type=F32)
 
     @pl.when(page == pl.num_programs(0) - 1)
     def _():
@@ -235,8 +252,10 @@
 
     query_raw, query_send = pl.pallas_call(
         query_kernel,
+        in_specs=[pl.BlockSpec(memory_space=pl.ANY)] * 2,
         out_shape=(shape((dim, rows), F32), shape((chips, dim, rows), BF16)),
-        compiler_params=vmem(8),
+        scratch_shapes=[pltpu.VMEM((rows, hidden_size), BF16), pltpu.VMEM((hidden_size, dim), BF16), pltpu.SemaphoreType.DMA((2,))],
+        compiler_params=vmem(QUERY_MIB),
         name="query_project",
     )(query_rows, projection)
     near = lax.all_to_all(query_send, "chip", 0, 0, tiled=True)
@@ -257,11 +276,12 @@
             pl.BlockSpec((1, tiles, dim, rows), lambda i: (i, 0, 0, 0)),
         ],
         out_shape=(shape((pages, dim, slots), F32), shape((pages, slots, dim), BF16), shape((pages, tiles, dim, rows), BF16)),
-        compiler_params=vmem(24),
+        compiler_params=vmem(PAGE_MIB),
         cost_estimate=cost(2 * pages * slots * dim * (hidden_size + tiles * rows), 16 * MIB),
         name="page_project",
     )(lengths, document_states, projection, index)
 
+    near, page_unit = lax.optimization_barrier((near, page_unit))
     far = swap_cores(near)
     near_best = pl.pallas_call(
         near_kernel,
@@ -307,19 +327,22 @@
             whole((chips, dim, rows)),
             whole((chips, dim, rows)),
             pl.BlockSpec((1, dim, slots), lambda i: (i, 0, 0)),
-            pl.BlockSpec((1, slots, hidden_size), lambda i: (i, 0, 0)),
+            pl.BlockSpec(memory_space=pl.ANY),
             whole((dim, rows)),
-            whole((rows, hidden_size)),
+            pl.BlockSpec(memory_space=pl.ANY),
         ],
         out_specs=[whole((hidden_size, dim)), whole((rows, dim))],
         out_shape=(shape((hidden_size, dim), BF16), shape((rows, dim), F32)),
         scratch_shapes=[
             pltpu.VMEM((tiles, rows), F32),
             pltpu.VMEM((tiles, rows), F32),
-            pltpu.VMEM((tiles, dim, rows), BF16),
+            pltpu.VMEM((slots // 256 * dim, 256), F32),
             pltpu.VMEM((dim, hidden_size), F32),
+            pltpu.VMEM((pages, slots, hidden_size), BF16),
+            pltpu.VMEM((rows, hidden_size), BF16),
+            pltpu.SemaphoreType.DMA((pages + 1,)),
         ],
-        compiler_params=vmem(32),
+        compiler_params=vmem(GRADIENT_MIB),
         cost_estimate=cost(2 * pages * slots * dim * (hidden_size + tiles * rows), 16 * MIB),
         name="gradients",
     )(place, index, expo, received, own, target, near, far, page_raw, document_states, query_raw, query_rows)

time: 116 us -> 107 us (0.922)
  waiting for transfers between devices: 11 us -> 2 us
  local copies, waits for them, and re-layouts: 9.7 us -> 5.05 us
  blocking collectives: 53.2 us -> 56.1 us
  Pallas kernels: 33.5 us -> 35 us
    all_to_all x1, waiting for transfers between devices: 8.99 us -> 0.01 us  [per_device(): near = lax.all_to_all(query_send, 'chip', 0, 0, tiled=True)]
    unnamed x19 -> x13, local copies, waits for them, and re-layouts: 8.43 us -> 3.79 us
    all_to_all x1, blocking collectives: 13.2 us -> 16 us  [per_device(): received = lax.all_to_all(send, 'chip', 0, 0, tiled=True)]
    pallas_call x1, Pallas kernels: 1.27 us -> 2.55 us  [per_device(): pl.pallas_call(query_kernel, in_specs=[pl.BlockSpec(memory_space=pl.ANY)]...]
  transfers between devices with their start and end apart: 3 -> 3, of which waited for: 2 -> 1; matrix products, arithmetic and copies ran while one was open for 1% -> 1% of each run, Pallas kernels for 13% -> 14%
where the time goes in v3:
time: 107 us
  blocking collectives  56.1 us (52%)
  Pallas kernels  35 us (33%)
  starting transfers between devices  7.43 us (7%)
  local copies, waits for them, and re-layouts  5.05 us (5%)
  waiting for transfers between devices  2 us (2%)
    all_to_all x1, blocking collectives, per_device(): lax.all_to_all(weight_part.reshape(devices, chunk, dim), everyone, 0, 0,...  22 us
    all_to_all x1, blocking collectives, per_device(): lax.all_to_all(jnp.broadcast_to(mine[None], (devices, chunk, dim)), every...  18.1 us
    all_to_all x1, blocking collectives, per_device(): received = lax.all_to_all(send, 'chip', 0, 0, tiled=True)  16 us
    pallas_call x1, Pallas kernels, per_device(): pl.pallas_call(page_kernel, grid=(pages,), in_specs=[smem, pl.BlockSpec((...  11.5 us
    pallas_call x1, Pallas kernels, per_device(): pl.pallas_call(lambda *refs: gradient_kernel(multiplier, *refs), grid=(pa...  10.9 us
    all_to_all x1, starting transfers between devices, per_device(): near = lax.all_to_all(query_send, 'chip', 0, 0, tiled=True)  6.38 us
    pallas_call x1, Pallas kernels, per_device(): pl.pallas_call(lambda *refs: far_kernel(multiplier, *refs), in_specs=[sme...  5.48 us
    pallas_call x1, Pallas kernels, per_device(): pl.pallas_call(near_kernel, out_shape=shape((pages, chips, rows), F32), c...  3.9 us
  transfers between devices with their start and end apart: 3, of which 1 were waited for; matrix products, arithmetic and copies ran while one was open for 1% of the time, Pallas kernels for 14%

profile of v3, /device:TPU:1, one launch (start us, length us, event | category | flops | bytes accessed | tf_op | source)
XLA Modules:
  0.0 106.6 jit_solution(8758974121152484422)
XLA Ops:
  0.6 2.5 %query_project.1 = (f32[128,256]{1,0:T(8,128)}, bf16[8,128,256]{2,1,0:T(8,128)(2,1)}) custom-call(bf16[256,1536]{1,0:T(8,128)(2,1)} %bitcast.9, bf16[1536,128]{1,0:T(8,128)(2,1)} %weight_ref.1), custom_call_target="tpu_custom_call" | custom-call | tf_op jit(solution)/shard_map/query_project/pallas_call | solution.py:253
  3.2 6.4 %all-to-all-start = ((bf16[8,128,256]{2,1,0:T(8,128)(2,1)}), bf16[8,128,256]{2,1,0:T(8,128)(2,1)S(1)}, u32[]{:S(2)}, u32[]{:S(2)}) async-start(bf16[8,128,256]{2,1,0:T(8,128)(2,1)} %get-tuple-element.18), calls=%async_computation | async-start | bytes 1048576 | tf_op jit(solution)/shard_map/all_to_all | solution.py:261
  9.6 1.0 copy.8
  10.6 0.1 reshape.24.index_ref.refs_1_
  10.7 0.0 copy-start.1
  10.7 1.0 copy-done.1
  11.7 0.0 copy-start.3
  11.7 0.7 copy-done.3
  12.4 11.5 %page_project.1 = (f32[4,128,768]{2,1,0:T(8,128)S(1)}, bf16[4,768,128]{2,1,0:T(8,128)(2,1)S(1)}, bf16[4,16,128,256]{3,2,1,0:T(8,128)(2,1)}) custom-call(s32[4]{0:T(128)S(1)} %copy-done.3, bf16[4,768,1536]{2,1,0:T(8,128)(2,1)} %refs_9_.1, bf16[1536,128]{1,0:T(8,128)(2,1)S(1)} %copy-done.1, s32[4,16,256]{2,1,0:T(8,128)S(1)} %reshape.24.index_ref.refs_1_), custom_call_target="tpu_custom_call" | custom-call | flops 4429185024 | bytes 16777216 | tf_op jit(solution)/shard_map/page_project/pallas_call | solution.py:264
  23.9 0.0 copy-start.5
  23.9 1.2 %copy-done.5 = f32[4,128,768]{2,1,0:T(8,128)} copy-done((f32[4,128,768]{2,1,0:T(8,128)}, f32[4,128,768]{2,1,0:T(8,128)S(1)}, u32[]{:S(2)}) %copy-start.5) | copy-done | bytes 1572888
  25.0 0.0 all-to-all-done.query_ref.refs_6_
  25.0 1.0 collective-permute-start
  26.0 0.0 copy-start.4
  26.0 0.1 pad_add_fusion.refs_0_.place_ref
  26.1 3.9 %near_scores.1.refs_3_ = f32[4,8,256]{2,1,0:T(8,128)S(1)} custom-call(bf16[8,128,256]{2,1,0:T(8,128)(2,1)S(1)} %all-to-all-done.query_ref.refs_6_, bf16[4,768,128]{2,1,0:T(8,128)(2,1)S(1)} %get-tuple-element.21.unit_ref.refs_2_), custom_call_target="tpu_custom_call" | custom-call | flops 1610612736 | bytes 2097152 | tf_op jit(solution)/shard_map/near_scores/pallas_call | solution.py:286
  30.0 0.0 collective-permute-done.refs_1_.refs_7_
  30.0 0.0 copy-done.4
  30.0 0.0 copy-start
  30.0 0.0 copy-start.2
  30.0 5.5 %far_scores.1 = (f32[4,16,256]{2,1,0:T(8,128)S(1)}, f32[8,128,256]{2,1,0:T(8,128)S(1)}, f32[16,128]{1,0:T(8,128)S(1)}, bf16[8,144,256]{2,1,0:T(8,128)(2,1)S(1)}, f32[128,256]{1,0:T(8,128)S(1)}) custom-call(s32[2]{0:T(128)S(1)} %pad_add_fusion.refs_0_.place_ref, bf16[8,128,256]{2,1,0:T(8,128)(2,1)S(1)} %collective-permute-done.refs_1_.refs_7_, ...), custom_call_target="tpu_custom_call" | custom-call | flops 1610612736 | bytes 8388608 | tf_op jit(solution)/shard_map/far_scores/pallas_call | solution.py:293
  35.5 0.1 collective-permute-start.1
  35.6 2.0 %collective-permute-done.1.pair_ref = bf16[8,144,256]{2,1,0:T(8,128)(2,1)S(1)} collective-permute-done((bf16[8,144,256]{2,1,0:T(8,128)(2,1)S(1)}, bf16[8,144,256]{2,1,0:T(8,128)(2,1)S(1)}, u32[]{:S(2)}, u32[]{:S(2)}) %collective-permute-start.1) | collective-permute-done | bytes 589856 | tf_op jit(solution)/shard_map/ppermute | solution.py:238
  37.6 0.6 add_pair.1
  38.2 16.0 %all_to_all.20.refs_3_ = bf16[8,144,256]{2,1,0:T(8,128)(2,1)S(1)} all-to-all(bf16[8,144,256]{2,1,0:T(8,128)(2,1)S(1)} %get-tuple-element.27), channel_id=1, replica_groups=mesh['dp'=8,'chip'=8,'core'=2] {'chip'}, dimensions={0} | all-to-all | bytes 1179648 | tf_op jit(solution)/shard_map/all_to_all | solution.py:315
  54.2 0.0 copy-done
  54.2 0.0 copy-done.2
  54.2 10.9 %gradients.1 = (bf16[1536,128]{1,0:T(8,128)(2,1)S(1)}, f32[256,128]{1,0:T(8,128)}) custom-call(s32[2]{0:T(128)S(1)} %pad_add_fusion.refs_0_.place_ref, s32[4,16,256]{2,1,0:T(8,128)S(1)} %reshape.24.index_ref.refs_1_, f32[4,16,256]{2,1,0:T(8,128)S(1)} %get-tuple-element.23.refs_2_, bf16[8,144,256]{2,1,0:T(8,128)(2,1)S(1)} %all_to_all.20.refs_3_, ...), custom_call_target="tpu_custom_call" | custom-call | flops 4429185024 | bytes 16777216 | tf_op jit(solution)/shard_map/gradients/pallas_call | solution.py:317
  65.2 0.1 reshape.26
  65.3 22.0 %all_to_all.21 = bf16[128,12,128]{2,1,0:T(8,128)(2,1)S(1)} all-to-all(bf16[128,12,128]{2,1,0:T(8,128)(2,1)S(1)} %reshape.26), channel_id=1, replica_groups=mesh['dp'=8,'chip'=8,'core'=2] {'dp','chip','core'}, dimensions={0} | all-to-all | bytes 786432 | tf_op jit(solution)/shard_map/all_to_all | solution.py:353
  87.3 0.1 reduce_sum.12
  87.4 0.1 broadcast_in_dim.2
  87.5 18.1 %all_to_all.22 = bf16[128,12,128]{2,1,0:T(8,128)(2,1)S(1)} all-to-all(bf16[128,12,128]{2,1,0:T(8,128)(2,1)S(1)} %broadcast_in_dim.2), channel_id=1, replica_groups=mesh['dp'=8,'chip'=8,'core'=2] {'dp','chip','core'}, dimensions={0} | all-to-all | bytes 786432 | tf_op jit(solution)/shard_map/all_to_all | solution.py:355
  105.6 1.0 reshape.28
  (1 shorter events, 0.0 us)
Async XLA Ops:
  3.2 21.8 %all-to-all-start = ((bf16[8,128,256]{2,1,0:T(8,128)(2,1)}), bf16[8,128,256]{2,1,0:T(8,128)(2,1)S(1)}, u32[]{:S(2)}, u32[]{:S(2)}) async-start(bf16[8,128,256]{2,1,0:T(8,128)(2,1)} %get-tuple-element.18), calls=%async_computation | async-start | bytes 1048576 | tf_op jit(solution)/shard_map/all_to_all | solution.py:261
  10.7 1.0 copy-start.1
  11.7 0.7 copy-start.3
  23.9 1.2 %copy-start.5 = (f32[4,128,768]{2,1,0:T(8,128)}, f32[4,128,768]{2,1,0:T(8,128)S(1)}, u32[]{:S(2)}) copy-start(f32[4,128,768]{2,1,0:T(8,128)S(1)} %get-tuple-element.30.refs_8_) | copy-start | bytes 4718596
  25.0 5.0 %collective-permute-start = (bf16[8,128,256]{2,1,0:T(8,128)(2,1)S(1)}, bf16[8,128,256]{2,1,0:T(8,128)(2,1)S(1)}, u32[]{:S(2)}, u32[]{:S(2)}) collective-permute-start(bf16[8,128,256]{2,1,0:T(8,128)(2,1)S(1)} %all-to-all-done.query_ref.refs_6_), channel_id=1, source_target_pairs={{0,1},{1,0},{2,3},{3,2},{4,5},{5,4},{6,7},{7,6},{8,9},{9,8},{10,11... | collective-permute-start | bytes 1572872 | tf_op jit(solution)/shard_map/ppermute | solution.py:238
  26.0 4.0 %copy-start.4 = (bf16[4,16,128,256]{3,2,1,0:T(8,128)(2,1)S(1)}, bf16[4,16,128,256]{3,2,1,0:T(8,128)(2,1)}, u32[]{:S(2)}) copy-start(bf16[4,16,128,256]{3,2,1,0:T(8,128)(2,1)} %get-tuple-element.22.refs_4_) | copy-start | bytes 12582916
  30.0 24.3 %copy-start = (bf16[8,32,1536]{2,1,0:T(8,128)(2,1)S(1)}, bf16[8,32,1536]{2,1,0:T(8,128)(2,1)}, u32[]{:S(2)}) copy-start(bf16[8,32,1536]{2,1,0:T(8,128)(2,1)} %param.5) | copy-start | bytes 2359300
  30.0 24.2 %copy-start.2 = (f32[128,256]{1,0:T(8,128)S(1)}, f32[128,256]{1,0:T(8,128)}, u32[]{:S(2)}) copy-start(f32[128,256]{1,0:T(8,128)} %get-tuple-element.31.refs_10_) | copy-start | bytes 393220
  35.5 2.1 %collective-permute-start.1 = (bf16[8,144,256]{2,1,0:T(8,128)(2,1)S(1)}, bf16[8,144,256]{2,1,0:T(8,128)(2,1)S(1)}, u32[]{:S(2)}, u32[]{:S(2)}) collective-permute-start(bf16[8,144,256]{2,1,0:T(8,128)(2,1)S(1)} %get-tuple-element.26), channel_id=1, source_target_pairs={{0,1},{1,0},{2,3},{3,2},{4,5},{5,4},{6,7},{7,6},{8,9},{9,8},{10,11... | collective-permute-start | bytes 1769480 | tf_op jit(solution)/shard_map/ppermute | solution.py:238

commit v4 on v3

v4 whole, which is shorter than its diff:
```python
import jax
import jax.numpy as jnp
from jax import lax
from jax.experimental import pallas as pl
from jax.experimental.pallas import tpu as pltpu
from jax.sharding import Mesh, PartitionSpec as P

F32 = jnp.float32
BF16 = jnp.bfloat16
EPSILON = 1e-06
TEMPERATURE = 0.02
MIB = 1024 * 1024
QUERY_MIB, PAGE_MIB, NEAR_MIB, FAR_MIB, GRADIENT_MIB = 60, 56, 40, 24, 14

NT = (((1,), (1,)), ((), ()))


def inverse_norm(raw):
    value = jnp.sum(raw * raw, axis=0, keepdims=True) + EPSILON
    guess = lax.rsqrt(value)
    return guess * (1.5 - 0.5 * value * guess * guess)


def unit_backward(grad_unit, raw):
    inverse = inverse_norm(raw)
    unit = raw * inverse
    return (grad_unit - unit * jnp.sum(unit * grad_unit, axis=0, keepdims=True)) * inverse


def iota(shape, axis):
    return lax.broadcasted_iota(jnp.int32, shape, axis)


def one_hot(low):
    index = low.astype(F32).astype(BF16)
    positions = iota((256, low.shape[1]), 0).astype(F32).astype(BF16)
    return jnp.where(positions == index, jnp.ones((), BF16), jnp.zeros((), BF16))


def query_kernel(hidden_any, weight_any, raw_ref, send_ref, hidden, weight, arrived):
    copies = [
        pltpu.make_async_copy(weight_any, weight, arrived.at[0]),
        pltpu.make_async_copy(hidden_any, hidden, arrived.at[1]),
    ]
    for copy in copies:
        copy.start()
    for copy in copies:
        copy.wait()
    raw = jnp.dot(hidden[...], weight[...], preferred_element_type=F32).T
    raw_ref[...] = raw
    unit = (raw * inverse_norm(raw)).astype(BF16)
    for block in range(send_ref.shape[0]):
        send_ref[block] = unit


def page_kernel(length_any, hidden_any, weight_any, best_any, raw_any, unit_any, chosen_any, index_ref,
                hidden, weight, best, length, turned, raw_ref, unit_ref, chosen_ref, arrived, left):
    pages, slots, _ = hidden.shape
    dim, tiles = weight.shape[1], index_ref.shape[1]
    parts = slots // 256
    small = [
        pltpu.make_async_copy(best_any, best, arrived.at[pages]),
        pltpu.make_async_copy(weight_any, weight, arrived.at[pages + 1]),
        pltpu.make_async_copy(length_any, length, arrived.at[pages + 2]),
    ]

    def page_copy(page):
        return pltpu.make_async_copy(hidden_any.at[page], hidden.at[page], arrived.at[page])

    def raw_copy(page):
        return pltpu.make_async_copy(raw_ref.at[page], raw_any.at[page], left.at[0, page])

    def unit_copy(page):
        return pltpu.make_async_copy(unit_ref.at[page], unit_any.at[page], left.at[1, page])

    def chosen_copy(page, part):
        some = pl.ds(part * (tiles // 2), tiles // 2)
        return pltpu.make_async_copy(chosen_ref.at[page, some], chosen_any.at[page, some], left.at[2 + part, page])

    page_copy(0).start()
    for copy in small:
        copy.start()
    page_copy(1).start()
    small[0].wait()
    for page in range(pages):
        tokens = best[:, page, :].astype(F32)
        turned[...] = jnp.concatenate([tokens, jnp.zeros((96, 128), F32)], axis=0).T
        for core in range(2):
            halves = []
            for half in range(2):
                row = jnp.zeros((8, 128), F32)
                for query in range(4):
                    piece = turned[pl.ds(core * 8 + half * 4 + query, 8, stride=16), :]
                    row = row + (pltpu.roll(piece, 32 * query, 1) if query else piece)
                halves.append(row)
            index_ref[page, core * 8:core * 8 + 8, :] = jnp.concatenate(halves, axis=1).astype(jnp.int32)
    small[1].wait()
    small[2].wait()

    def one_page(page, carry):
        page_copy(page).wait()

        @pl.when(page + 2 < pages)
        def _():
            page_copy(page + 2).start()

        raw = jnp.dot(hidden[page], weight[...], preferred_element_type=F32).T
        raw_ref[page] = raw
        raw_copy(page).start()
        unit = raw * inverse_norm(raw)
        unit_ref[page] = jnp.where(iota(unit.shape, 1) < length[page], unit, unit[:, 0:1]).T.astype(BF16)
        unit_copy(page).start()
        unit = unit.astype(BF16)
        table = jnp.concatenate([unit[:, part * 256:(part + 1) * 256] for part in range(parts)], axis=0)

        def one_tile(tile, inner):
            index = index_ref[page, pl.ds(tile, 1), :]
            found = jnp.dot(table, one_hot(index & 255), preferred_element_type=F32)
            which = index >> 8
            chosen = found[0:dim]
            for part in range(1, parts):
                chosen = jnp.where(which == part, found[part * dim:(part + 1) * dim], chosen)
            chosen_ref[page, tile] = chosen.astype(BF16)

        def half_of_tiles(part, inner):
            for tile in range(tiles // 2):
                one_tile(part * (tiles // 2) + tile, inner)
            chosen_copy(page, part).start()
            return inner

        return lax.fori_loop(0, 2, half_of_tiles, carry)

    lax.fori_loop(0, pages, one_page, 0)
    for page in range(pages):
        raw_copy(page).wait()
        unit_copy(page).wait()
        for part in range(2):
            chosen_copy(page, part).wait()


def best_scores(queries, unit_ref, out, row):
    for page in range(unit_ref.shape[0]):
        scores = jnp.dot(unit_ref[page], queries, preferred_element_type=F32)
        top = jnp.max(scores.reshape(-1, 8, scores.shape[1]), axis=0)
        out[page, pl.ds(row, 1), :] = jnp.max(top, axis=0, keepdims=True)


def near_kernel(query_ref, unit_ref, hidden_any, best_ref, hidden_ref, arrived):
    hidden_copy = pltpu.make_async_copy(hidden_any, hidden_ref, arrived)
    hidden_copy.start()

    def one_tile(tile, carry):
        best_scores(query_ref[tile], unit_ref, best_ref, tile)
        return carry

    lax.fori_loop(0, query_ref.shape[0], one_tile, 0, unroll=2)
    hidden_copy.wait()


def mixed(expo_ref, chosen_ref, tile):
    result = expo_ref[0, pl.ds(tile, 1), :] * chosen_ref[0, tile].astype(F32)
    for page in range(1, expo_ref.shape[0]):
        result = result + expo_ref[page, pl.ds(tile, 1), :] * chosen_ref[page, tile].astype(F32)
    return result


def far_kernel(multiplier, place_ref, query_ref, unit_ref, near_ref, chosen_ref, expo_ref, total_ref, pair_ref, best):
    core = place_ref[0]
    pages, chips = near_ref.shape[:2]
    dim, lanes = query_ref.shape[1:]
    near = pl.multiple_of(core * chips, chips)
    far = pl.multiple_of((1 - core) * chips, chips)
    for page in range(pages):
        best[page, pl.ds(near, chips), :] = near_ref[page]

    def one_tile(tile, carry):
        best_scores(query_ref[tile], unit_ref, best, far + tile)
        return carry

    lax.fori_loop(0, chips, one_tile, 0, unroll=2)

    segment = jnp.where(iota((lanes, lanes), 0) // 32 == iota((lanes, lanes), 1) // 32, 1.0, 0.0).astype(BF16)
    value = best[...].reshape(pages * 2 * chips, lanes)
    score = jnp.zeros_like(value)
    for _ in range(3):
        part = value.astype(BF16)
        score = score + jnp.dot(part, segment, preferred_element_type=F32)
        value = value - part.astype(F32)
    expo = jnp.exp(score * multiplier).reshape(pages, 2 * chips, lanes)
    expo_ref[...] = expo
    total = jnp.sum(expo, axis=0)
    total = jnp.where(iota((2 * chips, 128), 1) % 32 < 16, total[:, :128], total[:, 128:])
    total_ref[...] = total
    high = total.astype(BF16)
    low = (total - high.astype(F32)).astype(BF16)

    def one_mix(tile, carry):
        pair_ref[tile, 0:dim, :] = mixed(expo_ref, chosen_ref, far + tile).astype(BF16)
        pair_ref[tile, dim:dim + 16, 0:128] = high
        pair_ref[tile, dim:dim + 16, 128:256] = low
        return carry

    lax.fori_loop(0, chips, one_mix, 0, unroll=2)


def keep_kernel(place_ref, expo_ref, chosen_ref, keep_ref, target_ref):
    core, chip = place_ref[0], place_ref[1]
    chips, dim, lanes = keep_ref.shape
    near = core * chips

    def one_mix(tile, carry):
        keep_ref[tile] = mixed(expo_ref, chosen_ref, near + tile)
        return carry

    lax.fori_loop(0, chips, one_mix, 0, unroll=2)
    picked = jnp.zeros((dim, lanes), F32)
    for page in range(expo_ref.shape[0]):
        picked = jnp.where(iota((dim, lanes), 1) // 64 == page, chosen_ref[page, near + chip].astype(F32), picked)
    target_ref[...] = picked


def add_kernel(place_ref, keep_ref, total_ref, pair_ref, send_ref, own_ref):
    chips, dim, _ = keep_ref.shape
    total = total_ref[...] + (pair_ref[0, dim:dim + 16, 0:128].astype(F32) + pair_ref[0, dim:dim + 16, 128:256].astype(F32))
    high = total.astype(BF16)
    low = (total - high.astype(F32)).astype(BF16)
    for tile in range(chips):
        send_ref[tile, 0:dim, :] = (keep_ref[tile] + pair_ref[tile, 0:dim, :].astype(F32)).astype(BF16)
        send_ref[tile, dim:dim + 16, 0:128] = high
        send_ref[tile, dim:dim + 16, 128:256] = low
    chip = place_ref[1]
    own_ref[...] = keep_ref[chip] + pair_ref[chip, 0:dim, :].astype(F32)


def gradient_kernel(multiplier, place_ref, index_ref, expo_ref, received_ref, own_ref, target_ref, near_ref, far_ref, page_raw,
                    hidden, query_raw_ref, query_hidden, keep_ref, give_ref, query_grad_ref, inverse_total, score_grad, summed_grad,
                    accumulated, turned):
    core, chip = place_ref[0], place_ref[1]
    chips, dim, lanes = near_ref.shape
    tiles = 2 * chips
    mine = core * chips + chip
    pages, slots, _ = hidden.shape
    parts = slots // 256
    total = jnp.zeros((tiles, 128), F32)
    for source in range(chips):
        total = total + received_ref[source, dim:dim + 16, 0:128].astype(F32) + received_ref[source, dim:dim + 16, 128:256].astype(F32)
    inverse = 1.0 / total
    first = iota((tiles, 128), 1) % 32 < 16
    inverse_total[:, 0:128] = jnp.where(first, inverse, pltpu.roll(inverse, 16, 1))
    inverse_total[:, 128:256] = jnp.where(first, pltpu.roll(inverse, 112, 1), inverse)
    accumulated[...] = jnp.zeros_like(accumulated)

    def one_page(page, carry):
        is_target = (iota((tiles, lanes), 0) == mine) & (iota((tiles, lanes), 1) // 64 == page)
        score_grad[...] = (expo_ref[page] * inverse_total[...] - jnp.where(is_target, 1.0, 0.0)) * multiplier
        for side, queries_ref in ((core, near_ref), (1 - core, far_ref)):
            for chip_of in range(chips):
                tile = side * chips + chip_of
                index = index_ref[page, pl.ds(tile, 1), :]
                weighted = queries_ref[chip_of].astype(F32) * score_grad[pl.ds(tile, 1), :]
                which = index >> 8
                left = jnp.concatenate([jnp.where(which == part, weighted, 0.0).astype(BF16) for part in range(parts)], axis=0)
                term = lax.dot_general(left, one_hot(index & 255), NT, preferred_element_type=F32)
                if queries_ref is near_ref and chip_of == 0:
                    summed_grad[...] = term
                else:
                    summed_grad[...] += term
        grad = jnp.concatenate([summed_grad[part * dim:(part + 1) * dim] for part in range(parts)], axis=1)
        direction = unit_backward(grad, page_raw[page]).astype(BF16)
        accumulated[...] += jnp.dot(direction, hidden[page], preferred_element_type=F32)
        return carry

    lax.fori_loop(0, pages, one_page, 0)
    summed = own_ref[...]
    for source in range(chips):
        summed = summed + jnp.where(chip == source, 0.0, received_ref[source, 0:dim, :].astype(F32))
    query_grad = (summed * inverse_total[pl.ds(mine, 1), :] - target_ref[...]) * multiplier
    query_grad_ref[...] = query_grad.T
    direction = unit_backward(query_grad, query_raw_ref[...]).astype(BF16)
    turned[...] = (accumulated[...] + jnp.dot(direction, query_hidden[...], preferred_element_type=F32)).T
    half = keep_ref.shape[0]
    keep_ref[...] = turned[pl.ds(pl.multiple_of(core * half, half), half), :]
    give_ref[...] = turned[pl.ds(pl.multiple_of((1 - core) * half, half), half), :].astype(BF16)


def shape(dims, kind):
    return jax.ShapeDtypeStruct(dims, kind)


def vmem(mib):
    return pltpu.CompilerParams(vmem_limit_bytes=mib * MIB)


def cost(flops, read):
    return pl.CostEstimate(flops=flops, bytes_accessed=read, transcendentals=0)


def swap_cores(value):
    return lax.ppermute(value, "core", [(0, 1), (1, 0)])


def summed(terms):
    return lax.optimization_barrier(jnp.sum(terms.astype(F32), axis=0)).astype(BF16)


def to_all(value, axis):
    return lax.all_to_all(jnp.broadcast_to(value[None], (lax.axis_size(axis),) + value.shape), axis, 0, 0, tiled=True)


def per_device(query_hidden, document_states, projection, lengths, best_token):
    query_count, tokens, hidden_size = query_hidden.shape
    pages, slots, _ = document_states.shape
    dim = projection.shape[1]
    chips, cores = lax.axis_size("chip"), lax.axis_size("core")
    tiles = chips * cores
    rows = query_count * tokens
    multiplier = 1.0 / (tokens * TEMPERATURE)
    smem = pl.BlockSpec(memory_space=pltpu.SMEM)
    inside = pl.BlockSpec(memory_space=pltpu.VMEM)
    anywhere = pl.BlockSpec(memory_space=pl.ANY)
    place = jnp.stack([lax.axis_index("core"), lax.axis_index("chip")]).astype(jnp.int32)
    query_rows = query_hidden.reshape(rows, hidden_size)

    query_raw, query_send = pl.pallas_call(
        query_kernel,
        in_specs=[anywhere] * 2,
        out_shape=(shape((dim, rows), F32), shape((chips, dim, rows), BF16)),
        scratch_shapes=[pltpu.VMEM((rows, hidden_size), BF16), pltpu.VMEM((hidden_size, dim), BF16), pltpu.SemaphoreType.DMA((2,))],
        compiler_params=vmem(QUERY_MIB),
        cost_estimate=cost(2 * rows * hidden_size * dim, 2 * MIB),
        name="query_project",
    )(query_rows, projection)
    near = lax.all_to_all(query_send, "chip", 0, 0, tiled=True)

    page_raw, page_unit, chosen, index = pl.pallas_call(
        page_kernel,
        in_specs=[anywhere] * 4,
        out_specs=[anywhere] * 3 + [inside],
        out_shape=(
            shape((pages, dim, slots), F32),
            shape((pages, slots, dim), BF16),
            shape((pages, tiles, dim, rows), BF16),
            shape((pages, tiles, rows), jnp.int32),
        ),
        scratch_shapes=[
            pltpu.VMEM((pages, slots, hidden_size), BF16),
            pltpu.VMEM((hidden_size, dim), BF16),
            pltpu.VMEM((tokens, pages, chips * cores * query_count), jnp.int32),
            pltpu.SMEM((pages,), jnp.int32),
            pltpu.VMEM((128, 128), F32),
            pltpu.VMEM((pages, dim, slots), F32),
            pltpu.VMEM((pages, slots, dim), BF16),
            pltpu.VMEM((pages, tiles, dim, rows), BF16),
            pltpu.SemaphoreType.DMA((pages + 3,)),
            pltpu.SemaphoreType.DMA((4, pages)),
        ],
        compiler_params=vmem(PAGE_MIB),
        cost_estimate=cost(2 * pages * slots * dim * (hidden_size + tiles * rows), 16 * MIB),
        name="page_project",
    )(lengths, document_states, projection, jnp.transpose(best_token, (1, 2, 0)))

    near, index = lax.optimization_barrier((near, index))
    far = swap_cores(near)
    near_best, page_hidden = pl.pallas_call(
        near_kernel,
        in_specs=[inside] * 2 + [anywhere],
        out_shape=(shape((pages, chips, rows), F32), shape((pages, slots, hidden_size), BF16)),
        scratch_shapes=[pltpu.SemaphoreType.DMA],
        compiler_params=vmem(NEAR_MIB),
        cost_estimate=cost(pages * slots * dim * tiles * rows, 2 * MIB),
        name="near_scores",
    )(near, page_unit, document_states)
    expo, total, pair = pl.pallas_call(
        lambda *refs: far_kernel(multiplier, *refs),
        in_specs=[smem] + [inside] * 4,
        out_shape=(shape((pages, tiles, rows), F32), shape((tiles, 128), F32), shape((chips, dim + 16, rows), BF16)),
        scratch_shapes=[pltpu.VMEM((pages, tiles, rows), F32)],
        compiler_params=vmem(FAR_MIB),
        cost_estimate=cost(pages * slots * dim * tiles * rows, 8 * MIB),
        name="far_scores",
    )(place, far, page_unit, near_best, chosen)
    keep, target = pl.pallas_call(
        keep_kernel,
        in_specs=[smem] + [inside] * 2,
        out_shape=(shape((chips, dim, rows), F32), shape((dim, rows), F32)),
        compiler_params=vmem(24),
        cost_estimate=cost(2 * pages * dim * tiles * rows, 4 * MIB),
        name="keep_terms",
    )(place, expo, chosen)
    send, own = pl.pallas_call(
        add_kernel,
        in_specs=[smem] + [inside] * 3,
        out_shape=(shape((chips, dim + 16, rows), BF16), shape((dim, rows), F32)),
        compiler_params=vmem(8),
        name="add_pair",
    )(place, keep, total, swap_cores(pair))
    received = lax.all_to_all(send, "chip", 0, 0, tiled=True)

    half = hidden_size // cores
    weight_keep, weight_give, query_grad = pl.pallas_call(
        lambda *refs: gradient_kernel(multiplier, *refs),
        in_specs=[smem] + [inside] * 11,
        out_shape=(shape((half, dim), F32), shape((half, dim), BF16), shape((rows, dim), F32)),
        scratch_shapes=[
            pltpu.VMEM((tiles, rows), F32),
            pltpu.VMEM((tiles, rows), F32),
            pltpu.VMEM((slots // 256 * dim, 256), F32),
            pltpu.VMEM((dim, hidden_size), F32),
            pltpu.VMEM((hidden_size, dim), F32),
        ],
        compiler_params=vmem(GRADIENT_MIB),
        cost_estimate=cost(2 * pages * slots * dim * (hidden_size + tiles * rows), 16 * MIB),
        name="gradients",
    )(place, index, expo, received, own, target, near, far, page_raw, page_hidden, query_raw, query_rows)

    halves = (weight_keep + swap_cores(weight_give).astype(F32)).astype(BF16)
    chunk = summed(lax.all_to_all(halves.reshape(chips, half // chips, dim), "chip", 0, 0, tiled=True))
    chunk = summed(to_all(chunk, "dp"))
    mine = to_all(chunk, "chip").reshape(half, dim)
    other = swap_cores(mine)
    first = lax.axis_index("core") == 0
    weight_grad = jnp.concatenate([jnp.where(first, mine, other), jnp.where(first, other, mine)], axis=0).astype(F32)
    return (weight_grad, query_grad.reshape(query_count, tokens, dim))


def solution(mesh):
    groups, gallery = mesh.devices.shape
    levels = Mesh(mesh.devices.reshape(groups, gallery // 2, 2), ("dp", "chip", "core"))
    every = ("dp", "chip", "core")
    return jax.shard_map(
        per_device,
        mesh=levels,
        in_specs=(P(every, None, None), P(every, None, None), P(), P(every), P("dp", None, ("chip", "core"))),
        out_specs=(P(), P(every, None, None)),
        check_vma=False,
    )
```

time: 107 us -> 101 us (0.944)
  blocking collectives: 56.1 us -> 46.6 us
  starting transfers between devices: 7.43 us -> 12.5 us
  local copies, waits for them, and re-layouts: 5.05 us -> 1.36 us
  waiting for transfers between devices: 2 us -> 3.14 us
    all_to_all x2 -> x3, blocking collectives: 40.1 us -> 30.6 us  [the longest x2 22.2 us: to_all(): lax.all_to_all(jnp.broadcast_to(value[None], (lax.axis_size(axis),) + val...]
    ppermute x2 -> x4, starting transfers between devices: 1.05 us -> 6.16 us  [swap_cores(): return lax.ppermute(value, 'core', [(0, 1), (1, 0)])]
    unnamed x13 -> x12, local copies, waits for them, and re-layouts: 3.79 us -> 1.3 us
    ppermute x2 -> x4, waiting for transfers between devices: 1.99 us -> 3.14 us  [swap_cores(): return lax.ppermute(value, 'core', [(0, 1), (1, 0)])]
    pallas_call x5 -> x6, Pallas kernels: 29.5 us -> 30 us  [the longest x1 12.2 us: per_device(): pl.pallas_call(page_kernel, in_specs=[anywhere] * 4, out_specs=[anywhere]...]
  transfers between devices with their start and end apart: 3 -> 5, of which waited for: 1 -> 3; matrix products, arithmetic and copies ran while one was open for 1% -> 0% of each run, Pallas kernels for 14% -> 17%
where the time goes in v4:
time: 101 us
  blocking collectives  46.6 us (46%)
  Pallas kernels  35.1 us (35%)
  starting transfers between devices  12.5 us (12%)
  waiting for transfers between devices  3.14 us (3%)
  local copies, waits for them, and re-layouts  1.36 us (1%)
  other arithmetic  1.17 us (1%)
    all_to_all x2, blocking collectives, to_all(): lax.all_to_all(jnp.broadcast_to(value[None], (lax.axis_size(axis),) + val...  22.2 us
    all_to_all x1, blocking collectives, per_device(): received = lax.all_to_all(send, 'chip', 0, 0, tiled=True)  16 us
    pallas_call x1, Pallas kernels, per_device(): pl.pallas_call(page_kernel, in_specs=[anywhere] * 4, out_specs=[anywhere]...  12.2 us
    pallas_call x1, Pallas kernels, per_device(): pl.pallas_call(lambda *refs: gradient_kernel(multiplier, *refs), in_specs...  9.74 us
    all_to_all x1, blocking collectives, per_device(): lax.all_to_all(halves.reshape(chips, half // chips, dim), 'chip', 0, 0, t...  8.44 us
    all_to_all x1, starting transfers between devices, per_device(): near = lax.all_to_all(query_send, 'chip', 0, 0, tiled=True)  6.38 us
    ppermute x4, starting transfers between devices, swap_cores(): return lax.ppermute(value, 'core', [(0, 1), (1, 0)])  6.16 us
    pallas_call x1, Pallas kernels, per_device(): pl.pallas_call(lambda *refs: far_kernel(multiplier, *refs), in_specs=[sme...  5.09 us
  transfers between devices with their start and end apart: 5, of which 3 were waited for; matrix products, arithmetic and copies ran while one was open for 0% of the time, Pallas kernels for 17%

profile of v4, /device:TPU:1, one launch (start us, length us, event | category | flops | bytes accessed | tf_op | source)
XLA Modules:
  0.0 100.6 jit_solution(11959046735235695091)
XLA Ops:
  0.6 2.6 %query_project.1 = (f32[128,256]{1,0:T(8,128)}, bf16[8,128,256]{2,1,0:T(8,128)(2,1)}) custom-call(bf16[256,1536]{1,0:T(8,128)(2,1)} %bitcast.9, bf16[1536,128]{1,0:T(8,128)(2,1)} %weight_any.3), custom_call_target="tpu_custom_call" | custom-call | flops 100663296 | bytes 2097152 | tf_op jit(solution)/shard_map/query_project/pallas_call | solution.py:324
  3.2 6.4 %all-to-all-start = ((bf16[8,128,256]{2,1,0:T(8,128)(2,1)}), bf16[8,128,256]{2,1,0:T(8,128)(2,1)S(1)}, u32[]{:S(2)}, u32[]{:S(2)}) async-start(bf16[8,128,256]{2,1,0:T(8,128)(2,1)} %get-tuple-element.22), calls=%async_computation | async-start | bytes 1048576 | tf_op jit(solution)/shard_map/all_to_all | solution.py:333
  9.6 12.2 %page_project.1 = (f32[4,128,768]{2,1,0:T(8,128)}, bf16[4,768,128]{2,1,0:T(8,128)(2,1)}, bf16[4,16,128,256]{3,2,1,0:T(8,128)(2,1)}, s32[4,16,256]{2,1,0:T(8,128)}) custom-call(s32[4]{0:T(128)} %length_any.1, bf16[4,768,1536]{2,1,0:T(8,128)(2,1)} %hidden_any.3, bf16[1536,128]{1,0:T(8,128)(2,1)} %weight_any.3, s32[32,4,128]{2,1,0:T(4,128)} %bitcast.13), custom_call_target="tpu_custom_call" | custom-call | flops 4429185024 | bytes 16777216 | tf_op jit(solution)/shard_map/page_project/pallas_call | solution.py:335
  21.8 0.0 all-to-all-done.query_ref.refs_6_
  21.8 1.0 %collective-permute-start = (bf16[8,128,256]{2,1,0:T(8,128)(2,1)S(1)}, bf16[8,128,256]{2,1,0:T(8,128)(2,1)S(1)}, u32[]{:S(2)}, u32[]{:S(2)}) collective-permute-start(bf16[8,128,256]{2,1,0:T(8,128)(2,1)S(1)} %all-to-all-done.query_ref.refs_6_), channel_id=1, source_target_pairs={{0,1},{1,0},{2,3},{3,2},{4,5},{5,4},{6,7},{7,6},{8,9},{9,8},{10,11... | collective-permute-start | bytes 1572872 | tf_op jit(solution)/shard_map/ppermute | solution.py:299
  22.8 0.0 copy-start
  22.8 0.1 pad_add_fusion.refs_0_.place_ref
  22.9 0.0 copy-start.2
  22.9 1.3 %copy-done.2 = bf16[4,768,128]{2,1,0:T(8,128)(2,1)S(1)} copy-done((bf16[4,768,128]{2,1,0:T(8,128)(2,1)S(1)}, bf16[4,768,128]{2,1,0:T(8,128)(2,1)}, u32[]{:S(2)}) %copy-start.2) | copy-done | bytes 786456
  24.2 0.0 copy-start.1
  24.2 0.0 copy-start.3
  24.2 0.0 copy-start.4
  24.2 0.0 copy-start.5
  24.2 3.9 %near_scores.1 = (f32[4,8,256]{2,1,0:T(8,128)S(1)}, bf16[4,768,1536]{2,1,0:T(8,128)(2,1)S(1)}) custom-call(bf16[8,128,256]{2,1,0:T(8,128)(2,1)S(1)} %all-to-all-done.query_ref.refs_6_, bf16[4,768,128]{2,1,0:T(8,128)(2,1)S(1)} %copy-done.2, bf16[4,768,1536]{2,1,0:T(8,128)(2,1)} %hidden_any.3), custom_call_target="tpu_custom_call" | custom-call | flops 1610612736 | bytes 2097152 | tf_op jit(solution)/shard_map/near_scores/pallas_call | solution.py:364
  28.1 0.0 collective-permute-done.refs_1_.refs_7_
  28.1 0.0 copy-done
  28.1 5.1 %far_scores.1 = (f32[4,16,256]{2,1,0:T(8,128)S(1)}, f32[16,128]{1,0:T(8,128)S(1)}, bf16[8,144,256]{2,1,0:T(8,128)(2,1)S(1)}) custom-call(s32[2]{0:T(128)S(1)} %pad_add_fusion.refs_0_.place_ref, bf16[8,128,256]{2,1,0:T(8,128)(2,1)S(1)} %collective-permute-done.refs_1_.refs_7_, bf16[4,768,128]{2,1,0:T(8,128)(2,1)S(1)} %copy-done.2, ...), custom_call_target="tpu_custom_call" | custom-call | flops 1610612736 | bytes 8388608 | tf_op jit(solution)/shard_map/far_scores/pallas_call | solution.py:373
  33.2 0.1 collective-permute-start.1
  33.3 1.0 keep_terms.1
  34.3 1.0 collective-permute-done.1.pair_ref
  35.3 0.6 add_pair.1
  35.9 16.0 %all_to_all.25.refs_3_ = bf16[8,144,256]{2,1,0:T(8,128)(2,1)S(1)} all-to-all(bf16[8,144,256]{2,1,0:T(8,128)(2,1)S(1)} %get-tuple-element.33), channel_id=1, replica_groups=mesh['dp'=8,'chip'=8,'core'=2] {'chip'}, dimensions={0} | all-to-all | bytes 1179648 | tf_op jit(solution)/shard_map/all_to_all | solution.py:397
  52.0 0.0 copy-done.1
  52.0 0.0 copy-done.3
  52.0 0.0 copy-done.4
  52.0 0.0 copy-done.5
  52.0 9.7 %gradients.1 = (f32[768,128]{1,0:T(8,128)S(1)}, bf16[768,128]{1,0:T(8,128)(2,1)S(1)}, f32[256,128]{1,0:T(8,128)}) custom-call(s32[2]{0:T(128)S(1)} %pad_add_fusion.refs_0_.place_ref, s32[4,16,256]{2,1,0:T(8,128)S(1)} %copy-done.5, f32[4,16,256]{2,1,0:T(8,128)S(1)} %get-tuple-element.29.expo_ref.refs_2_, bf16[8,144,256]{2,1,0:T(8,128)(2,1)S(1)} %all_to_all.25.refs_3_, ...), custom_call_target="tpu_custom_call" | custom-call | flops 4429185024 | bytes 16777216 | tf_op jit(solution)/shard_map/gradients/pallas_call | solution.py:400
  61.7 1.0 %collective-permute-start.2 = (bf16[768,128]{1,0:T(8,128)(2,1)S(1)}, bf16[768,128]{1,0:T(8,128)(2,1)S(1)}, u32[]{:S(2)}, u32[]{:S(2)}) collective-permute-start(bf16[768,128]{1,0:T(8,128)(2,1)S(1)} %get-tuple-element.40), channel_id=1, source_target_pairs={{0,1},{1,0},{2,3},{3,2},{4,5},{5,4},{6,7},{7,6},{8,9},{9,8},{10,11... | collective-permute-start | bytes 589832 | tf_op jit(solution)/shard_map/ppermute | solution.py:299
  62.8 1.1 %collective-permute-done.2 = bf16[768,128]{1,0:T(8,128)(2,1)S(1)} collective-permute-done((bf16[768,128]{1,0:T(8,128)(2,1)S(1)}, bf16[768,128]{1,0:T(8,128)(2,1)S(1)}, u32[]{:S(2)}, u32[]{:S(2)}) %collective-permute-start.2) | collective-permute-done | bytes 196640 | tf_op jit(solution)/shard_map/ppermute | solution.py:299
  63.8 0.1 add_convert_fusion
  63.9 8.4 %all_to_all.26 = bf16[8,96,128]{2,1,0:T(8,128)(2,1)S(1)} all-to-all(bf16[8,96,128]{2,1,0:T(8,128)(2,1)S(1)} %bitcast.12), channel_id=1, replica_groups=mesh['dp'=8,'chip'=8,'core'=2] {'chip'}, dimensions={0} | all-to-all | bytes 393216 | tf_op jit(solution)/shard_map/all_to_all | solution.py:417
  72.4 14.0 %all_to_all.27 = bf16[8,96,128]{2,1,0:T(8,128)(2,1)S(1)} all-to-all(bf16[8,96,128]{2,1,0:T(8,128)(2,1)S(1)} %broadcast_in_dim.4), channel_id=1, replica_groups=mesh['dp'=8,'chip'=8,'core'=2] {'dp'}, dimensions={0} | all-to-all | bytes 393216 | tf_op jit(solution)/shard_map/all_to_all | solution.py:307
  86.4 8.2 %all_to_all.28 = bf16[8,96,128]{2,1,0:T(8,128)(2,1)S(1)} all-to-all(bf16[8,96,128]{2,1,0:T(8,128)(2,1)S(1)} %broadcast_in_dim.5), channel_id=1, replica_groups=mesh['dp'=8,'chip'=8,'core'=2] {'chip'}, dimensions={0} | all-to-all | bytes 393216 | tf_op jit(solution)/shard_map/all_to_all | solution.py:307
  94.6 4.0 %collective-permute-start.3 = (bf16[768,128]{1,0:T(8,128)(2,1)S(1)}, bf16[768,128]{1,0:T(8,128)(2,1)S(1)}, u32[]{:S(2)}, u32[]{:S(2)}) collective-permute-start(bf16[768,128]{1,0:T(8,128)(2,1)S(1)} %bitcast.11), channel_id=1, source_target_pairs={{0,1},{1,0},{2,3},{3,2},{4,5},{5,4},{6,7},{7,6},{8,9},{9,8},{10,11... | collective-permute-start | bytes 589832 | tf_op jit(solution)/shard_map/ppermute | solution.py:299
  98.6 1.1 %collective-permute-done.3 = bf16[768,128]{1,0:T(8,128)(2,1)S(1)} collective-permute-done((bf16[768,128]{1,0:T(8,128)(2,1)S(1)}, bf16[768,128]{1,0:T(8,128)(2,1)S(1)}, u32[]{:S(2)}, u32[]{:S(2)}) %collective-permute-start.3) | collective-permute-done | bytes 196640 | tf_op jit(solution)/shard_map/ppermute | solution.py:299
  99.7 0.9 maximum_convert_fusion
  (5 shorter events, 0.2 us)
Async XLA Ops:
  3.2 18.6 %all-to-all-start = ((bf16[8,128,256]{2,1,0:T(8,128)(2,1)}), bf16[8,128,256]{2,1,0:T(8,128)(2,1)S(1)}, u32[]{:S(2)}, u32[]{:S(2)}) async-start(bf16[8,128,256]{2,1,0:T(8,128)(2,1)} %get-tuple-element.22), calls=%async_computation | async-start | bytes 1048576 | tf_op jit(solution)/shard_map/all_to_all | solution.py:333
  21.8 6.3 %collective-permute-start = (bf16[8,128,256]{2,1,0:T(8,128)(2,1)S(1)}, bf16[8,128,256]{2,1,0:T(8,128)(2,1)S(1)}, u32[]{:S(2)}, u32[]{:S(2)}) collective-permute-start(bf16[8,128,256]{2,1,0:T(8,128)(2,1)S(1)} %all-to-all-done.query_ref.refs_6_), channel_id=1, source_target_pairs={{0,1},{1,0},{2,3},{3,2},{4,5},{5,4},{6,7},{7,6},{8,9},{9,8},{10,11... | collective-permute-start | bytes 1572872 | tf_op jit(solution)/shard_map/ppermute | solution.py:299
  22.8 5.3 %copy-start = (bf16[4,16,128,256]{3,2,1,0:T(8,128)(2,1)S(1)}, bf16[4,16,128,256]{3,2,1,0:T(8,128)(2,1)}, u32[]{:S(2)}) copy-start(bf16[4,16,128,256]{3,2,1,0:T(8,128)(2,1)} %get-tuple-element.28.refs_4_.chosen_ref) | copy-start | bytes 12582916
  22.9 1.3 %copy-start.2 = (bf16[4,768,128]{2,1,0:T(8,128)(2,1)S(1)}, bf16[4,768,128]{2,1,0:T(8,128)(2,1)}, u32[]{:S(2)}) copy-start(bf16[4,768,128]{2,1,0:T(8,128)(2,1)} %get-tuple-element.26.unit_ref.refs_2_) | copy-start | bytes 2359300
  24.2 27.8 %copy-start.1 = (bf16[8,32,1536]{2,1,0:T(8,128)(2,1)S(1)}, bf16[8,32,1536]{2,1,0:T(8,128)(2,1)}, u32[]{:S(2)}) copy-start(bf16[8,32,1536]{2,1,0:T(8,128)(2,1)} %param.5) | copy-start | bytes 2359300
  24.2 27.8 %copy-start.3 = (f32[128,256]{1,0:T(8,128)S(1)}, f32[128,256]{1,0:T(8,128)}, u32[]{:S(2)}) copy-start(f32[128,256]{1,0:T(8,128)} %get-tuple-element.38.refs_10_) | copy-start | bytes 393220
  24.2 27.8 %copy-start.4 = (f32[4,128,768]{2,1,0:T(8,128)S(1)}, f32[4,128,768]{2,1,0:T(8,128)}, u32[]{:S(2)}) copy-start(f32[4,128,768]{2,1,0:T(8,128)} %get-tuple-element.36.refs_8_) | copy-start | bytes 4718596
  24.2 27.8 %copy-start.5 = (s32[4,16,256]{2,1,0:T(8,128)S(1)}, s32[4,16,256]{2,1,0:T(8,128)}, u32[]{:S(2)}) copy-start(s32[4,16,256]{2,1,0:T(8,128)} %get-tuple-element.24.refs_1_) | copy-start | bytes 196612
  33.2 2.1 %collective-permute-start.1 = (bf16[8,144,256]{2,1,0:T(8,128)(2,1)S(1)}, bf16[8,144,256]{2,1,0:T(8,128)(2,1)S(1)}, u32[]{:S(2)}, u32[]{:S(2)}) collective-permute-start(bf16[8,144,256]{2,1,0:T(8,128)(2,1)S(1)} %get-tuple-element.32), channel_id=1, source_target_pairs={{0,1},{1,0},{2,3},{3,2},{4,5},{5,4},{6,7},{7,6},{8,9},{9,8},{10,11... | collective-permute-start | bytes 1769480 | tf_op jit(solution)/shard_map/ppermute | solution.py:299
  61.7 2.1 %collective-permute-start.2 = (bf16[768,128]{1,0:T(8,128)(2,1)S(1)}, bf16[768,128]{1,0:T(8,128)(2,1)S(1)}, u32[]{:S(2)}, u32[]{:S(2)}) collective-permute-start(bf16[768,128]{1,0:T(8,128)(2,1)S(1)} %get-tuple-element.40), channel_id=1, source_target_pairs={{0,1},{1,0},{2,3},{3,2},{4,5},{5,4},{6,7},{7,6},{8,9},{9,8},{10,11... | collective-permute-start | bytes 589832 | tf_op jit(solution)/shard_map/ppermute | solution.py:299
  94.6 5.0 %collective-permute-start.3 = (bf16[768,128]{1,0:T(8,128)(2,1)S(1)}, bf16[768,128]{1,0:T(8,128)(2,1)S(1)}, u32[]{:S(2)}, u32[]{:S(2)}) collective-permute-start(bf16[768,128]{1,0:T(8,128)(2,1)S(1)} %bitcast.11), channel_id=1, source_target_pairs={{0,1},{1,0},{2,3},{3,2},{4,5},{5,4},{6,7},{7,6},{8,9},{9,8},{10,11... | collective-permute-start | bytes 589832 | tf_op jit(solution)/shard_map/ppermute | solution.py:299

commit v5 on v4

--- a/solution.py
+++ b/solution.py
@@ -97,40 +97,34 @@
     small[1].wait()
     small[2].wait()
 
-    def one_page(page, carry):
+    def project(page):
         page_copy(page).wait()
-
-        @pl.when(page + 2 < pages)
-        def _():
+        if page + 2 < pages:
             page_copy(page + 2).start()
-
-        raw = jnp.dot(hidden[page], weight[...], preferred_element_type=F32).T
-        raw_ref[page] = raw
+        raw_ref[page] = jnp.dot(hidden[page], weight[...], preferred_element_type=F32).T
         raw_copy(page).start()
+
+    project(0)
+    for page in range(pages):
+        if page + 1 < pages:
+            project(page + 1)
+        raw = raw_ref[page]
         unit = raw * inverse_norm(raw)
         unit_ref[page] = jnp.where(iota(unit.shape, 1) < length[page], unit, unit[:, 0:1]).T.astype(BF16)
         unit_copy(page).start()
         unit = unit.astype(BF16)
         table = jnp.concatenate([unit[:, part * 256:(part + 1) * 256] for part in range(parts)], axis=0)
 
-        def one_tile(tile, inner):
-            index = index_ref[page, pl.ds(tile, 1), :]
+        for tile in range(tiles):
+            index = index_ref[page, tile:tile + 1, :]
             found = jnp.dot(table, one_hot(index & 255), preferred_element_type=F32)
             which = index >> 8
             chosen = found[0:dim]
             for part in range(1, parts):
                 chosen = jnp.where(which == part, found[part * dim:(part + 1) * dim], chosen)
             chosen_ref[page, tile] = chosen.astype(BF16)
-
-        def half_of_tiles(part, inner):
-            for tile in range(tiles // 2):
-                one_tile(part * (tiles // 2) + tile, inner)
-            chosen_copy(page, part).start()
-            return inner
-
-        return lax.fori_loop(0, 2, half_of_tiles, carry)
-
-    lax.fori_loop(0, pages, one_page, 0)
+            if (tile + 1) % (tiles // 2) == 0:
+                chosen_copy(page, tile // (tiles // 2)).start()
     for page in range(pages):
         raw_copy(page).wait()
         unit_copy(page).wait()
@@ -149,11 +143,8 @@
     hidden_copy = pltpu.make_async_copy(hidden_any, hidden_ref, arrived)
     hidden_copy.start()
 
-    def one_tile(tile, carry):
+    for tile in range(query_ref.shape[0]):
         best_scores(query_ref[tile], unit_ref, best_ref, tile)
-        return carry
-
-    lax.fori_loop(0, query_ref.shape[0], one_tile, 0, unroll=2)
     hidden_copy.wait()
 
 
@@ -173,11 +164,8 @@
     for page in range(pages):
         best[page, pl.ds(near, chips), :] = near_ref[page]
 
-    def one_tile(tile, carry):
+    for tile in range(chips):
         best_scores(query_ref[tile], unit_ref, best, far + tile)
-        return carry
-
-    lax.fori_loop(0, chips, one_tile, 0, unroll=2)
 
     segment = jnp.where(iota((lanes, lanes), 0) // 32 == iota((lanes, lanes), 1) // 32, 1.0, 0.0).astype(BF16)
     value = best[...].reshape(pages * 2 * chips, lanes)
@@ -250,27 +238,24 @@
     inverse_total[:, 128:256] = jnp.where(first, pltpu.roll(inverse, 112, 1), inverse)
     accumulated[...] = jnp.zeros_like(accumulated)
 
-    def one_page(page, carry):
+    def scattered(page, tile, weighted):
+        index = index_ref[page, pl.ds(tile, 1), :]
+        which = index >> 8
+        left = jnp.concatenate([jnp.where(which == part, weighted, 0.0).astype(BF16) for part in range(parts)], axis=0)
+        return lax.dot_general(left, one_hot(index & 255), NT, preferred_element_type=F32)
+
+    for page in range(pages):
         is_target = (iota((tiles, lanes), 0) == mine) & (iota((tiles, lanes), 1) // 64 == page)
         score_grad[...] = (expo_ref[page] * inverse_total[...] - jnp.where(is_target, 1.0, 0.0)) * multiplier
+        weighted = near_ref[chip].astype(F32) * score_grad[pl.ds(mine, 1), :]
+        summed_grad[...] = scattered(page, mine, weighted - weighted.astype(BF16).astype(F32))
         for side, queries_ref in ((core, near_ref), (1 - core, far_ref)):
             for chip_of in range(chips):
                 tile = side * chips + chip_of
-                index = index_ref[page, pl.ds(tile, 1), :]
-                weighted = queries_ref[chip_of].astype(F32) * score_grad[pl.ds(tile, 1), :]
-                which = index >> 8
-                left = jnp.concatenate([jnp.where(which == part, weighted, 0.0).astype(BF16) for part in range(parts)], axis=0)
-                term = lax.dot_general(left, one_hot(index & 255), NT, preferred_element_type=F32)
-                if queries_ref is near_ref and chip_of == 0:
-                    summed_grad[...] = term
-                else:
-                    summed_grad[...] += term
+                summed_grad[...] += scattered(page, tile, queries_ref[chip_of].astype(F32) * score_grad[pl.ds(tile, 1), :])
         grad = jnp.concatenate([summed_grad[part * dim:(part + 1) * dim] for part in range(parts)], axis=1)
         direction = unit_backward(grad, page_raw[page]).astype(BF16)
         accumulated[...] += jnp.dot(direction, hidden[page], preferred_element_type=F32)
-        return carry
-
-    lax.fori_loop(0, pages, one_page, 0)
     summed = own_ref[...]
     for source in range(chips):
         summed = summed + jnp.where(chip == source, 0.0, received_ref[source, 0:dim, :].astype(F32))
@@ -280,7 +265,7 @@
     turned[...] = (accumulated[...] + jnp.dot(direction, query_hidden[...], preferred_element_type=F32)).T
     half = keep_ref.shape[0]
     keep_ref[...] = turned[pl.ds(pl.multiple_of(core * half, half), half), :]
-    give_ref[...] = turned[pl.ds(pl.multiple_of((1 - core) * half, half), half), :].astype(BF16)
+    give_ref[...] = turned[pl.ds(pl.multiple_of((1 - core) * half, half), half), :]
 
 
 def shape(dims, kind):
@@ -400,7 +385,7 @@
     weight_keep, weight_give, query_grad = pl.pallas_call(
         lambda *refs: gradient_kernel(multiplier, *refs),
         in_specs=[smem] + [inside] * 11,
-        out_shape=(shape((half, dim), F32), shape((half, dim), BF16), shape((rows, dim), F32)),
+        out_shape=(shape((half, dim), F32), shape((half, dim), F32), shape((rows, dim), F32)),
         scratch_shapes=[
             pltpu.VMEM((tiles, rows), F32),
             pltpu.VMEM((tiles, rows), F32),
@@ -413,7 +398,7 @@
         name="gradients",
     )(place, index, expo, received, own, target, near, far, page_raw, page_hidden, query_raw, query_rows)
 
-    halves = (weight_keep + swap_cores(weight_give).astype(F32)).astype(BF16)
+    halves = (weight_keep + swap_cores(weight_give)).astype(BF16)
     chunk = summed(lax.all_to_all(halves.reshape(chips, half // chips, dim), "chip", 0, 0, tiled=True))
     chunk = summed(to_all(chunk, "dp"))
     mine = to_all(chunk, "chip").reshape(half, dim)

time: 101 us -> 97.8 us (0.968)
  Pallas kernels: 35.1 us -> 31.4 us
    pallas_call x1, Pallas kernels: 9.74 us -> 7.48 us  [per_device(): pl.pallas_call(lambda *refs: gradient_kernel(multiplier, *refs), in_specs...]
where the time goes in v5:
time: 97.8 us; the launch traced here: 97.5 us
  blocking collectives  46.6 us (48%)
  Pallas kernels  31.4 us (32%)
  starting transfers between devices  12.7 us (13%)
  waiting for transfers between devices  3.42 us (3%)
  local copies, waits for them, and re-layouts  1.36 us (1%)
  other arithmetic  1.15 us (1%)
    all_to_all x2, blocking collectives, to_all(): lax.all_to_all(jnp.broadcast_to(value[None], (lax.axis_size(axis),) + val...  22.2 us
    all_to_all x1, blocking collectives, per_device(): received = lax.all_to_all(send, 'chip', 0, 0, tiled=True)  16 us
    pallas_call x1, Pallas kernels, per_device(): pl.pallas_call(page_kernel, in_specs=[anywhere] * 4, out_specs=[anywhere]...  11.3 us
    all_to_all x1, blocking collectives, per_device(): lax.all_to_all(halves.reshape(chips, half // chips, dim), 'chip', 0, 0, t...  8.44 us
    pallas_call x1, Pallas kernels, per_device(): pl.pallas_call(lambda *refs: gradient_kernel(multiplier, *refs), in_specs...  7.48 us
    all_to_all x1, starting transfers between devices, per_device(): near = lax.all_to_all(query_send, 'chip', 0, 0, tiled=True)  6.39 us
    ppermute x4, starting transfers between devices, swap_cores(): return lax.ppermute(value, 'core', [(0, 1), (1, 0)])  6.36 us
    pallas_call x1, Pallas kernels, per_device(): pl.pallas_call(lambda *refs: far_kernel(multiplier, *refs), in_specs=[sme...  4.65 us
  transfers between devices with their start and end apart: 5, of which 3 were waited for; matrix products, arithmetic and copies ran while one was open for 0% of the time, Pallas kernels for 17%

profile of v5, /device:TPU:1, one launch (start us, length us, event | category | flops | bytes accessed | tf_op | source)
XLA Modules:
  0.0 97.5 jit_solution(10696043307075428232)
XLA Ops:
  0.6 2.6 %query_project.1 = (f32[128,256]{1,0:T(8,128)}, bf16[8,128,256]{2,1,0:T(8,128)(2,1)}) custom-call(bf16[256,1536]{1,0:T(8,128)(2,1)} %bitcast.9, bf16[1536,128]{1,0:T(8,128)(2,1)} %weight_any.3), custom_call_target="tpu_custom_call" | custom-call | flops 100663296 | bytes 2097152 | tf_op jit(solution)/shard_map/query_project/pallas_call | solution.py:309
  3.2 6.4 %all-to-all-start = ((bf16[8,128,256]{2,1,0:T(8,128)(2,1)}), bf16[8,128,256]{2,1,0:T(8,128)(2,1)S(1)}, u32[]{:S(2)}, u32[]{:S(2)}) async-start(bf16[8,128,256]{2,1,0:T(8,128)(2,1)} %get-tuple-element.22), calls=%async_computation | async-start | bytes 1048576 | tf_op jit(solution)/shard_map/all_to_all | solution.py:318
  9.6 11.3 %page_project.1 = (f32[4,128,768]{2,1,0:T(8,128)}, bf16[4,768,128]{2,1,0:T(8,128)(2,1)}, bf16[4,16,128,256]{3,2,1,0:T(8,128)(2,1)}, s32[4,16,256]{2,1,0:T(8,128)}) custom-call(s32[4]{0:T(128)} %length_any.1, bf16[4,768,1536]{2,1,0:T(8,128)(2,1)} %hidden_any.3, bf16[1536,128]{1,0:T(8,128)(2,1)} %weight_any.3, s32[32,4,128]{2,1,0:T(4,128)} %bitcast.13), custom_call_target="tpu_custom_call" | custom-call | flops 4429185024 | bytes 16777216 | tf_op jit(solution)/shard_map/page_project/pallas_call | solution.py:320
  20.9 0.0 all-to-all-done.query_ref.refs_6_
  20.9 1.2 %collective-permute-start = (bf16[8,128,256]{2,1,0:T(8,128)(2,1)S(1)}, bf16[8,128,256]{2,1,0:T(8,128)(2,1)S(1)}, u32[]{:S(2)}, u32[]{:S(2)}) collective-permute-start(bf16[8,128,256]{2,1,0:T(8,128)(2,1)S(1)} %all-to-all-done.query_ref.refs_6_), channel_id=1, source_target_pairs={{0,1},{1,0},{2,3},{3,2},{4,5},{5,4},{6,7},{7,6},{8,9},{9,8},{10,11... | collective-permute-start | bytes 1572872 | tf_op jit(solution)/shard_map/ppermute | solution.py:284
  22.1 0.0 copy-start
  22.1 0.1 pad_add_fusion.refs_0_.place_ref
  22.2 0.0 copy-start.2
  22.2 1.3 %copy-done.2 = bf16[4,768,128]{2,1,0:T(8,128)(2,1)S(1)} copy-done((bf16[4,768,128]{2,1,0:T(8,128)(2,1)S(1)}, bf16[4,768,128]{2,1,0:T(8,128)(2,1)}, u32[]{:S(2)}) %copy-start.2) | copy-done | bytes 786456
  23.5 0.0 copy-start.1
  23.5 0.0 copy-start.3
  23.5 0.0 copy-start.4
  23.5 0.0 copy-start.5
  23.5 3.8 %near_scores.1 = (f32[4,8,256]{2,1,0:T(8,128)S(1)}, bf16[4,768,1536]{2,1,0:T(8,128)(2,1)S(1)}) custom-call(bf16[8,128,256]{2,1,0:T(8,128)(2,1)S(1)} %all-to-all-done.query_ref.refs_6_, bf16[4,768,128]{2,1,0:T(8,128)(2,1)S(1)} %copy-done.2, bf16[4,768,1536]{2,1,0:T(8,128)(2,1)} %hidden_any.3), custom_call_target="tpu_custom_call" | custom-call | flops 1610612736 | bytes 2097152 | tf_op jit(solution)/shard_map/near_scores/pallas_call | solution.py:349
  27.3 0.0 collective-permute-done.refs_1_.refs_7_
  27.3 0.0 copy-done
  27.4 4.7 %far_scores.1 = (f32[4,16,256]{2,1,0:T(8,128)S(1)}, f32[16,128]{1,0:T(8,128)S(1)}, bf16[8,144,256]{2,1,0:T(8,128)(2,1)S(1)}) custom-call(s32[2]{0:T(128)S(1)} %pad_add_fusion.refs_0_.place_ref, bf16[8,128,256]{2,1,0:T(8,128)(2,1)S(1)} %collective-permute-done.refs_1_.refs_7_, bf16[4,768,128]{2,1,0:T(8,128)(2,1)S(1)} %copy-done.2, ...), custom_call_target="tpu_custom_call" | custom-call | flops 1610612736 | bytes 8388608 | tf_op jit(solution)/shard_map/far_scores/pallas_call | solution.py:358
  32.0 0.1 collective-permute-start.1
  32.1 1.0 keep_terms.1
  33.1 1.0 %collective-permute-done.1.pair_ref = bf16[8,144,256]{2,1,0:T(8,128)(2,1)S(1)} collective-permute-done((bf16[8,144,256]{2,1,0:T(8,128)(2,1)S(1)}, bf16[8,144,256]{2,1,0:T(8,128)(2,1)S(1)}, u32[]{:S(2)}, u32[]{:S(2)}) %collective-permute-start.1) | collective-permute-done | bytes 589856 | tf_op jit(solution)/shard_map/ppermute | solution.py:284
  34.1 0.6 add_pair.1
  34.7 16.0 %all_to_all.25.refs_3_ = bf16[8,144,256]{2,1,0:T(8,128)(2,1)S(1)} all-to-all(bf16[8,144,256]{2,1,0:T(8,128)(2,1)S(1)} %get-tuple-element.33), channel_id=1, replica_groups=mesh['dp'=8,'chip'=8,'core'=2] {'chip'}, dimensions={0} | all-to-all | bytes 1179648 | tf_op jit(solution)/shard_map/all_to_all | solution.py:382
  50.8 0.0 copy-done.1
  50.8 0.0 copy-done.3
  50.8 0.0 copy-done.4
  50.8 0.0 copy-done.5
  50.8 7.5 %gradients.1 = (f32[768,128]{1,0:T(8,128)S(1)}, f32[768,128]{1,0:T(8,128)S(1)}, f32[256,128]{1,0:T(8,128)}) custom-call(s32[2]{0:T(128)S(1)} %pad_add_fusion.refs_0_.place_ref, s32[4,16,256]{2,1,0:T(8,128)S(1)} %copy-done.5, f32[4,16,256]{2,1,0:T(8,128)S(1)} %get-tuple-element.29.expo_ref.refs_2_, bf16[8,144,256]{2,1,0:T(8,128)(2,1)S(1)} %all_to_all.25.refs_3_, ...), custom_call_target="tpu_custom_call" | custom-call | flops 4429185024 | bytes 16777216 | tf_op jit(solution)/shard_map/gradients/pallas_call | solution.py:385
  58.3 1.1 %collective-permute-start.2 = (f32[768,128]{1,0:T(8,128)S(1)}, f32[768,128]{1,0:T(8,128)S(1)}, u32[]{:S(2)}, u32[]{:S(2)}) collective-permute-start(f32[768,128]{1,0:T(8,128)S(1)} %get-tuple-element.40), channel_id=1, source_target_pairs={{0,1},{1,0},{2,3},{3,2},{4,5},{5,4},{6,7},{7,6},{8,9},{9,8},{10,11... | collective-permute-start | bytes 1179656 | tf_op jit(solution)/shard_map/ppermute | solution.py:284
  59.3 1.3 %collective-permute-done.2 = f32[768,128]{1,0:T(8,128)S(1)} collective-permute-done((f32[768,128]{1,0:T(8,128)S(1)}, f32[768,128]{1,0:T(8,128)S(1)}, u32[]{:S(2)}, u32[]{:S(2)}) %collective-permute-start.2) | collective-permute-done | bytes 393248 | tf_op jit(solution)/shard_map/ppermute | solution.py:284
  60.7 8.4 %all_to_all.26 = bf16[8,96,128]{2,1,0:T(8,128)(2,1)S(1)} all-to-all(bf16[8,96,128]{2,1,0:T(8,128)(2,1)S(1)} %bitcast.12), channel_id=1, replica_groups=mesh['dp'=8,'chip'=8,'core'=2] {'chip'}, dimensions={0} | all-to-all | bytes 393216 | tf_op jit(solution)/shard_map/all_to_all | solution.py:402
  69.2 14.0 %all_to_all.27 = bf16[8,96,128]{2,1,0:T(8,128)(2,1)S(1)} all-to-all(bf16[8,96,128]{2,1,0:T(8,128)(2,1)S(1)} %broadcast_in_dim.4), channel_id=1, replica_groups=mesh['dp'=8,'chip'=8,'core'=2] {'dp'}, dimensions={0} | all-to-all | bytes 393216 | tf_op jit(solution)/shard_map/all_to_all | solution.py:292
  83.3 8.2 %all_to_all.28 = bf16[8,96,128]{2,1,0:T(8,128)(2,1)S(1)} all-to-all(bf16[8,96,128]{2,1,0:T(8,128)(2,1)S(1)} %broadcast_in_dim.5), channel_id=1, replica_groups=mesh['dp'=8,'chip'=8,'core'=2] {'chip'}, dimensions={0} | all-to-all | bytes 393216 | tf_op jit(solution)/shard_map/all_to_all | solution.py:292
  91.4 4.0 %collective-permute-start.3 = (bf16[768,128]{1,0:T(8,128)(2,1)S(1)}, bf16[768,128]{1,0:T(8,128)(2,1)S(1)}, u32[]{:S(2)}, u32[]{:S(2)}) collective-permute-start(bf16[768,128]{1,0:T(8,128)(2,1)S(1)} %bitcast.11), channel_id=1, source_target_pairs={{0,1},{1,0},{2,3},{3,2},{4,5},{5,4},{6,7},{7,6},{8,9},{9,8},{10,11... | collective-permute-start | bytes 589832 | tf_op jit(solution)/shard_map/ppermute | solution.py:284
  95.4 1.1 %collective-permute-done.3 = bf16[768,128]{1,0:T(8,128)(2,1)S(1)} collective-permute-done((bf16[768,128]{1,0:T(8,128)(2,1)S(1)}, bf16[768,128]{1,0:T(8,128)(2,1)S(1)}, u32[]{:S(2)}, u32[]{:S(2)}) %collective-permute-start.3) | collective-permute-done | bytes 196640 | tf_op jit(solution)/shard_map/ppermute | solution.py:284
  96.5 0.9 maximum_convert_fusion
  (6 shorter events, 0.2 us)
Async XLA Ops:
  3.2 17.7 %all-to-all-start = ((bf16[8,128,256]{2,1,0:T(8,128)(2,1)}), bf16[8,128,256]{2,1,0:T(8,128)(2,1)S(1)}, u32[]{:S(2)}, u32[]{:S(2)}) async-start(bf16[8,128,256]{2,1,0:T(8,128)(2,1)} %get-tuple-element.22), calls=%async_computation | async-start | bytes 1048576 | tf_op jit(solution)/shard_map/all_to_all | solution.py:318
  20.9 6.4 %collective-permute-start = (bf16[8,128,256]{2,1,0:T(8,128)(2,1)S(1)}, bf16[8,128,256]{2,1,0:T(8,128)(2,1)S(1)}, u32[]{:S(2)}, u32[]{:S(2)}) collective-permute-start(bf16[8,128,256]{2,1,0:T(8,128)(2,1)S(1)} %all-to-all-done.query_ref.refs_6_), channel_id=1, source_target_pairs={{0,1},{1,0},{2,3},{3,2},{4,5},{5,4},{6,7},{7,6},{8,9},{9,8},{10,11... | collective-permute-start | bytes 1572872 | tf_op jit(solution)/shard_map/ppermute | solution.py:284
  22.1 5.2 %copy-start = (bf16[4,16,128,256]{3,2,1,0:T(8,128)(2,1)S(1)}, bf16[4,16,128,256]{3,2,1,0:T(8,128)(2,1)}, u32[]{:S(2)}) copy-start(bf16[4,16,128,256]{3,2,1,0:T(8,128)(2,1)} %get-tuple-element.28.refs_4_.chosen_ref) | copy-start | bytes 12582916
  22.2 1.3 %copy-start.2 = (bf16[4,768,128]{2,1,0:T(8,128)(2,1)S(1)}, bf16[4,768,128]{2,1,0:T(8,128)(2,1)}, u32[]{:S(2)}) copy-start(bf16[4,768,128]{2,1,0:T(8,128)(2,1)} %get-tuple-element.26.unit_ref.refs_2_) | copy-start | bytes 2359300
  23.5 27.3 %copy-start.1 = (bf16[8,32,1536]{2,1,0:T(8,128)(2,1)S(1)}, bf16[8,32,1536]{2,1,0:T(8,128)(2,1)}, u32[]{:S(2)}) copy-start(bf16[8,32,1536]{2,1,0:T(8,128)(2,1)} %param.5) | copy-start | bytes 2359300
  23.5 27.3 %copy-start.3 = (f32[128,256]{1,0:T(8,128)S(1)}, f32[128,256]{1,0:T(8,128)}, u32[]{:S(2)}) copy-start(f32[128,256]{1,0:T(8,128)} %get-tuple-element.38.refs_10_) | copy-start | bytes 393220
  23.5 27.3 %copy-start.4 = (f32[4,128,768]{2,1,0:T(8,128)S(1)}, f32[4,128,768]{2,1,0:T(8,128)}, u32[]{:S(2)}) copy-start(f32[4,128,768]{2,1,0:T(8,128)} %get-tuple-element.36.refs_8_) | copy-start | bytes 4718596
  23.5 27.3 %copy-start.5 = (s32[4,16,256]{2,1,0:T(8,128)S(1)}, s32[4,16,256]{2,1,0:T(8,128)}, u32[]{:S(2)}) copy-start(s32[4,16,256]{2,1,0:T(8,128)} %get-tuple-element.24.refs_1_) | copy-start | bytes 196612
  32.0 2.1 %collective-permute-start.1 = (bf16[8,144,256]{2,1,0:T(8,128)(2,1)S(1)}, bf16[8,144,256]{2,1,0:T(8,128)(2,1)S(1)}, u32[]{:S(2)}, u32[]{:S(2)}) collective-permute-start(bf16[8,144,256]{2,1,0:T(8,128)(2,1)S(1)} %get-tuple-element.32), channel_id=1, source_target_pairs={{0,1},{1,0},{2,3},{3,2},{4,5},{5,4},{6,7},{7,6},{8,9},{9,8},{10,11... | collective-permute-start | bytes 1769480 | tf_op jit(solution)/shard_map/ppermute | solution.py:284
  58.3 2.4 %collective-permute-start.2 = (f32[768,128]{1,0:T(8,128)S(1)}, f32[768,128]{1,0:T(8,128)S(1)}, u32[]{:S(2)}, u32[]{:S(2)}) collective-permute-start(f32[768,128]{1,0:T(8,128)S(1)} %get-tuple-element.40), channel_id=1, source_target_pairs={{0,1},{1,0},{2,3},{3,2},{4,5},{5,4},{6,7},{7,6},{8,9},{9,8},{10,11... | collective-permute-start | bytes 1179656 | tf_op jit(solution)/shard_map/ppermute | solution.py:284
  91.4 5.0 %collective-permute-start.3 = (bf16[768,128]{1,0:T(8,128)(2,1)S(1)}, bf16[768,128]{1,0:T(8,128)(2,1)S(1)}, u32[]{:S(2)}, u32[]{:S(2)}) collective-permute-start(bf16[768,128]{1,0:T(8,128)(2,1)S(1)} %bitcast.11), channel_id=1, source_target_pairs={{0,1},{1,0},{2,3},{3,2},{4,5},{5,4},{6,7},{7,6},{8,9},{9,8},{10,11... | collective-permute-start | bytes 589832 | tf_op jit(solution)/shard_map/ppermute | solution.py:284

commit v6 on v5

--- a/solution.py
+++ b/solution.py
@@ -53,8 +53,8 @@
         send_ref[block] = unit
 
 
-def page_kernel(length_any, hidden_any, weight_any, best_any, raw_any, unit_any, chosen_any, index_ref,
-                hidden, weight, best, length, turned, raw_ref, unit_ref, chosen_ref, arrived, left):
+def page_kernel(length_any, hidden_any, weight_any, best_any, raw_any, unit_any, chosen_any, index_any,
+                hidden, weight, best, length, turned, raw_ref, unit_ref, chosen_ref, index_ref, arrived, left, index_left):
     pages, slots, _ = hidden.shape
     dim, tiles = weight.shape[1], index_ref.shape[1]
     parts = slots // 256
@@ -67,6 +67,10 @@
     def page_copy(page):
         return pltpu.make_async_copy(hidden_any.at[page], hidden.at[page], arrived.at[page])
 
+    def first_copy(part):
+        some = pl.ds(part * slots // 2, slots // 2)
+        return pltpu.make_async_copy(hidden_any.at[0, some], hidden.at[0, some], arrived.at[pages + 2 + part if part else 0])
+
     def raw_copy(page):
         return pltpu.make_async_copy(raw_ref.at[page], raw_any.at[page], left.at[0, page])
 
@@ -77,9 +81,10 @@
         some = pl.ds(part * (tiles // 2), tiles // 2)
         return pltpu.make_async_copy(chosen_ref.at[page, some], chosen_any.at[page, some], left.at[2 + part, page])
 
-    page_copy(0).start()
+    first_copy(0).start()
     for copy in small:
         copy.start()
+    first_copy(1).start()
     page_copy(1).start()
     small[0].wait()
     for page in range(pages):
@@ -94,14 +99,22 @@
                     row = row + (pltpu.roll(piece, 32 * query, 1) if query else piece)
                 halves.append(row)
             index_ref[page, core * 8:core * 8 + 8, :] = jnp.concatenate(halves, axis=1).astype(jnp.int32)
+    index_copy = pltpu.make_async_copy(index_ref, index_any, index_left)
+    index_copy.start()
     small[1].wait()
     small[2].wait()
 
     def project(page):
-        page_copy(page).wait()
         if page + 2 < pages:
             page_copy(page + 2).start()
-        raw_ref[page] = jnp.dot(hidden[page], weight[...], preferred_element_type=F32).T
+        if page:
+            page_copy(page).wait()
+            raw_ref[page] = jnp.dot(hidden[page], weight[...], preferred_element_type=F32).T
+        else:
+            for part in range(2):
+                some = slice(part * slots // 2, (part + 1) * slots // 2)
+                first_copy(part).wait()
+                raw_ref[0, :, some] = jnp.dot(hidden[0, some], weight[...], preferred_element_type=F32).T
         raw_copy(page).start()
 
     project(0)
@@ -125,6 +138,7 @@
             chosen_ref[page, tile] = chosen.astype(BF16)
             if (tile + 1) % (tiles // 2) == 0:
                 chosen_copy(page, tile // (tiles // 2)).start()
+    index_copy.wait()
     for page in range(pages):
         raw_copy(page).wait()
         unit_copy(page).wait()
@@ -320,7 +334,7 @@
     page_raw, page_unit, chosen, index = pl.pallas_call(
         page_kernel,
         in_specs=[anywhere] * 4,
-        out_specs=[anywhere] * 3 + [inside],
+        out_specs=[anywhere] * 4,
         out_shape=(
             shape((pages, dim, slots), F32),
             shape((pages, slots, dim), BF16),
@@ -336,8 +350,10 @@
             pltpu.VMEM((pages, dim, slots), F32),
             pltpu.VMEM((pages, slots, dim), BF16),
             pltpu.VMEM((pages, tiles, dim, rows), BF16),
-            pltpu.SemaphoreType.DMA((pages + 3,)),
+            pltpu.VMEM((pages, tiles, rows), jnp.int32),
+            pltpu.SemaphoreType.DMA((pages + 4,)),
             pltpu.SemaphoreType.DMA((4, pages)),
+            pltpu.SemaphoreType.DMA,
         ],
         compiler_params=vmem(PAGE_MIB),
         cost_estimate=cost(2 * pages * slots * dim * (hidden_size + tiles * rows), 16 * MIB),

time: 97.8 us -> 96.5 us (0.987)
  Pallas kernels: 31.4 us -> 30.1 us
    pallas_call x1, Pallas kernels: 11.3 us -> 9.98 us  [per_device(): pl.pallas_call(page_kernel, in_specs=[anywhere] * 4, out_specs=[anywhere]...]
  transfers between devices with their start and end apart: 5 -> 5, of which waited for: 3 -> 4; matrix products, arithmetic and copies ran while one was open for 0% -> 0% of each run, Pallas kernels for 17% -> 15%
where the time goes in v6:
time: 96.5 us; the launch traced here: 96.1 us
  blocking collectives  46.6 us (48%)
  Pallas kernels  30.1 us (31%)
  starting transfers between devices  12.6 us (13%)
  waiting for transfers between devices  3.62 us (4%)
  local copies, waits for them, and re-layouts  1.36 us (1%)
  other arithmetic  1.15 us (1%)
    all_to_all x2, blocking collectives, to_all(): lax.all_to_all(jnp.broadcast_to(value[None], (lax.axis_size(axis),) + val...  22.1 us
    all_to_all x1, blocking collectives, per_device(): received = lax.all_to_all(send, 'chip', 0, 0, tiled=True)  16 us
    pallas_call x1, Pallas kernels, per_device(): pl.pallas_call(page_kernel, in_specs=[anywhere] * 4, out_specs=[anywhere]...  9.98 us
    all_to_all x1, blocking collectives, per_device(): lax.all_to_all(halves.reshape(chips, half // chips, dim), 'chip', 0, 0, t...  8.43 us
    pallas_call x1, Pallas kernels, per_device(): pl.pallas_call(lambda *refs: gradient_kernel(multiplier, *refs), in_specs...  7.48 us
    all_to_all x1, starting transfers between devices, per_device(): near = lax.all_to_all(query_send, 'chip', 0, 0, tiled=True)  6.39 us
    ppermute x4, starting transfers between devices, swap_cores(): return lax.ppermute(value, 'core', [(0, 1), (1, 0)])  6.17 us
    pallas_call x1, Pallas kernels, per_device(): pl.pallas_call(lambda *refs: far_kernel(multiplier, *refs), in_specs=[sme...  4.65 us
  transfers between devices with their start and end apart: 5, of which 4 were waited for; matrix products, arithmetic and copies ran while one was open for 0% of the time, Pallas kernels for 15%

profile of v6, /device:TPU:1, one launch (start us, length us, event | category | flops | bytes accessed | tf_op | source)
XLA Modules:
  0.0 96.1 jit_solution(13635204817140094186)
XLA Ops:
  0.6 2.6 %query_project.1 = (f32[128,256]{1,0:T(8,128)}, bf16[8,128,256]{2,1,0:T(8,128)(2,1)}) custom-call(bf16[256,1536]{1,0:T(8,128)(2,1)} %bitcast.9, bf16[1536,128]{1,0:T(8,128)(2,1)} %weight_any.3), custom_call_target="tpu_custom_call" | custom-call | flops 100663296 | bytes 2097152 | tf_op jit(solution)/shard_map/query_project/pallas_call | solution.py:323
  3.2 6.4 %all-to-all-start = ((bf16[8,128,256]{2,1,0:T(8,128)(2,1)}), bf16[8,128,256]{2,1,0:T(8,128)(2,1)S(1)}, u32[]{:S(2)}, u32[]{:S(2)}) async-start(bf16[8,128,256]{2,1,0:T(8,128)(2,1)} %get-tuple-element.22), calls=%async_computation | async-start | bytes 1048576 | tf_op jit(solution)/shard_map/all_to_all | solution.py:332
  9.6 10.0 %page_project.1 = (f32[4,128,768]{2,1,0:T(8,128)}, bf16[4,768,128]{2,1,0:T(8,128)(2,1)}, bf16[4,16,128,256]{3,2,1,0:T(8,128)(2,1)}, s32[4,16,256]{2,1,0:T(8,128)}) custom-call(s32[4]{0:T(128)} %length_any.1, bf16[4,768,1536]{2,1,0:T(8,128)(2,1)} %hidden_any.3, bf16[1536,128]{1,0:T(8,128)(2,1)} %weight_any.3, s32[32,4,128]{2,1,0:T(4,128)} %bitcast.13), custom_call_target="tpu_custom_call" | custom-call | flops 4429185024 | bytes 16777216 | tf_op jit(solution)/shard_map/page_project/pallas_call | solution.py:334
  19.6 0.2 all-to-all-done.query_ref.refs_6_
  19.8 1.0 %collective-permute-start = (bf16[8,128,256]{2,1,0:T(8,128)(2,1)S(1)}, bf16[8,128,256]{2,1,0:T(8,128)(2,1)S(1)}, u32[]{:S(2)}, u32[]{:S(2)}) collective-permute-start(bf16[8,128,256]{2,1,0:T(8,128)(2,1)S(1)} %all-to-all-done.query_ref.refs_6_), channel_id=1, source_target_pairs={{0,1},{1,0},{2,3},{3,2},{4,5},{5,4},{6,7},{7,6},{8,9},{9,8},{10,11... | collective-permute-start | bytes 1572872 | tf_op jit(solution)/shard_map/ppermute | solution.py:298
  20.8 0.0 copy-start
  20.8 0.1 pad_add_fusion.refs_0_.place_ref
  20.9 0.0 copy-start.2
  20.9 1.3 %copy-done.2 = bf16[4,768,128]{2,1,0:T(8,128)(2,1)S(1)} copy-done((bf16[4,768,128]{2,1,0:T(8,128)(2,1)S(1)}, bf16[4,768,128]{2,1,0:T(8,128)(2,1)}, u32[]{:S(2)}) %copy-start.2) | copy-done | bytes 786456
  22.2 0.0 copy-start.1
  22.2 0.0 copy-start.3
  22.2 0.0 copy-start.4
  22.2 0.0 copy-start.5
  22.2 3.8 %near_scores.1 = (f32[4,8,256]{2,1,0:T(8,128)S(1)}, bf16[4,768,1536]{2,1,0:T(8,128)(2,1)S(1)}) custom-call(bf16[8,128,256]{2,1,0:T(8,128)(2,1)S(1)} %all-to-all-done.query_ref.refs_6_, bf16[4,768,128]{2,1,0:T(8,128)(2,1)S(1)} %copy-done.2, bf16[4,768,1536]{2,1,0:T(8,128)(2,1)} %hidden_any.3), custom_call_target="tpu_custom_call" | custom-call | flops 1610612736 | bytes 2097152 | tf_op jit(solution)/shard_map/near_scores/pallas_call | solution.py:365
  26.0 0.0 collective-permute-done.refs_1_.refs_7_
  26.0 0.0 copy-done
  26.0 4.6 %far_scores.1 = (f32[4,16,256]{2,1,0:T(8,128)S(1)}, f32[16,128]{1,0:T(8,128)S(1)}, bf16[8,144,256]{2,1,0:T(8,128)(2,1)S(1)}) custom-call(s32[2]{0:T(128)S(1)} %pad_add_fusion.refs_0_.place_ref, bf16[8,128,256]{2,1,0:T(8,128)(2,1)S(1)} %collective-permute-done.refs_1_.refs_7_, bf16[4,768,128]{2,1,0:T(8,128)(2,1)S(1)} %copy-done.2, ...), custom_call_target="tpu_custom_call" | custom-call | flops 1610612736 | bytes 8388608 | tf_op jit(solution)/shard_map/far_scores/pallas_call | solution.py:374
  30.7 0.1 collective-permute-start.1
  30.8 1.0 %keep_terms.1 = (f32[8,128,256]{2,1,0:T(8,128)S(1)}, f32[128,256]{1,0:T(8,128)S(1)}) custom-call(s32[2]{0:T(128)S(1)} %pad_add_fusion.refs_0_.place_ref, f32[4,16,256]{2,1,0:T(8,128)S(1)} %get-tuple-element.29.expo_ref.refs_2_, bf16[4,16,128,256]{3,2,1,0:T(8,128)(2,1)S(1)} %copy-done), custom_call_target="tpu_custom_call" | custom-call | flops 4194304 | bytes 4194304 | tf_op jit(solution)/shard_map/keep_terms/pallas_call | solution.py:383
  31.8 1.0 %collective-permute-done.1.pair_ref = bf16[8,144,256]{2,1,0:T(8,128)(2,1)S(1)} collective-permute-done((bf16[8,144,256]{2,1,0:T(8,128)(2,1)S(1)}, bf16[8,144,256]{2,1,0:T(8,128)(2,1)S(1)}, u32[]{:S(2)}, u32[]{:S(2)}) %collective-permute-start.1) | collective-permute-done | bytes 589856 | tf_op jit(solution)/shard_map/ppermute | solution.py:298
  32.8 0.6 add_pair.1
  33.4 16.0 %all_to_all.25.refs_3_ = bf16[8,144,256]{2,1,0:T(8,128)(2,1)S(1)} all-to-all(bf16[8,144,256]{2,1,0:T(8,128)(2,1)S(1)} %get-tuple-element.33), channel_id=1, replica_groups=mesh['dp'=8,'chip'=8,'core'=2] {'chip'}, dimensions={0} | all-to-all | bytes 1179648 | tf_op jit(solution)/shard_map/all_to_all | solution.py:398
  49.4 0.0 copy-done.1
  49.5 0.0 copy-done.3
  49.5 0.0 copy-done.4
  49.5 0.0 copy-done.5
  49.5 7.5 %gradients.1 = (f32[768,128]{1,0:T(8,128)S(1)}, f32[768,128]{1,0:T(8,128)S(1)}, f32[256,128]{1,0:T(8,128)}) custom-call(s32[2]{0:T(128)S(1)} %pad_add_fusion.refs_0_.place_ref, s32[4,16,256]{2,1,0:T(8,128)S(1)} %copy-done.5, f32[4,16,256]{2,1,0:T(8,128)S(1)} %get-tuple-element.29.expo_ref.refs_2_, bf16[8,144,256]{2,1,0:T(8,128)(2,1)S(1)} %all_to_all.25.refs_3_, ...), custom_call_target="tpu_custom_call" | custom-call | flops 4429185024 | bytes 16777216 | tf_op jit(solution)/shard_map/gradients/pallas_call | solution.py:401
  57.0 1.1 %collective-permute-start.2 = (f32[768,128]{1,0:T(8,128)S(1)}, f32[768,128]{1,0:T(8,128)S(1)}, u32[]{:S(2)}, u32[]{:S(2)}) collective-permute-start(f32[768,128]{1,0:T(8,128)S(1)} %get-tuple-element.40), channel_id=1, source_target_pairs={{0,1},{1,0},{2,3},{3,2},{4,5},{5,4},{6,7},{7,6},{8,9},{9,8},{10,11... | collective-permute-start | bytes 1179656 | tf_op jit(solution)/shard_map/ppermute | solution.py:298
  58.0 1.3 %collective-permute-done.2 = f32[768,128]{1,0:T(8,128)S(1)} collective-permute-done((f32[768,128]{1,0:T(8,128)S(1)}, f32[768,128]{1,0:T(8,128)S(1)}, u32[]{:S(2)}, u32[]{:S(2)}) %collective-permute-start.2) | collective-permute-done | bytes 393248 | tf_op jit(solution)/shard_map/ppermute | solution.py:298
  59.4 8.4 %all_to_all.26 = bf16[8,96,128]{2,1,0:T(8,128)(2,1)S(1)} all-to-all(bf16[8,96,128]{2,1,0:T(8,128)(2,1)S(1)} %bitcast.12), channel_id=1, replica_groups=mesh['dp'=8,'chip'=8,'core'=2] {'chip'}, dimensions={0} | all-to-all | bytes 393216 | tf_op jit(solution)/shard_map/all_to_all | solution.py:418
  67.9 14.0 %all_to_all.27 = bf16[8,96,128]{2,1,0:T(8,128)(2,1)S(1)} all-to-all(bf16[8,96,128]{2,1,0:T(8,128)(2,1)S(1)} %broadcast_in_dim.4), channel_id=1, replica_groups=mesh['dp'=8,'chip'=8,'core'=2] {'dp'}, dimensions={0} | all-to-all | bytes 393216 | tf_op jit(solution)/shard_map/all_to_all | solution.py:306
  81.9 8.2 %all_to_all.28 = bf16[8,96,128]{2,1,0:T(8,128)(2,1)S(1)} all-to-all(bf16[8,96,128]{2,1,0:T(8,128)(2,1)S(1)} %broadcast_in_dim.5), channel_id=1, replica_groups=mesh['dp'=8,'chip'=8,'core'=2] {'chip'}, dimensions={0} | all-to-all | bytes 393216 | tf_op jit(solution)/shard_map/all_to_all | solution.py:306
  90.1 4.0 %collective-permute-start.3 = (bf16[768,128]{1,0:T(8,128)(2,1)S(1)}, bf16[768,128]{1,0:T(8,128)(2,1)S(1)}, u32[]{:S(2)}, u32[]{:S(2)}) collective-permute-start(bf16[768,128]{1,0:T(8,128)(2,1)S(1)} %bitcast.11), channel_id=1, source_target_pairs={{0,1},{1,0},{2,3},{3,2},{4,5},{5,4},{6,7},{7,6},{8,9},{9,8},{10,11... | collective-permute-start | bytes 589832 | tf_op jit(solution)/shard_map/ppermute | solution.py:298
  94.1 1.1 %collective-permute-done.3 = bf16[768,128]{1,0:T(8,128)(2,1)S(1)} collective-permute-done((bf16[768,128]{1,0:T(8,128)(2,1)S(1)}, bf16[768,128]{1,0:T(8,128)(2,1)S(1)}, u32[]{:S(2)}, u32[]{:S(2)}) %collective-permute-start.3) | collective-permute-done | bytes 196640 | tf_op jit(solution)/shard_map/ppermute | solution.py:298
  95.2 0.9 maximum_convert_fusion
  (6 shorter events, 0.2 us)
Async XLA Ops:
  3.2 16.6 %all-to-all-start = ((bf16[8,128,256]{2,1,0:T(8,128)(2,1)}), bf16[8,128,256]{2,1,0:T(8,128)(2,1)S(1)}, u32[]{:S(2)}, u32[]{:S(2)}) async-start(bf16[8,128,256]{2,1,0:T(8,128)(2,1)} %get-tuple-element.22), calls=%async_computation | async-start | bytes 1048576 | tf_op jit(solution)/shard_map/all_to_all | solution.py:332
  19.8 6.2 %collective-permute-start = (bf16[8,128,256]{2,1,0:T(8,128)(2,1)S(1)}, bf16[8,128,256]{2,1,0:T(8,128)(2,1)S(1)}, u32[]{:S(2)}, u32[]{:S(2)}) collective-permute-start(bf16[8,128,256]{2,1,0:T(8,128)(2,1)S(1)} %all-to-all-done.query_ref.refs_6_), channel_id=1, source_target_pairs={{0,1},{1,0},{2,3},{3,2},{4,5},{5,4},{6,7},{7,6},{8,9},{9,8},{10,11... | collective-permute-start | bytes 1572872 | tf_op jit(solution)/shard_map/ppermute | solution.py:298
  20.8 5.2 %copy-start = (bf16[4,16,128,256]{3,2,1,0:T(8,128)(2,1)S(1)}, bf16[4,16,128,256]{3,2,1,0:T(8,128)(2,1)}, u32[]{:S(2)}) copy-start(bf16[4,16,128,256]{3,2,1,0:T(8,128)(2,1)} %get-tuple-element.28.refs_4_.chosen_ref) | copy-start | bytes 12582916
  20.9 1.3 %copy-start.2 = (bf16[4,768,128]{2,1,0:T(8,128)(2,1)S(1)}, bf16[4,768,128]{2,1,0:T(8,128)(2,1)}, u32[]{:S(2)}) copy-start(bf16[4,768,128]{2,1,0:T(8,128)(2,1)} %get-tuple-element.26.unit_ref.refs_2_) | copy-start | bytes 2359300
  22.2 27.3 %copy-start.1 = (bf16[8,32,1536]{2,1,0:T(8,128)(2,1)S(1)}, bf16[8,32,1536]{2,1,0:T(8,128)(2,1)}, u32[]{:S(2)}) copy-start(bf16[8,32,1536]{2,1,0:T(8,128)(2,1)} %param.5) | copy-start | bytes 2359300
  22.2 27.3 %copy-start.3 = (f32[128,256]{1,0:T(8,128)S(1)}, f32[128,256]{1,0:T(8,128)}, u32[]{:S(2)}) copy-start(f32[128,256]{1,0:T(8,128)} %get-tuple-element.38.refs_10_) | copy-start | bytes 393220
  22.2 27.3 %copy-start.4 = (f32[4,128,768]{2,1,0:T(8,128)S(1)}, f32[4,128,768]{2,1,0:T(8,128)}, u32[]{:S(2)}) copy-start(f32[4,128,768]{2,1,0:T(8,128)} %get-tuple-element.36.refs_8_) | copy-start | bytes 4718596
  22.2 27.3 %copy-start.5 = (s32[4,16,256]{2,1,0:T(8,128)S(1)}, s32[4,16,256]{2,1,0:T(8,128)}, u32[]{:S(2)}) copy-start(s32[4,16,256]{2,1,0:T(8,128)} %get-tuple-element.24.refs_1_) | copy-start | bytes 196612
  30.7 2.1 %collective-permute-start.1 = (bf16[8,144,256]{2,1,0:T(8,128)(2,1)S(1)}, bf16[8,144,256]{2,1,0:T(8,128)(2,1)S(1)}, u32[]{:S(2)}, u32[]{:S(2)}) collective-permute-start(bf16[8,144,256]{2,1,0:T(8,128)(2,1)S(1)} %get-tuple-element.32), channel_id=1, source_target_pairs={{0,1},{1,0},{2,3},{3,2},{4,5},{5,4},{6,7},{7,6},{8,9},{9,8},{10,11... | collective-permute-start | bytes 1769480 | tf_op jit(solution)/shard_map/ppermute | solution.py:298
  57.0 2.4 %collective-permute-start.2 = (f32[768,128]{1,0:T(8,128)S(1)}, f32[768,128]{1,0:T(8,128)S(1)}, u32[]{:S(2)}, u32[]{:S(2)}) collective-permute-start(f32[768,128]{1,0:T(8,128)S(1)} %get-tuple-element.40), channel_id=1, source_target_pairs={{0,1},{1,0},{2,3},{3,2},{4,5},{5,4},{6,7},{7,6},{8,9},{9,8},{10,11... | collective-permute-start | bytes 1179656 | tf_op jit(solution)/shard_map/ppermute | solution.py:298
  90.1 5.0 %collective-permute-start.3 = (bf16[768,128]{1,0:T(8,128)(2,1)S(1)}, bf16[768,128]{1,0:T(8,128)(2,1)S(1)}, u32[]{:S(2)}, u32[]{:S(2)}) collective-permute-start(bf16[768,128]{1,0:T(8,128)(2,1)S(1)} %bitcast.11), channel_id=1, source_target_pairs={{0,1},{1,0},{2,3},{3,2},{4,5},{5,4},{6,7},{7,6},{8,9},{9,8},{10,11... | collective-permute-start | bytes 589832 | tf_op jit(solution)/shard_map/ppermute | solution.py:298

commit v7 on v6

--- a/solution.py
+++ b/solution.py
@@ -235,8 +235,8 @@
 
 
 def gradient_kernel(multiplier, place_ref, index_ref, expo_ref, received_ref, own_ref, target_ref, near_ref, far_ref, page_raw,
-                    hidden, query_raw_ref, query_hidden, keep_ref, give_ref, query_grad_ref, inverse_total, score_grad, summed_grad,
-                    accumulated, turned):
+                    hidden, query_raw_ref, query_hidden, give_ref, query_grad_ref, page_direction_ref, query_direction_ref,
+                    inverse_total, score_grad, summed_grad):
     core, chip = place_ref[0], place_ref[1]
     chips, dim, lanes = near_ref.shape
     tiles = 2 * chips
@@ -250,7 +250,8 @@
     first = iota((tiles, 128), 1) % 32 < 16
     inverse_total[:, 0:128] = jnp.where(first, inverse, pltpu.roll(inverse, 16, 1))
     inverse_total[:, 128:256] = jnp.where(first, pltpu.roll(inverse, 112, 1), inverse)
-    accumulated[...] = jnp.zeros_like(accumulated)
+    half = give_ref.shape[0]
+    columns = pl.ds(pl.multiple_of((1 - core) * half, half), half)
 
     def scattered(page, tile, weighted):
         index = index_ref[page, pl.ds(tile, 1), :]
@@ -269,17 +270,27 @@
                 summed_grad[...] += scattered(page, tile, queries_ref[chip_of].astype(F32) * score_grad[pl.ds(tile, 1), :])
         grad = jnp.concatenate([summed_grad[part * dim:(part + 1) * dim] for part in range(parts)], axis=1)
         direction = unit_backward(grad, page_raw[page]).astype(BF16)
-        accumulated[...] += jnp.dot(direction, hidden[page], preferred_element_type=F32)
+        page_direction_ref[page] = direction
     summed = own_ref[...]
     for source in range(chips):
         summed = summed + jnp.where(chip == source, 0.0, received_ref[source, 0:dim, :].astype(F32))
     query_grad = (summed * inverse_total[pl.ds(mine, 1), :] - target_ref[...]) * multiplier
     query_grad_ref[...] = query_grad.T
     direction = unit_backward(query_grad, query_raw_ref[...]).astype(BF16)
-    turned[...] = (accumulated[...] + jnp.dot(direction, query_hidden[...], preferred_element_type=F32)).T
+    query_direction_ref[...] = direction
+    grad = jnp.dot(direction, query_hidden[:, columns], preferred_element_type=F32)
+    for page in range(pages):
+        grad = grad + jnp.dot(page_direction_ref[page], hidden[page, :, columns], preferred_element_type=F32)
+    give_ref[...] = grad.T
+
+
+def weight_keep_kernel(place_ref, page_direction_ref, query_direction_ref, hidden, query_hidden, keep_ref):
     half = keep_ref.shape[0]
-    keep_ref[...] = turned[pl.ds(pl.multiple_of(core * half, half), half), :]
-    give_ref[...] = turned[pl.ds(pl.multiple_of((1 - core) * half, half), half), :]
+    columns = pl.ds(pl.multiple_of(place_ref[0] * half, half), half)
+    grad = jnp.dot(query_direction_ref[...], query_hidden[:, columns], preferred_element_type=F32)
+    for page in range(hidden.shape[0]):
+        grad = grad + jnp.dot(page_direction_ref[page], hidden[page, :, columns], preferred_element_type=F32)
+    keep_ref[...] = grad.T
 
 
 def shape(dims, kind):
@@ -398,21 +409,33 @@
     received = lax.all_to_all(send, "chip", 0, 0, tiled=True)
 
     half = hidden_size // cores
-    weight_keep, weight_give, query_grad = pl.pallas_call(
+    weight_give, query_grad, page_direction, query_direction = pl.pallas_call(
         lambda *refs: gradient_kernel(multiplier, *refs),
         in_specs=[smem] + [inside] * 11,
-        out_shape=(shape((half, dim), F32), shape((half, dim), F32), shape((rows, dim), F32)),
+        out_shape=(
+            shape((half, dim), F32),
+            shape((rows, dim), F32),
+            shape((pages, dim, slots), BF16),
+            shape((dim, rows), BF16),
+        ),
         scratch_shapes=[
             pltpu.VMEM((tiles, rows), F32),
             pltpu.VMEM((tiles, rows), F32),
             pltpu.VMEM((slots // 256 * dim, 256), F32),
-            pltpu.VMEM((dim, hidden_size), F32),
-            pltpu.VMEM((hidden_size, dim), F32),
         ],
         compiler_params=vmem(GRADIENT_MIB),
         cost_estimate=cost(2 * pages * slots * dim * (hidden_size + tiles * rows), 16 * MIB),
         name="gradients",
     )(place, index, expo, received, own, target, near, far, page_raw, page_hidden, query_raw, query_rows)
+
+    weight_keep = pl.pallas_call(
+        weight_keep_kernel,
+        in_specs=[smem] + [inside] * 4,
+        out_shape=shape((half, dim), F32),
+        compiler_params=vmem(GRADIENT_MIB),
+        cost_estimate=cost(pages * slots * dim * hidden_size, 6 * MIB),
+        name="weight_keep",
+    )(place, page_direction, query_direction, page_hidden, query_rows)
 
     halves = (weight_keep + swap_cores(weight_give)).astype(BF16)
     chunk = summed(lax.all_to_all(halves.reshape(chips, half // chips, dim), "chip", 0, 0, tiled=True))

time: 96.5 us -> 94.9 us (0.983)
  waiting for transfers between devices: 3.62 us -> 2.27 us
    pallas_call x1, Pallas kernels: 7.48 us -> 5.86 us  [per_device(): pl.pallas_call(lambda *refs: gradient_kernel(multiplier, *refs), in_specs...]
    pallas_call x0 -> x1, Pallas kernels: none -> 1.47 us  [per_device(): pl.pallas_call(weight_keep_kernel, in_specs=[smem] + [inside] * 4, out_sh...]
    ppermute x4, waiting for transfers between devices: 3.41 us -> 2.07 us  [swap_cores(): return lax.ppermute(value, 'core', [(0, 1), (1, 0)])]
  transfers between devices with their start and end apart: 5 -> 5, of which waited for: 4 -> 3; matrix products, arithmetic and copies ran while one was open for 0% -> 0% of each run, Pallas kernels for 15% -> 17%
where the time goes in v7:
time: 94.9 us; the launch traced here: 94.6 us
  blocking collectives  47 us (50%)
  Pallas kernels  30 us (32%)
  starting transfers between devices  12 us (13%)
  waiting for transfers between devices  2.27 us (2%)
  local copies, waits for them, and re-layouts  1.36 us (1%)
  other arithmetic  1.17 us (1%)
    all_to_all x2, blocking collectives, to_all(): lax.all_to_all(jnp.broadcast_to(value[None], (lax.axis_size(axis),) + val...  22.1 us
    all_to_all x1, blocking collectives, per_device(): received = lax.all_to_all(send, 'chip', 0, 0, tiled=True)  16 us
    pallas_call x1, Pallas kernels, per_device(): pl.pallas_call(page_kernel, in_specs=[anywhere] * 4, out_specs=[anywhere]...  9.98 us
    all_to_all x1, blocking collectives, per_device(): lax.all_to_all(halves.reshape(chips, half // chips, dim), 'chip', 0, 0, t...  8.93 us
    all_to_all x1, starting transfers between devices, per_device(): near = lax.all_to_all(query_send, 'chip', 0, 0, tiled=True)  6.39 us
    pallas_call x1, Pallas kernels, per_device(): pl.pallas_call(lambda *refs: gradient_kernel(multiplier, *refs), in_specs...  5.86 us
    ppermute x4, starting transfers between devices, swap_cores(): return lax.ppermute(value, 'core', [(0, 1), (1, 0)])  5.65 us
    pallas_call x1, Pallas kernels, per_device(): pl.pallas_call(lambda *refs: far_kernel(multiplier, *refs), in_specs=[sme...  4.65 us
  transfers between devices with their start and end apart: 5, of which 3 were waited for; matrix products, arithmetic and copies ran while one was open for 0% of the time, Pallas kernels for 17%

profile of v7, /device:TPU:1, one launch (start us, length us, event | category | flops | bytes accessed | tf_op | source)
XLA Modules:
  0.0 94.6 jit_solution(2961633484468936996)
XLA Ops:
  0.6 2.6 %query_project.1 = (f32[128,256]{1,0:T(8,128)}, bf16[8,128,256]{2,1,0:T(8,128)(2,1)}) custom-call(bf16[256,1536]{1,0:T(8,128)(2,1)} %bitcast.9, bf16[1536,128]{1,0:T(8,128)(2,1)} %weight_any.3), custom_call_target="tpu_custom_call" | custom-call | flops 100663296 | bytes 2097152 | tf_op jit(solution)/shard_map/query_project/pallas_call | solution.py:334
  3.2 6.4 %all-to-all-start = ((bf16[8,128,256]{2,1,0:T(8,128)(2,1)}), bf16[8,128,256]{2,1,0:T(8,128)(2,1)S(1)}, u32[]{:S(2)}, u32[]{:S(2)}) async-start(bf16[8,128,256]{2,1,0:T(8,128)(2,1)} %get-tuple-element.23), calls=%async_computation | async-start | bytes 1048576 | tf_op jit(solution)/shard_map/all_to_all | solution.py:343
  9.6 10.0 %page_project.1 = (f32[4,128,768]{2,1,0:T(8,128)}, bf16[4,768,128]{2,1,0:T(8,128)(2,1)}, bf16[4,16,128,256]{3,2,1,0:T(8,128)(2,1)}, s32[4,16,256]{2,1,0:T(8,128)}) custom-call(s32[4]{0:T(128)} %length_any.1, bf16[4,768,1536]{2,1,0:T(8,128)(2,1)} %hidden_any.3, bf16[1536,128]{1,0:T(8,128)(2,1)} %weight_any.3, s32[32,4,128]{2,1,0:T(4,128)} %bitcast.14), custom_call_target="tpu_custom_call" | custom-call | flops 4429185024 | bytes 16777216 | tf_op jit(solution)/shard_map/page_project/pallas_call | solution.py:345
  19.6 0.2 all-to-all-done.query_ref.refs_6_
  19.8 1.0 %collective-permute-start = (bf16[8,128,256]{2,1,0:T(8,128)(2,1)S(1)}, bf16[8,128,256]{2,1,0:T(8,128)(2,1)S(1)}, u32[]{:S(2)}, u32[]{:S(2)}) collective-permute-start(bf16[8,128,256]{2,1,0:T(8,128)(2,1)S(1)} %all-to-all-done.query_ref.refs_6_), channel_id=1, source_target_pairs={{0,1},{1,0},{2,3},{3,2},{4,5},{5,4},{6,7},{7,6},{8,9},{9,8},{10,11... | collective-permute-start | bytes 1572872 | tf_op jit(solution)/shard_map/ppermute | solution.py:309
  20.8 0.0 copy-start
  20.8 0.1 pad_add_fusion.refs_0_.place_ref
  20.9 0.0 copy-start.2
  20.9 1.3 %copy-done.2 = bf16[4,768,128]{2,1,0:T(8,128)(2,1)S(1)} copy-done((bf16[4,768,128]{2,1,0:T(8,128)(2,1)S(1)}, bf16[4,768,128]{2,1,0:T(8,128)(2,1)}, u32[]{:S(2)}) %copy-start.2) | copy-done | bytes 786456
  22.2 0.0 copy-start.1
  22.2 0.0 copy-start.3
  22.2 0.0 copy-start.4
  22.2 0.0 copy-start.5
  22.2 3.8 %near_scores.1 = (f32[4,8,256]{2,1,0:T(8,128)S(1)}, bf16[4,768,1536]{2,1,0:T(8,128)(2,1)S(1)}) custom-call(bf16[8,128,256]{2,1,0:T(8,128)(2,1)S(1)} %all-to-all-done.query_ref.refs_6_, bf16[4,768,128]{2,1,0:T(8,128)(2,1)S(1)} %copy-done.2, bf16[4,768,1536]{2,1,0:T(8,128)(2,1)} %hidden_any.3), custom_call_target="tpu_custom_call" | custom-call | flops 1610612736 | bytes 2097152 | tf_op jit(solution)/shard_map/near_scores/pallas_call | solution.py:376
  26.0 0.0 collective-permute-done.refs_1_.refs_7_
  26.0 0.0 copy-done
  26.0 4.6 %far_scores.1 = (f32[4,16,256]{2,1,0:T(8,128)S(1)}, f32[16,128]{1,0:T(8,128)S(1)}, bf16[8,144,256]{2,1,0:T(8,128)(2,1)S(1)}) custom-call(s32[2]{0:T(128)S(1)} %pad_add_fusion.refs_0_.place_ref, bf16[8,128,256]{2,1,0:T(8,128)(2,1)S(1)} %collective-permute-done.refs_1_.refs_7_, bf16[4,768,128]{2,1,0:T(8,128)(2,1)S(1)} %copy-done.2, ...), custom_call_target="tpu_custom_call" | custom-call | flops 1610612736 | bytes 8388608 | tf_op jit(solution)/shard_map/far_scores/pallas_call | solution.py:385
  30.7 0.1 collective-permute-start.1
  30.8 1.0 %keep_terms.1 = (f32[8,128,256]{2,1,0:T(8,128)S(1)}, f32[128,256]{1,0:T(8,128)S(1)}) custom-call(s32[2]{0:T(128)S(1)} %pad_add_fusion.refs_0_.place_ref, f32[4,16,256]{2,1,0:T(8,128)S(1)} %get-tuple-element.30.expo_ref.refs_2_, bf16[4,16,128,256]{3,2,1,0:T(8,128)(2,1)S(1)} %copy-done), custom_call_target="tpu_custom_call" | custom-call | flops 4194304 | bytes 4194304 | tf_op jit(solution)/shard_map/keep_terms/pallas_call | solution.py:394
  31.8 1.0 %collective-permute-done.1.pair_ref = bf16[8,144,256]{2,1,0:T(8,128)(2,1)S(1)} collective-permute-done((bf16[8,144,256]{2,1,0:T(8,128)(2,1)S(1)}, bf16[8,144,256]{2,1,0:T(8,128)(2,1)S(1)}, u32[]{:S(2)}, u32[]{:S(2)}) %collective-permute-start.1) | collective-permute-done | bytes 589856 | tf_op jit(solution)/shard_map/ppermute | solution.py:309
  32.8 0.6 add_pair.1
  33.4 16.0 %all_to_all.25.refs_3_ = bf16[8,144,256]{2,1,0:T(8,128)(2,1)S(1)} all-to-all(bf16[8,144,256]{2,1,0:T(8,128)(2,1)S(1)} %get-tuple-element.34), channel_id=1, replica_groups=mesh['dp'=8,'chip'=8,'core'=2] {'chip'}, dimensions={0} | all-to-all | bytes 1179648 | tf_op jit(solution)/shard_map/all_to_all | solution.py:409
  49.4 0.0 copy-done.1
  49.5 0.0 copy-done.3
  49.5 0.0 copy-done.4
  49.5 0.0 copy-done.5
  49.5 5.9 %gradients.1 = (f32[768,128]{1,0:T(8,128)S(1)}, f32[256,128]{1,0:T(8,128)}, bf16[4,128,768]{2,1,0:T(8,128)(2,1)S(1)}, bf16[128,256]{1,0:T(8,128)(2,1)S(1)}) custom-call(s32[2]{0:T(128)S(1)} %pad_add_fusion.refs_0_.place_ref, s32[4,16,256]{2,1,0:T(8,128)S(1)} %copy-done.5, f32[4,16,256]{2,1,0:T(8,128)S(1)} %get-tuple-element.30.expo_ref.refs_2_, ...), custom_call_target="tpu_custom_call" | custom-call | flops 4429185024 | bytes 16777216 | tf_op jit(solution)/shard_map/gradients/pallas_call | solution.py:412
  55.3 1.0 %collective-permute-start.2 = (f32[768,128]{1,0:T(8,128)S(1)}, f32[768,128]{1,0:T(8,128)S(1)}, u32[]{:S(2)}, u32[]{:S(2)}) collective-permute-start(f32[768,128]{1,0:T(8,128)S(1)} %get-tuple-element.42), channel_id=1, source_target_pairs={{0,1},{1,0},{2,3},{3,2},{4,5},{5,4},{6,7},{7,6},{8,9},{9,8},{10,11... | collective-permute-start | bytes 1179656 | tf_op jit(solution)/shard_map/ppermute | solution.py:309
  56.3 1.5 %weight_keep.1 = f32[768,128]{1,0:T(8,128)S(1)} custom-call(s32[2]{0:T(128)S(1)} %pad_add_fusion.refs_0_.place_ref, bf16[4,128,768]{2,1,0:T(8,128)(2,1)S(1)} %get-tuple-element.40.page_direction_ref, bf16[128,256]{1,0:T(8,128)(2,1)S(1)} %get-tuple-element.41.query_direction_ref, bf16[4,768,1536]{2,1,0:T(8,128)(2,1)S(1)} %get-tuple-element.38.refs_9_.hidden, ...), custom_call_target="tpu_custom_call" | custom-call | flops 603979776 | bytes 6291456 | tf_op jit(solution)/shard_map/weight_keep/pallas_call | solution.py:431
  57.8 0.0 collective-permute-done.2
  57.8 0.1 add_convert_fusion
  57.8 8.9 %all_to_all.26 = bf16[8,96,128]{2,1,0:T(8,128)(2,1)S(1)} all-to-all(bf16[8,96,128]{2,1,0:T(8,128)(2,1)S(1)} %bitcast.13), channel_id=1, replica_groups=mesh['dp'=8,'chip'=8,'core'=2] {'chip'}, dimensions={0} | all-to-all | bytes 393216 | tf_op jit(solution)/shard_map/all_to_all | solution.py:441
  66.8 13.9 %all_to_all.27 = bf16[8,96,128]{2,1,0:T(8,128)(2,1)S(1)} all-to-all(bf16[8,96,128]{2,1,0:T(8,128)(2,1)S(1)} %broadcast_in_dim.4), channel_id=1, replica_groups=mesh['dp'=8,'chip'=8,'core'=2] {'dp'}, dimensions={0} | all-to-all | bytes 393216 | tf_op jit(solution)/shard_map/all_to_all | solution.py:317
  80.8 8.2 %all_to_all.28 = bf16[8,96,128]{2,1,0:T(8,128)(2,1)S(1)} all-to-all(bf16[8,96,128]{2,1,0:T(8,128)(2,1)S(1)} %broadcast_in_dim.5), channel_id=1, replica_groups=mesh['dp'=8,'chip'=8,'core'=2] {'chip'}, dimensions={0} | all-to-all | bytes 393216 | tf_op jit(solution)/shard_map/all_to_all | solution.py:317
  89.0 3.5 %collective-permute-start.3 = (bf16[768,128]{1,0:T(8,128)(2,1)S(1)}, bf16[768,128]{1,0:T(8,128)(2,1)S(1)}, u32[]{:S(2)}, u32[]{:S(2)}) collective-permute-start(bf16[768,128]{1,0:T(8,128)(2,1)S(1)} %bitcast.12), channel_id=1, source_target_pairs={{0,1},{1,0},{2,3},{3,2},{4,5},{5,4},{6,7},{7,6},{8,9},{9,8},{10,11... | collective-permute-start | bytes 589832 | tf_op jit(solution)/shard_map/ppermute | solution.py:309
  92.5 1.1 %collective-permute-done.3 = bf16[768,128]{1,0:T(8,128)(2,1)S(1)} collective-permute-done((bf16[768,128]{1,0:T(8,128)(2,1)S(1)}, bf16[768,128]{1,0:T(8,128)(2,1)S(1)}, u32[]{:S(2)}, u32[]{:S(2)}) %collective-permute-start.3) | collective-permute-done | bytes 196640 | tf_op jit(solution)/shard_map/ppermute | solution.py:309
  93.7 0.9 maximum_convert_fusion
  (5 shorter events, 0.2 us)
Async XLA Ops:
  3.2 16.6 %all-to-all-start = ((bf16[8,128,256]{2,1,0:T(8,128)(2,1)}), bf16[8,128,256]{2,1,0:T(8,128)(2,1)S(1)}, u32[]{:S(2)}, u32[]{:S(2)}) async-start(bf16[8,128,256]{2,1,0:T(8,128)(2,1)} %get-tuple-element.23), calls=%async_computation | async-start | bytes 1048576 | tf_op jit(solution)/shard_map/all_to_all | solution.py:343
  19.8 6.2 %collective-permute-start = (bf16[8,128,256]{2,1,0:T(8,128)(2,1)S(1)}, bf16[8,128,256]{2,1,0:T(8,128)(2,1)S(1)}, u32[]{:S(2)}, u32[]{:S(2)}) collective-permute-start(bf16[8,128,256]{2,1,0:T(8,128)(2,1)S(1)} %all-to-all-done.query_ref.refs_6_), channel_id=1, source_target_pairs={{0,1},{1,0},{2,3},{3,2},{4,5},{5,4},{6,7},{7,6},{8,9},{9,8},{10,11... | collective-permute-start | bytes 1572872 | tf_op jit(solution)/shard_map/ppermute | solution.py:309
  20.8 5.2 %copy-start = (bf16[4,16,128,256]{3,2,1,0:T(8,128)(2,1)S(1)}, bf16[4,16,128,256]{3,2,1,0:T(8,128)(2,1)}, u32[]{:S(2)}) copy-start(bf16[4,16,128,256]{3,2,1,0:T(8,128)(2,1)} %get-tuple-element.29.refs_4_.chosen_ref) | copy-start | bytes 12582916
  20.9 1.3 %copy-start.2 = (bf16[4,768,128]{2,1,0:T(8,128)(2,1)S(1)}, bf16[4,768,128]{2,1,0:T(8,128)(2,1)}, u32[]{:S(2)}) copy-start(bf16[4,768,128]{2,1,0:T(8,128)(2,1)} %get-tuple-element.27.unit_ref.refs_2_) | copy-start | bytes 2359300
  22.2 27.3 %copy-start.1 = (bf16[8,32,1536]{2,1,0:T(8,128)(2,1)S(1)}, bf16[8,32,1536]{2,1,0:T(8,128)(2,1)}, u32[]{:S(2)}) copy-start(bf16[8,32,1536]{2,1,0:T(8,128)(2,1)} %param.5) | copy-start | bytes 2359300
  22.2 27.3 %copy-start.3 = (f32[128,256]{1,0:T(8,128)S(1)}, f32[128,256]{1,0:T(8,128)}, u32[]{:S(2)}) copy-start(f32[128,256]{1,0:T(8,128)} %get-tuple-element.39.refs_10_) | copy-start | bytes 393220
  22.2 27.3 %copy-start.4 = (f32[4,128,768]{2,1,0:T(8,128)S(1)}, f32[4,128,768]{2,1,0:T(8,128)}, u32[]{:S(2)}) copy-start(f32[4,128,768]{2,1,0:T(8,128)} %get-tuple-element.37.refs_8_) | copy-start | bytes 4718596
  22.2 27.3 %copy-start.5 = (s32[4,16,256]{2,1,0:T(8,128)S(1)}, s32[4,16,256]{2,1,0:T(8,128)}, u32[]{:S(2)}) copy-start(s32[4,16,256]{2,1,0:T(8,128)} %get-tuple-element.25.refs_1_) | copy-start | bytes 196612
  30.7 2.1 %collective-permute-start.1 = (bf16[8,144,256]{2,1,0:T(8,128)(2,1)S(1)}, bf16[8,144,256]{2,1,0:T(8,128)(2,1)S(1)}, u32[]{:S(2)}, u32[]{:S(2)}) collective-permute-start(bf16[8,144,256]{2,1,0:T(8,128)(2,1)S(1)} %get-tuple-element.33), channel_id=1, source_target_pairs={{0,1},{1,0},{2,3},{3,2},{4,5},{5,4},{6,7},{7,6},{8,9},{9,8},{10,11... | collective-permute-start | bytes 1769480 | tf_op jit(solution)/shard_map/ppermute | solution.py:309
  55.3 2.4 %collective-permute-start.2 = (f32[768,128]{1,0:T(8,128)S(1)}, f32[768,128]{1,0:T(8,128)S(1)}, u32[]{:S(2)}, u32[]{:S(2)}) collective-permute-start(f32[768,128]{1,0:T(8,128)S(1)} %get-tuple-element.42), channel_id=1, source_target_pairs={{0,1},{1,0},{2,3},{3,2},{4,5},{5,4},{6,7},{7,6},{8,9},{9,8},{10,11... | collective-permute-start | bytes 1179656 | tf_op jit(solution)/shard_map/ppermute | solution.py:309
  89.0 4.6 %collective-permute-start.3 = (bf16[768,128]{1,0:T(8,128)(2,1)S(1)}, bf16[768,128]{1,0:T(8,128)(2,1)S(1)}, u32[]{:S(2)}, u32[]{:S(2)}) collective-permute-start(bf16[768,128]{1,0:T(8,128)(2,1)S(1)} %bitcast.12), channel_id=1, source_target_pairs={{0,1},{1,0},{2,3},{3,2},{4,5},{5,4},{6,7},{7,6},{8,9},{9,8},{10,11... | collective-permute-start | bytes 589832 | tf_op jit(solution)/shard_map/ppermute | solution.py:309

commit v8 on v7

--- a/solution.py
+++ b/solution.py
@@ -162,6 +162,19 @@
     hidden_copy.wait()
 
 
+def split_total(total):
+    high = total.astype(BF16)
+    rest = total - high.astype(F32)
+    middle = rest.astype(BF16).astype(F32)
+    return high, jnp.where(iota(total.shape, 1) % 16 < 8, middle, rest - middle).astype(BF16)
+
+
+def joined_total(high, small):
+    small = small.astype(F32)
+    other = jnp.where(iota(small.shape, 1) % 16 < 8, pltpu.roll(small, 120, 1), pltpu.roll(small, 8, 1))
+    return high.astype(F32) + (small + other)
+
+
 def mixed(expo_ref, chosen_ref, tile):
     result = expo_ref[0, pl.ds(tile, 1), :] * chosen_ref[0, tile].astype(F32)
     for page in range(1, expo_ref.shape[0]):
@@ -193,8 +206,7 @@
     total = jnp.sum(expo, axis=0)
     total = jnp.where(iota((2 * chips, 128), 1) % 32 < 16, total[:, :128], total[:, 128:])
     total_ref[...] = total
-    high = total.astype(BF16)
-    low = (total - high.astype(F32)).astype(BF16)
+    high, low = split_total(total)
 
     def one_mix(tile, carry):
         pair_ref[tile, 0:dim, :] = mixed(expo_ref, chosen_ref, far + tile).astype(BF16)
@@ -223,9 +235,8 @@
 
 def add_kernel(place_ref, keep_ref, total_ref, pair_ref, send_ref, own_ref):
     chips, dim, _ = keep_ref.shape
-    total = total_ref[...] + (pair_ref[0, dim:dim + 16, 0:128].astype(F32) + pair_ref[0, dim:dim + 16, 128:256].astype(F32))
-    high = total.astype(BF16)
-    low = (total - high.astype(F32)).astype(BF16)
+    total = total_ref[...] + joined_total(pair_ref[0, dim:dim + 16, 0:128], pair_ref[0, dim:dim + 16, 128:256])
+    high, low = split_total(total)
     for tile in range(chips):
         send_ref[tile, 0:dim, :] = (keep_ref[tile] + pair_ref[tile, 0:dim, :].astype(F32)).astype(BF16)
         send_ref[tile, dim:dim + 16, 0:128] = high
@@ -245,7 +256,7 @@
     parts = slots // 256
     total = jnp.zeros((tiles, 128), F32)
     for source in range(chips):
-        total = total + received_ref[source, dim:dim + 16, 0:128].astype(F32) + received_ref[source, dim:dim + 16, 128:256].astype(F32)
+        total = total + joined_total(received_ref[source, dim:dim + 16, 0:128], received_ref[source, dim:dim + 16, 128:256])
     inverse = 1.0 / total
     first = iota((tiles, 128), 1) % 32 < 16
     inverse_total[:, 0:128] = jnp.where(first, inverse, pltpu.roll(inverse, 16, 1))

time: 94.9 us -> 95 us (level)
  no operation moved by 1% of the time
where the time goes in v8:
time: 95 us; the launch traced here: 94.7 us
  blocking collectives  47 us (49%)
  Pallas kernels  30 us (32%)
  starting transfers between devices  12 us (13%)
  waiting for transfers between devices  2.27 us (2%)
  local copies, waits for them, and re-layouts  1.36 us (1%)
  other arithmetic  1.17 us (1%)
    all_to_all x2, blocking collectives, to_all(): lax.all_to_all(jnp.broadcast_to(value[None], (lax.axis_size(axis),) + val...  22.1 us
    all_to_all x1, blocking collectives, per_device(): received = lax.all_to_all(send, 'chip', 0, 0, tiled=True)  16 us
    pallas_call x1, Pallas kernels, per_device(): pl.pallas_call(page_kernel, in_specs=[anywhere] * 4, out_specs=[anywhere]...  9.98 us
    all_to_all x1, blocking collectives, per_device(): lax.all_to_all(halves.reshape(chips, half // chips, dim), 'chip', 0, 0, t...  8.93 us
    all_to_all x1, starting transfers between devices, per_device(): near = lax.all_to_all(query_send, 'chip', 0, 0, tiled=True)  6.39 us
    pallas_call x1, Pallas kernels, per_device(): pl.pallas_call(lambda *refs: gradient_kernel(multiplier, *refs), in_specs...  5.92 us
    ppermute x4, starting transfers between devices, swap_cores(): return lax.ppermute(value, 'core', [(0, 1), (1, 0)])  5.66 us
    pallas_call x1, Pallas kernels, per_device(): pl.pallas_call(lambda *refs: far_kernel(multiplier, *refs), in_specs=[sme...  4.65 us
  transfers between devices with their start and end apart: 5, of which 3 were waited for; matrix products, arithmetic and copies ran while one was open for 0% of the time, Pallas kernels for 17%

profile of v8, /device:TPU:1, one launch (start us, length us, event | category | flops | bytes accessed | tf_op | source)
XLA Modules:
  0.0 94.7 jit_solution(4672862706290772789)
XLA Ops:
  0.6 2.6 %query_project.1 = (f32[128,256]{1,0:T(8,128)}, bf16[8,128,256]{2,1,0:T(8,128)(2,1)}) custom-call(bf16[256,1536]{1,0:T(8,128)(2,1)} %bitcast.9, bf16[1536,128]{1,0:T(8,128)(2,1)} %weight_any.3), custom_call_target="tpu_custom_call" | custom-call | flops 100663296 | bytes 2097152 | tf_op jit(solution)/shard_map/query_project/pallas_call | solution.py:345
  3.2 6.4 %all-to-all-start = ((bf16[8,128,256]{2,1,0:T(8,128)(2,1)}), bf16[8,128,256]{2,1,0:T(8,128)(2,1)S(1)}, u32[]{:S(2)}, u32[]{:S(2)}) async-start(bf16[8,128,256]{2,1,0:T(8,128)(2,1)} %get-tuple-element.23), calls=%async_computation | async-start | bytes 1048576 | tf_op jit(solution)/shard_map/all_to_all | solution.py:354
  9.6 10.0 %page_project.1 = (f32[4,128,768]{2,1,0:T(8,128)}, bf16[4,768,128]{2,1,0:T(8,128)(2,1)}, bf16[4,16,128,256]{3,2,1,0:T(8,128)(2,1)}, s32[4,16,256]{2,1,0:T(8,128)}) custom-call(s32[4]{0:T(128)} %length_any.1, bf16[4,768,1536]{2,1,0:T(8,128)(2,1)} %hidden_any.3, bf16[1536,128]{1,0:T(8,128)(2,1)} %weight_any.3, s32[32,4,128]{2,1,0:T(4,128)} %bitcast.14), custom_call_target="tpu_custom_call" | custom-call | flops 4429185024 | bytes 16777216 | tf_op jit(solution)/shard_map/page_project/pallas_call | solution.py:356
  19.6 0.2 all-to-all-done.query_ref.refs_6_
  19.8 1.0 %collective-permute-start = (bf16[8,128,256]{2,1,0:T(8,128)(2,1)S(1)}, bf16[8,128,256]{2,1,0:T(8,128)(2,1)S(1)}, u32[]{:S(2)}, u32[]{:S(2)}) collective-permute-start(bf16[8,128,256]{2,1,0:T(8,128)(2,1)S(1)} %all-to-all-done.query_ref.refs_6_), channel_id=1, source_target_pairs={{0,1},{1,0},{2,3},{3,2},{4,5},{5,4},{6,7},{7,6},{8,9},{9,8},{10,11... | collective-permute-start | bytes 1572872 | tf_op jit(solution)/shard_map/ppermute | solution.py:320
  20.8 0.0 copy-start
  20.8 0.1 pad_add_fusion.refs_0_.place_ref
  20.9 0.0 copy-start.2
  20.9 1.3 %copy-done.2 = bf16[4,768,128]{2,1,0:T(8,128)(2,1)S(1)} copy-done((bf16[4,768,128]{2,1,0:T(8,128)(2,1)S(1)}, bf16[4,768,128]{2,1,0:T(8,128)(2,1)}, u32[]{:S(2)}) %copy-start.2) | copy-done | bytes 786456
  22.2 0.0 copy-start.1
  22.2 0.0 copy-start.3
  22.2 0.0 copy-start.4
  22.2 0.0 copy-start.5
  22.2 3.8 %near_scores.1 = (f32[4,8,256]{2,1,0:T(8,128)S(1)}, bf16[4,768,1536]{2,1,0:T(8,128)(2,1)S(1)}) custom-call(bf16[8,128,256]{2,1,0:T(8,128)(2,1)S(1)} %all-to-all-done.query_ref.refs_6_, bf16[4,768,128]{2,1,0:T(8,128)(2,1)S(1)} %copy-done.2, bf16[4,768,1536]{2,1,0:T(8,128)(2,1)} %hidden_any.3), custom_call_target="tpu_custom_call" | custom-call | flops 1610612736 | bytes 2097152 | tf_op jit(solution)/shard_map/near_scores/pallas_call | solution.py:387
  26.0 0.0 collective-permute-done.refs_1_.refs_7_
  26.0 0.0 copy-done
  26.0 4.7 %far_scores.1 = (f32[4,16,256]{2,1,0:T(8,128)S(1)}, f32[16,128]{1,0:T(8,128)S(1)}, bf16[8,144,256]{2,1,0:T(8,128)(2,1)S(1)}) custom-call(s32[2]{0:T(128)S(1)} %pad_add_fusion.refs_0_.place_ref, bf16[8,128,256]{2,1,0:T(8,128)(2,1)S(1)} %collective-permute-done.refs_1_.refs_7_, bf16[4,768,128]{2,1,0:T(8,128)(2,1)S(1)} %copy-done.2, ...), custom_call_target="tpu_custom_call" | custom-call | flops 1610612736 | bytes 8388608 | tf_op jit(solution)/shard_map/far_scores/pallas_call | solution.py:396
  30.7 0.1 collective-permute-start.1
  30.8 1.0 %keep_terms.1 = (f32[8,128,256]{2,1,0:T(8,128)S(1)}, f32[128,256]{1,0:T(8,128)S(1)}) custom-call(s32[2]{0:T(128)S(1)} %pad_add_fusion.refs_0_.place_ref, f32[4,16,256]{2,1,0:T(8,128)S(1)} %get-tuple-element.30.expo_ref.refs_2_, bf16[4,16,128,256]{3,2,1,0:T(8,128)(2,1)S(1)} %copy-done), custom_call_target="tpu_custom_call" | custom-call | flops 4194304 | bytes 4194304 | tf_op jit(solution)/shard_map/keep_terms/pallas_call | solution.py:405
  31.8 1.0 %collective-permute-done.1.pair_ref = bf16[8,144,256]{2,1,0:T(8,128)(2,1)S(1)} collective-permute-done((bf16[8,144,256]{2,1,0:T(8,128)(2,1)S(1)}, bf16[8,144,256]{2,1,0:T(8,128)(2,1)S(1)}, u32[]{:S(2)}, u32[]{:S(2)}) %collective-permute-start.1) | collective-permute-done | bytes 589856 | tf_op jit(solution)/shard_map/ppermute | solution.py:320
  32.8 0.7 add_pair.1
  33.4 16.0 %all_to_all.25.refs_3_ = bf16[8,144,256]{2,1,0:T(8,128)(2,1)S(1)} all-to-all(bf16[8,144,256]{2,1,0:T(8,128)(2,1)S(1)} %get-tuple-element.34), channel_id=1, replica_groups=mesh['dp'=8,'chip'=8,'core'=2] {'chip'}, dimensions={0} | all-to-all | bytes 1179648 | tf_op jit(solution)/shard_map/all_to_all | solution.py:420
  49.5 0.0 copy-done.1
  49.5 0.0 copy-done.3
  49.5 0.0 copy-done.4
  49.5 0.0 copy-done.5
  49.5 5.9 %gradients.1 = (f32[768,128]{1,0:T(8,128)S(1)}, f32[256,128]{1,0:T(8,128)}, bf16[4,128,768]{2,1,0:T(8,128)(2,1)S(1)}, bf16[128,256]{1,0:T(8,128)(2,1)S(1)}) custom-call(s32[2]{0:T(128)S(1)} %pad_add_fusion.refs_0_.place_ref, s32[4,16,256]{2,1,0:T(8,128)S(1)} %copy-done.5, f32[4,16,256]{2,1,0:T(8,128)S(1)} %get-tuple-element.30.expo_ref.refs_2_, ...), custom_call_target="tpu_custom_call" | custom-call | flops 4429185024 | bytes 16777216 | tf_op jit(solution)/shard_map/gradients/pallas_call | solution.py:423
  55.4 1.0 %collective-permute-start.2 = (f32[768,128]{1,0:T(8,128)S(1)}, f32[768,128]{1,0:T(8,128)S(1)}, u32[]{:S(2)}, u32[]{:S(2)}) collective-permute-start(f32[768,128]{1,0:T(8,128)S(1)} %get-tuple-element.42), channel_id=1, source_target_pairs={{0,1},{1,0},{2,3},{3,2},{4,5},{5,4},{6,7},{7,6},{8,9},{9,8},{10,11... | collective-permute-start | bytes 1179656 | tf_op jit(solution)/shard_map/ppermute | solution.py:320
  56.4 1.5 %weight_keep.1 = f32[768,128]{1,0:T(8,128)S(1)} custom-call(s32[2]{0:T(128)S(1)} %pad_add_fusion.refs_0_.place_ref, bf16[4,128,768]{2,1,0:T(8,128)(2,1)S(1)} %get-tuple-element.40.page_direction_ref, bf16[128,256]{1,0:T(8,128)(2,1)S(1)} %get-tuple-element.41.query_direction_ref, bf16[4,768,1536]{2,1,0:T(8,128)(2,1)S(1)} %get-tuple-element.38.refs_9_.hidden, ...), custom_call_target="tpu_custom_call" | custom-call | flops 603979776 | bytes 6291456 | tf_op jit(solution)/shard_map/weight_keep/pallas_call | solution.py:442
  57.8 0.0 collective-permute-done.2
  57.9 0.1 add_convert_fusion
  57.9 8.9 %all_to_all.26 = bf16[8,96,128]{2,1,0:T(8,128)(2,1)S(1)} all-to-all(bf16[8,96,128]{2,1,0:T(8,128)(2,1)S(1)} %bitcast.13), channel_id=1, replica_groups=mesh['dp'=8,'chip'=8,'core'=2] {'chip'}, dimensions={0} | all-to-all | bytes 393216 | tf_op jit(solution)/shard_map/all_to_all | solution.py:452
  66.9 13.9 %all_to_all.27 = bf16[8,96,128]{2,1,0:T(8,128)(2,1)S(1)} all-to-all(bf16[8,96,128]{2,1,0:T(8,128)(2,1)S(1)} %broadcast_in_dim.4), channel_id=1, replica_groups=mesh['dp'=8,'chip'=8,'core'=2] {'dp'}, dimensions={0} | all-to-all | bytes 393216 | tf_op jit(solution)/shard_map/all_to_all | solution.py:328
  80.8 8.2 %all_to_all.28 = bf16[8,96,128]{2,1,0:T(8,128)(2,1)S(1)} all-to-all(bf16[8,96,128]{2,1,0:T(8,128)(2,1)S(1)} %broadcast_in_dim.5), channel_id=1, replica_groups=mesh['dp'=8,'chip'=8,'core'=2] {'chip'}, dimensions={0} | all-to-all | bytes 393216 | tf_op jit(solution)/shard_map/all_to_all | solution.py:328
  89.1 3.6 %collective-permute-start.3 = (bf16[768,128]{1,0:T(8,128)(2,1)S(1)}, bf16[768,128]{1,0:T(8,128)(2,1)S(1)}, u32[]{:S(2)}, u32[]{:S(2)}) collective-permute-start(bf16[768,128]{1,0:T(8,128)(2,1)S(1)} %bitcast.12), channel_id=1, source_target_pairs={{0,1},{1,0},{2,3},{3,2},{4,5},{5,4},{6,7},{7,6},{8,9},{9,8},{10,11... | collective-permute-start | bytes 589832 | tf_op jit(solution)/shard_map/ppermute | solution.py:320
  92.6 1.1 %collective-permute-done.3 = bf16[768,128]{1,0:T(8,128)(2,1)S(1)} collective-permute-done((bf16[768,128]{1,0:T(8,128)(2,1)S(1)}, bf16[768,128]{1,0:T(8,128)(2,1)S(1)}, u32[]{:S(2)}, u32[]{:S(2)}) %collective-permute-start.3) | collective-permute-done | bytes 196640 | tf_op jit(solution)/shard_map/ppermute | solution.py:320
  93.7 0.9 maximum_convert_fusion
  (5 shorter events, 0.2 us)
Async XLA Ops:
  3.2 16.6 %all-to-all-start = ((bf16[8,128,256]{2,1,0:T(8,128)(2,1)}), bf16[8,128,256]{2,1,0:T(8,128)(2,1)S(1)}, u32[]{:S(2)}, u32[]{:S(2)}) async-start(bf16[8,128,256]{2,1,0:T(8,128)(2,1)} %get-tuple-element.23), calls=%async_computation | async-start | bytes 1048576 | tf_op jit(solution)/shard_map/all_to_all | solution.py:354
  19.8 6.2 %collective-permute-start = (bf16[8,128,256]{2,1,0:T(8,128)(2,1)S(1)}, bf16[8,128,256]{2,1,0:T(8,128)(2,1)S(1)}, u32[]{:S(2)}, u32[]{:S(2)}) collective-permute-start(bf16[8,128,256]{2,1,0:T(8,128)(2,1)S(1)} %all-to-all-done.query_ref.refs_6_), channel_id=1, source_target_pairs={{0,1},{1,0},{2,3},{3,2},{4,5},{5,4},{6,7},{7,6},{8,9},{9,8},{10,11... | collective-permute-start | bytes 1572872 | tf_op jit(solution)/shard_map/ppermute | solution.py:320
  20.8 5.2 %copy-start = (bf16[4,16,128,256]{3,2,1,0:T(8,128)(2,1)S(1)}, bf16[4,16,128,256]{3,2,1,0:T(8,128)(2,1)}, u32[]{:S(2)}) copy-start(bf16[4,16,128,256]{3,2,1,0:T(8,128)(2,1)} %get-tuple-element.29.refs_4_.chosen_ref) | copy-start | bytes 12582916
  20.9 1.3 %copy-start.2 = (bf16[4,768,128]{2,1,0:T(8,128)(2,1)S(1)}, bf16[4,768,128]{2,1,0:T(8,128)(2,1)}, u32[]{:S(2)}) copy-start(bf16[4,768,128]{2,1,0:T(8,128)(2,1)} %get-tuple-element.27.unit_ref.refs_2_) | copy-start | bytes 2359300
  22.2 27.3 %copy-start.1 = (bf16[8,32,1536]{2,1,0:T(8,128)(2,1)S(1)}, bf16[8,32,1536]{2,1,0:T(8,128)(2,1)}, u32[]{:S(2)}) copy-start(bf16[8,32,1536]{2,1,0:T(8,128)(2,1)} %param.5) | copy-start | bytes 2359300
  22.2 27.3 %copy-start.3 = (f32[128,256]{1,0:T(8,128)S(1)}, f32[128,256]{1,0:T(8,128)}, u32[]{:S(2)}) copy-start(f32[128,256]{1,0:T(8,128)} %get-tuple-element.39.refs_10_) | copy-start | bytes 393220
  22.2 27.3 %copy-start.4 = (f32[4,128,768]{2,1,0:T(8,128)S(1)}, f32[4,128,768]{2,1,0:T(8,128)}, u32[]{:S(2)}) copy-start(f32[4,128,768]{2,1,0:T(8,128)} %get-tuple-element.37.refs_8_) | copy-start | bytes 4718596
  22.2 27.3 %copy-start.5 = (s32[4,16,256]{2,1,0:T(8,128)S(1)}, s32[4,16,256]{2,1,0:T(8,128)}, u32[]{:S(2)}) copy-start(s32[4,16,256]{2,1,0:T(8,128)} %get-tuple-element.25.refs_1_) | copy-start | bytes 196612
  30.7 2.1 %collective-permute-start.1 = (bf16[8,144,256]{2,1,0:T(8,128)(2,1)S(1)}, bf16[8,144,256]{2,1,0:T(8,128)(2,1)S(1)}, u32[]{:S(2)}, u32[]{:S(2)}) collective-permute-start(bf16[8,144,256]{2,1,0:T(8,128)(2,1)S(1)} %get-tuple-element.33), channel_id=1, source_target_pairs={{0,1},{1,0},{2,3},{3,2},{4,5},{5,4},{6,7},{7,6},{8,9},{9,8},{10,11... | collective-permute-start | bytes 1769480 | tf_op jit(solution)/shard_map/ppermute | solution.py:320
  55.4 2.4 %collective-permute-start.2 = (f32[768,128]{1,0:T(8,128)S(1)}, f32[768,128]{1,0:T(8,128)S(1)}, u32[]{:S(2)}, u32[]{:S(2)}) collective-permute-start(f32[768,128]{1,0:T(8,128)S(1)} %get-tuple-element.42), channel_id=1, source_target_pairs={{0,1},{1,0},{2,3},{3,2},{4,5},{5,4},{6,7},{7,6},{8,9},{9,8},{10,11... | collective-permute-start | bytes 1179656 | tf_op jit(solution)/shard_map/ppermute | solution.py:320
  89.1 4.6 %collective-permute-start.3 = (bf16[768,128]{1,0:T(8,128)(2,1)S(1)}, bf16[768,128]{1,0:T(8,128)(2,1)S(1)}, u32[]{:S(2)}, u32[]{:S(2)}) collective-permute-start(bf16[768,128]{1,0:T(8,128)(2,1)S(1)} %bitcast.12), channel_id=1, source_target_pairs={{0,1},{1,0},{2,3},{3,2},{4,5},{5,4},{6,7},{7,6},{8,9},{9,8},{10,11... | collective-permute-start | bytes 589832 | tf_op jit(solution)/shard_map/ppermute | solution.py:320

commit v9 on v8

--- a/solution.py
+++ b/solution.py
@@ -448,8 +448,8 @@
         name="weight_keep",
     )(place, page_direction, query_direction, page_hidden, query_rows)
 
-    halves = (weight_keep + swap_cores(weight_give)).astype(BF16)
-    chunk = summed(lax.all_to_all(halves.reshape(chips, half // chips, dim), "chip", 0, 0, tiled=True))
+    halves = weight_keep + swap_cores(weight_give)
+    chunk = jnp.sum(lax.all_to_all(halves.reshape(chips, half // chips, dim), "chip", 0, 0, tiled=True), axis=0)
     chunk = summed(to_all(chunk, "dp"))
     mine = to_all(chunk, "chip").reshape(half, dim)
     other = swap_cores(mine)

time: 95 us -> 98.5 us (1.037)
  blocking collectives: 47 us -> 50.4 us
    all_to_all x1, blocking collectives: 8.93 us -> 10.9 us  [per_device(): lax.all_to_all(halves.reshape(chips, half // chips, dim), 'chip', 0, 0, t...]
    all_to_all x2, blocking collectives: 22.1 us -> 23.4 us  [to_all(): lax.all_to_all(jnp.broadcast_to(value[None], (lax.axis_size(axis),) + val...]
where the time goes in v9:
time: 98.5 us; the launch traced here: 98.1 us
  blocking collectives  50.4 us (51%)
  Pallas kernels  30 us (30%)
  starting transfers between devices  12.2 us (12%)
  waiting for transfers between devices  2.27 us (2%)
  local copies, waits for them, and re-layouts  1.36 us (1%)
  other arithmetic  1.16 us (1%)
    all_to_all x2, blocking collectives, to_all(): lax.all_to_all(jnp.broadcast_to(value[None], (lax.axis_size(axis),) + val...  23.4 us
    all_to_all x1, blocking collectives, per_device(): received = lax.all_to_all(send, 'chip', 0, 0, tiled=True)  16 us
    all_to_all x1, blocking collectives, per_device(): lax.all_to_all(halves.reshape(chips, half // chips, dim), 'chip', 0, 0, t...  10.9 us
    pallas_call x1, Pallas kernels, per_device(): pl.pallas_call(page_kernel, in_specs=[anywhere] * 4, out_specs=[anywhere]...  9.98 us
    all_to_all x1, starting transfers between devices, per_device(): near = lax.all_to_all(query_send, 'chip', 0, 0, tiled=True)  6.39 us
    pallas_call x1, Pallas kernels, per_device(): pl.pallas_call(lambda *refs: gradient_kernel(multiplier, *refs), in_specs...  5.92 us
    ppermute x4, starting transfers between devices, swap_cores(): return lax.ppermute(value, 'core', [(0, 1), (1, 0)])  5.81 us
    pallas_call x1, Pallas kernels, per_device(): pl.pallas_call(lambda *refs: far_kernel(multiplier, *refs), in_specs=[sme...  4.65 us
  transfers between devices with their start and end apart: 5, of which 3 were waited for; matrix products, arithmetic and copies ran while one was open for 0% of the time, Pallas kernels for 17%

profile of v9, /device:TPU:1, one launch (start us, length us, event | category | flops | bytes accessed | tf_op | source)
XLA Modules:
  0.0 98.1 jit_solution(1648407288556393891)
XLA Ops:
  0.6 2.6 %query_project.1 = (f32[128,256]{1,0:T(8,128)}, bf16[8,128,256]{2,1,0:T(8,128)(2,1)}) custom-call(bf16[256,1536]{1,0:T(8,128)(2,1)} %bitcast.9, bf16[1536,128]{1,0:T(8,128)(2,1)} %weight_any.3), custom_call_target="tpu_custom_call" | custom-call | flops 100663296 | bytes 2097152 | tf_op jit(solution)/shard_map/query_project/pallas_call | solution.py:345
  3.2 6.4 %all-to-all-start = ((bf16[8,128,256]{2,1,0:T(8,128)(2,1)}), bf16[8,128,256]{2,1,0:T(8,128)(2,1)S(1)}, u32[]{:S(2)}, u32[]{:S(2)}) async-start(bf16[8,128,256]{2,1,0:T(8,128)(2,1)} %get-tuple-element.23), calls=%async_computation | async-start | bytes 1048576 | tf_op jit(solution)/shard_map/all_to_all | solution.py:354
  9.6 10.0 %page_project.1 = (f32[4,128,768]{2,1,0:T(8,128)}, bf16[4,768,128]{2,1,0:T(8,128)(2,1)}, bf16[4,16,128,256]{3,2,1,0:T(8,128)(2,1)}, s32[4,16,256]{2,1,0:T(8,128)}) custom-call(s32[4]{0:T(128)} %length_any.1, bf16[4,768,1536]{2,1,0:T(8,128)(2,1)} %hidden_any.3, bf16[1536,128]{1,0:T(8,128)(2,1)} %weight_any.3, s32[32,4,128]{2,1,0:T(4,128)} %bitcast.14), custom_call_target="tpu_custom_call" | custom-call | flops 4429185024 | bytes 16777216 | tf_op jit(solution)/shard_map/page_project/pallas_call | solution.py:356
  19.6 0.2 all-to-all-done.query_ref.refs_6_
  19.8 1.0 %collective-permute-start = (bf16[8,128,256]{2,1,0:T(8,128)(2,1)S(1)}, bf16[8,128,256]{2,1,0:T(8,128)(2,1)S(1)}, u32[]{:S(2)}, u32[]{:S(2)}) collective-permute-start(bf16[8,128,256]{2,1,0:T(8,128)(2,1)S(1)} %all-to-all-done.query_ref.refs_6_), channel_id=1, source_target_pairs={{0,1},{1,0},{2,3},{3,2},{4,5},{5,4},{6,7},{7,6},{8,9},{9,8},{10,11... | collective-permute-start | bytes 1572872 | tf_op jit(solution)/shard_map/ppermute | solution.py:320
  20.8 0.0 copy-start
  20.8 0.1 pad_add_fusion.refs_0_.place_ref
  20.9 0.0 copy-start.2
  20.9 1.3 %copy-done.2 = bf16[4,768,128]{2,1,0:T(8,128)(2,1)S(1)} copy-done((bf16[4,768,128]{2,1,0:T(8,128)(2,1)S(1)}, bf16[4,768,128]{2,1,0:T(8,128)(2,1)}, u32[]{:S(2)}) %copy-start.2) | copy-done | bytes 786456
  22.2 0.0 copy-start.1
  22.2 0.0 copy-start.3
  22.2 0.0 copy-start.4
  22.2 0.0 copy-start.5
  22.2 3.8 %near_scores.1 = (f32[4,8,256]{2,1,0:T(8,128)S(1)}, bf16[4,768,1536]{2,1,0:T(8,128)(2,1)S(1)}) custom-call(bf16[8,128,256]{2,1,0:T(8,128)(2,1)S(1)} %all-to-all-done.query_ref.refs_6_, bf16[4,768,128]{2,1,0:T(8,128)(2,1)S(1)} %copy-done.2, bf16[4,768,1536]{2,1,0:T(8,128)(2,1)} %hidden_any.3), custom_call_target="tpu_custom_call" | custom-call | flops 1610612736 | bytes 2097152 | tf_op jit(solution)/shard_map/near_scores/pallas_call | solution.py:387
  26.0 0.0 collective-permute-done.refs_1_.refs_7_
  26.0 0.0 copy-done
  26.0 4.7 %far_scores.1 = (f32[4,16,256]{2,1,0:T(8,128)S(1)}, f32[16,128]{1,0:T(8,128)S(1)}, bf16[8,144,256]{2,1,0:T(8,128)(2,1)S(1)}) custom-call(s32[2]{0:T(128)S(1)} %pad_add_fusion.refs_0_.place_ref, bf16[8,128,256]{2,1,0:T(8,128)(2,1)S(1)} %collective-permute-done.refs_1_.refs_7_, bf16[4,768,128]{2,1,0:T(8,128)(2,1)S(1)} %copy-done.2, ...), custom_call_target="tpu_custom_call" | custom-call | flops 1610612736 | bytes 8388608 | tf_op jit(solution)/shard_map/far_scores/pallas_call | solution.py:396
  30.7 0.1 collective-permute-start.1
  30.8 1.0 keep_terms.1
  31.8 1.0 %collective-permute-done.1.pair_ref = bf16[8,144,256]{2,1,0:T(8,128)(2,1)S(1)} collective-permute-done((bf16[8,144,256]{2,1,0:T(8,128)(2,1)S(1)}, bf16[8,144,256]{2,1,0:T(8,128)(2,1)S(1)}, u32[]{:S(2)}, u32[]{:S(2)}) %collective-permute-start.1) | collective-permute-done | bytes 589856 | tf_op jit(solution)/shard_map/ppermute | solution.py:320
  32.8 0.7 add_pair.1
  33.4 16.0 %all_to_all.25.refs_3_ = bf16[8,144,256]{2,1,0:T(8,128)(2,1)S(1)} all-to-all(bf16[8,144,256]{2,1,0:T(8,128)(2,1)S(1)} %get-tuple-element.34), channel_id=1, replica_groups=mesh['dp'=8,'chip'=8,'core'=2] {'chip'}, dimensions={0} | all-to-all | bytes 1179648 | tf_op jit(solution)/shard_map/all_to_all | solution.py:420
  49.5 0.0 copy-done.1
  49.5 0.0 copy-done.3
  49.5 0.0 copy-done.4
  49.5 0.0 copy-done.5
  49.5 5.9 %gradients.1 = (f32[768,128]{1,0:T(8,128)S(1)}, f32[256,128]{1,0:T(8,128)}, bf16[4,128,768]{2,1,0:T(8,128)(2,1)S(1)}, bf16[128,256]{1,0:T(8,128)(2,1)S(1)}) custom-call(s32[2]{0:T(128)S(1)} %pad_add_fusion.refs_0_.place_ref, s32[4,16,256]{2,1,0:T(8,128)S(1)} %copy-done.5, f32[4,16,256]{2,1,0:T(8,128)S(1)} %get-tuple-element.30.expo_ref.refs_2_, ...), custom_call_target="tpu_custom_call" | custom-call | flops 4429185024 | bytes 16777216 | tf_op jit(solution)/shard_map/gradients/pallas_call | solution.py:423
  55.4 1.0 collective-permute-start.2
  56.4 1.5 %weight_keep.1 = f32[768,128]{1,0:T(8,128)S(1)} custom-call(s32[2]{0:T(128)S(1)} %pad_add_fusion.refs_0_.place_ref, bf16[4,128,768]{2,1,0:T(8,128)(2,1)S(1)} %get-tuple-element.40.page_direction_ref, bf16[128,256]{1,0:T(8,128)(2,1)S(1)} %get-tuple-element.41.query_direction_ref, bf16[4,768,1536]{2,1,0:T(8,128)(2,1)S(1)} %get-tuple-element.38.refs_9_.hidden, ...), custom_call_target="tpu_custom_call" | custom-call | flops 603979776 | bytes 6291456 | tf_op jit(solution)/shard_map/weight_keep/pallas_call | solution.py:442
  57.8 0.0 collective-permute-done.2
  57.9 0.1 add.3
  57.9 10.9 %all_to_all.26 = f32[8,96,128]{2,1,0:T(8,128)S(1)} all-to-all(f32[8,96,128]{2,1,0:T(8,128)S(1)} %bitcast.12), channel_id=1, replica_groups=mesh['dp'=8,'chip'=8,'core'=2] {'chip'}, dimensions={0} | all-to-all | bytes 786432 | tf_op jit(solution)/shard_map/all_to_all | solution.py:452
  68.9 15.2 %all_to_all.27 = f32[8,96,128]{2,1,0:T(8,128)S(1)} all-to-all(f32[8,96,128]{2,1,0:T(8,128)S(1)} %broadcast_in_dim.4), channel_id=1, replica_groups=mesh['dp'=8,'chip'=8,'core'=2] {'dp'}, dimensions={0} | all-to-all | bytes 786432 | tf_op jit(solution)/shard_map/all_to_all | solution.py:328
  84.2 8.2 %all_to_all.28 = bf16[8,96,128]{2,1,0:T(8,128)(2,1)S(1)} all-to-all(bf16[8,96,128]{2,1,0:T(8,128)(2,1)S(1)} %broadcast_in_dim.5), channel_id=1, replica_groups=mesh['dp'=8,'chip'=8,'core'=2] {'chip'}, dimensions={0} | all-to-all | bytes 393216 | tf_op jit(solution)/shard_map/all_to_all | solution.py:328
  92.4 3.7 %collective-permute-start.3 = (bf16[768,128]{1,0:T(8,128)(2,1)S(1)}, bf16[768,128]{1,0:T(8,128)(2,1)S(1)}, u32[]{:S(2)}, u32[]{:S(2)}) collective-permute-start(bf16[768,128]{1,0:T(8,128)(2,1)S(1)} %bitcast.13), channel_id=1, source_target_pairs={{0,1},{1,0},{2,3},{3,2},{4,5},{5,4},{6,7},{7,6},{8,9},{9,8},{10,11... | collective-permute-start | bytes 589832 | tf_op jit(solution)/shard_map/ppermute | solution.py:320
  96.1 1.1 %collective-permute-done.3 = bf16[768,128]{1,0:T(8,128)(2,1)S(1)} collective-permute-done((bf16[768,128]{1,0:T(8,128)(2,1)S(1)}, bf16[768,128]{1,0:T(8,128)(2,1)S(1)}, u32[]{:S(2)}, u32[]{:S(2)}) %collective-permute-start.3) | collective-permute-done | bytes 196640 | tf_op jit(solution)/shard_map/ppermute | solution.py:320
  97.2 0.9 maximum_convert_fusion
  (5 shorter events, 0.1 us)
Async XLA Ops:
  3.2 16.6 %all-to-all-start = ((bf16[8,128,256]{2,1,0:T(8,128)(2,1)}), bf16[8,128,256]{2,1,0:T(8,128)(2,1)S(1)}, u32[]{:S(2)}, u32[]{:S(2)}) async-start(bf16[8,128,256]{2,1,0:T(8,128)(2,1)} %get-tuple-element.23), calls=%async_computation | async-start | bytes 1048576 | tf_op jit(solution)/shard_map/all_to_all | solution.py:354
  19.8 6.2 %collective-permute-start = (bf16[8,128,256]{2,1,0:T(8,128)(2,1)S(1)}, bf16[8,128,256]{2,1,0:T(8,128)(2,1)S(1)}, u32[]{:S(2)}, u32[]{:S(2)}) collective-permute-start(bf16[8,128,256]{2,1,0:T(8,128)(2,1)S(1)} %all-to-all-done.query_ref.refs_6_), channel_id=1, source_target_pairs={{0,1},{1,0},{2,3},{3,2},{4,5},{5,4},{6,7},{7,6},{8,9},{9,8},{10,11... | collective-permute-start | bytes 1572872 | tf_op jit(solution)/shard_map/ppermute | solution.py:320
  20.8 5.2 %copy-start = (bf16[4,16,128,256]{3,2,1,0:T(8,128)(2,1)S(1)}, bf16[4,16,128,256]{3,2,1,0:T(8,128)(2,1)}, u32[]{:S(2)}) copy-start(bf16[4,16,128,256]{3,2,1,0:T(8,128)(2,1)} %get-tuple-element.29.refs_4_.chosen_ref) | copy-start | bytes 12582916
  20.9 1.3 %copy-start.2 = (bf16[4,768,128]{2,1,0:T(8,128)(2,1)S(1)}, bf16[4,768,128]{2,1,0:T(8,128)(2,1)}, u32[]{:S(2)}) copy-start(bf16[4,768,128]{2,1,0:T(8,128)(2,1)} %get-tuple-element.27.unit_ref.refs_2_) | copy-start | bytes 2359300
  22.2 27.3 %copy-start.1 = (bf16[8,32,1536]{2,1,0:T(8,128)(2,1)S(1)}, bf16[8,32,1536]{2,1,0:T(8,128)(2,1)}, u32[]{:S(2)}) copy-start(bf16[8,32,1536]{2,1,0:T(8,128)(2,1)} %param.5) | copy-start | bytes 2359300
  22.2 27.3 %copy-start.3 = (f32[128,256]{1,0:T(8,128)S(1)}, f32[128,256]{1,0:T(8,128)}, u32[]{:S(2)}) copy-start(f32[128,256]{1,0:T(8,128)} %get-tuple-element.39.refs_10_) | copy-start | bytes 393220
  22.2 27.3 %copy-start.4 = (f32[4,128,768]{2,1,0:T(8,128)S(1)}, f32[4,128,768]{2,1,0:T(8,128)}, u32[]{:S(2)}) copy-start(f32[4,128,768]{2,1,0:T(8,128)} %get-tuple-element.37.refs_8_) | copy-start | bytes 4718596
  22.2 27.3 %copy-start.5 = (s32[4,16,256]{2,1,0:T(8,128)S(1)}, s32[4,16,256]{2,1,0:T(8,128)}, u32[]{:S(2)}) copy-start(s32[4,16,256]{2,1,0:T(8,128)} %get-tuple-element.25.refs_1_) | copy-start | bytes 196612
  30.7 2.1 %collective-permute-start.1 = (bf16[8,144,256]{2,1,0:T(8,128)(2,1)S(1)}, bf16[8,144,256]{2,1,0:T(8,128)(2,1)S(1)}, u32[]{:S(2)}, u32[]{:S(2)}) collective-permute-start(bf16[8,144,256]{2,1,0:T(8,128)(2,1)S(1)} %get-tuple-element.33), channel_id=1, source_target_pairs={{0,1},{1,0},{2,3},{3,2},{4,5},{5,4},{6,7},{7,6},{8,9},{9,8},{10,11... | collective-permute-start | bytes 1769480 | tf_op jit(solution)/shard_map/ppermute | solution.py:320
  55.4 2.4 %collective-permute-start.2 = (f32[768,128]{1,0:T(8,128)S(1)}, f32[768,128]{1,0:T(8,128)S(1)}, u32[]{:S(2)}, u32[]{:S(2)}) collective-permute-start(f32[768,128]{1,0:T(8,128)S(1)} %get-tuple-element.42), channel_id=1, source_target_pairs={{0,1},{1,0},{2,3},{3,2},{4,5},{5,4},{6,7},{7,6},{8,9},{9,8},{10,11... | collective-permute-start | bytes 1179656 | tf_op jit(solution)/shard_map/ppermute | solution.py:320
  92.4 4.8 %collective-permute-start.3 = (bf16[768,128]{1,0:T(8,128)(2,1)S(1)}, bf16[768,128]{1,0:T(8,128)(2,1)S(1)}, u32[]{:S(2)}, u32[]{:S(2)}) collective-permute-start(bf16[768,128]{1,0:T(8,128)(2,1)S(1)} %bitcast.13), channel_id=1, source_target_pairs={{0,1},{1,0},{2,3},{3,2},{4,5},{5,4},{6,7},{7,6},{8,9},{9,8},{10,11... | collective-permute-start | bytes 589832 | tf_op jit(solution)/shard_map/ppermute | solution.py:320
